TPU v7x, 32 devices: a whole 2x2x4 slice. The times are simulated.
32 devices in a mesh: seq: 4 (over z), fsdp: 8 (over y, x, core).
Axes of the slice: x: 2, y: 2, z: 4, core: 2. Of those that a mesh axis runs over, the one named last changes fastest.
Arguments:
- block_input: bfloat16 [8, 1024, 2048], P('fsdp', 'seq'), may hold values from -6 to 6
- query_weight: bfloat16 [2048, 2048], P('fsdp'), may hold values from -0.125 to 0.125
- key_weight: bfloat16 [2048, 2048], P('fsdp'), may hold values from -0.125 to 0.125
- value_weight: bfloat16 [2048, 2048], P('fsdp'), may hold values from -0.125 to 0.125
- out_weight: bfloat16 [2048, 2048], P('fsdp'), may hold values from -0.125 to 0.125
- gate_weight: bfloat16 [2048, 8192], P('fsdp'), may hold values from -0.125 to 0.125
- up_weight: bfloat16 [2048, 8192], P('fsdp'), may hold values from -0.125 to 0.125
- down_weight: bfloat16 [8192, 2048], P('fsdp'), may hold values from -0.0625 to 0.0625
- query_gain: float32 [2048], replicated, may hold values from 1 to 2
- key_gain: float32 [2048], replicated, may hold values from 1 to 2
- attention_gain: float32 [2048], replicated, may hold values from 0.25 to 1.75
- swiglu_gain: float32 [2048], replicated, may hold values from 0.25 to 1.75
- cotangent: bfloat16 [8, 1024, 2048], P('fsdp', 'seq'), may hold values from -6 to 6
Outputs:
- output: float32 [8, 1024, 2048], P('fsdp', 'seq')
- input_grad: float32 [8, 1024, 2048], P('fsdp', 'seq')
- query_weight_grad: float32 [2048, 2048], P('fsdp')
- key_weight_grad: float32 [2048, 2048], P('fsdp')
- value_weight_grad: float32 [2048, 2048], P('fsdp')
- out_weight_grad: float32 [2048, 2048], P('fsdp')
- gate_weight_grad: float32 [2048, 8192], P('fsdp')
- up_weight_grad: float32 [2048, 8192], P('fsdp')
- down_weight_grad: float32 [8192, 2048], P('fsdp')
- query_gain_grad: float32 [2048], replicated
- key_gain_grad: float32 [2048], replicated
- attention_gain_grad: float32 [2048], replicated
- swiglu_gain_grad: float32 [2048], replicated
All inputs are finite; a program needn't handle non-finite values.
Results may differ from a plain program's by a relative error of at most 0.023.
Values may be sent and summed in bfloat16 or wider, within the bound.
A program may use at most 512 MiB of HBM per device.

v0:
```python
import jax
import jax.numpy as jnp
from jax import lax
from jax.sharding import PartitionSpec as P

HEADS = 16


epsilon = 1e-06
rotary_base = 500000.0
masked_value = -1e30


def norm_factor(values):
    return lax.rsqrt(jnp.mean(values * values, axis=-1, keepdims=True) + epsilon)


def norm_backward(values, factor, gain_vector, upstream):
    scaled = upstream * gain_vector
    inner_mean = jnp.mean(scaled * values, axis=-1, keepdims=True)
    value_grad = factor * scaled - values * factor * factor * factor * inner_mean
    gain_grad = jnp.sum(upstream * values * factor, axis=0)
    return (value_grad, gain_grad)


def rotary_tables(count, offset, head_size):
    positions = (offset + jnp.arange(count, dtype=jnp.int32)).astype(jnp.float32)
    middle = head_size // 2
    frequency = rotary_base ** (-2.0 * jnp.arange(middle, dtype=jnp.float32) / head_size)
    angles = positions[:, None] * frequency[None, :]
    return (jnp.cos(angles)[:, None, :], jnp.sin(angles)[:, None, :])


def rotate(values, cosine, sine_table, direction_sign):
    middle = values.shape[-1] // 2
    leading = values[..., :middle]
    trailing = values[..., middle:]
    signed = sine_table * direction_sign
    return jnp.concatenate(
        [leading * cosine - trailing * signed, trailing * cosine + leading * signed], axis=-1
    )


def times_transposed(operand, matrix):
    return lax.dot_general(
        operand, matrix, (((1,), (1,)), ((), ())), preferred_element_type=jnp.float32
    )


def transposed_times(operand, matrix):
    return lax.dot_general(
        operand, matrix, (((0,), (0,)), ((), ())), preferred_element_type=jnp.float32
    )


def masked_scores(query_block, keys, row_start, block_rows, score_scale):
    length = keys.shape[0]
    scores = (
        jnp.einsum("qhd,khd->hqk", query_block, keys, preferred_element_type=jnp.float32)
        * score_scale
    )
    query_positions = row_start + jnp.arange(block_rows, dtype=jnp.int32)
    key_positions = jnp.arange(length, dtype=jnp.int32)
    allowed = key_positions[None, :] <= query_positions[:, None]
    return jnp.where(allowed[None], scores, masked_value)


def attention_forward(queries, keys, values):
    length = queries.shape[0]
    block_rows = min(512, length)
    blocks = length // block_rows
    score_scale = queries.shape[-1] ** (-0.5)

    def one_block(block_index):
        row_start = block_index * block_rows
        query_block = lax.dynamic_slice_in_dim(queries, row_start, block_rows, 0)
        scores = masked_scores(query_block, keys, row_start, block_rows, score_scale)
        maximum = jnp.max(scores, axis=-1, keepdims=True)
        exponent = jnp.exp(scores - maximum)
        row_total = jnp.sum(exponent, axis=-1, keepdims=True)
        log_total = maximum[..., 0] + jnp.log(row_total[..., 0])
        weights_low = (exponent / row_total).astype(jnp.bfloat16)
        attended = jnp.einsum(
            "hqk,khd->qhd", weights_low, values, preferred_element_type=jnp.float32
        )
        return (attended.astype(jnp.bfloat16), log_total)

    attended, log_total = lax.map(one_block, jnp.arange(blocks, dtype=jnp.int32))
    return (attended.reshape(length, -1), log_total)


def attention_backward(queries, keys, values, attended_grad, log_total):
    length = queries.shape[0]
    block_rows = min(512, length)
    blocks = length // block_rows
    score_scale = queries.shape[-1] ** (-0.5)
    empty = jnp.zeros(keys.shape, jnp.float32)

    def one_block(carried, operands):
        key_sum, value_sum = carried
        block_index, block_total = operands
        row_start = block_index * block_rows
        query_block = lax.dynamic_slice_in_dim(queries, row_start, block_rows, 0)
        grad_block = lax.dynamic_slice_in_dim(attended_grad, row_start, block_rows, 0)
        scores = masked_scores(query_block, keys, row_start, block_rows, score_scale)
        probabilities = jnp.exp(scores - block_total[..., None])
        weights_low = probabilities.astype(jnp.bfloat16)
        value_sum = value_sum + jnp.einsum(
            "hqk,qhd->khd", weights_low, grad_block, preferred_element_type=jnp.float32
        )
        probability_grad = jnp.einsum(
            "qhd,khd->hqk", grad_block, values, preferred_element_type=jnp.float32
        )
        inner_sum = jnp.sum(probabilities * probability_grad, axis=-1, keepdims=True)
        score_grad = (probabilities * (probability_grad - inner_sum)).astype(jnp.bfloat16)
        query_grad = (
            jnp.einsum("hqk,khd->qhd", score_grad, keys, preferred_element_type=jnp.float32)
            * score_scale
        )
        key_sum = (
            key_sum
            + jnp.einsum(
                "hqk,qhd->khd", score_grad, query_block, preferred_element_type=jnp.float32
            )
            * score_scale
        )
        return ((key_sum, value_sum), query_grad.astype(jnp.bfloat16))

    (key_sum, value_sum), query_grads = lax.scan(
        one_block, (empty, empty), (jnp.arange(blocks, dtype=jnp.int32), log_total)
    )
    return (
        query_grads.reshape(keys.shape),
        key_sum.astype(jnp.bfloat16),
        value_sum.astype(jnp.bfloat16),
    )


def local(
    block_input,
    query_weight,
    key_weight,
    value_weight,
    out_weight,
    gate_weight,
    up_weight,
    down_weight,
    query_gain,
    key_gain,
    attention_gain,
    swiglu_gain,
    cotangent,
):
    tokens = block_input.shape[1]
    model_width = block_input.shape[2]
    head_size = model_width // HEADS
    groups = lax.axis_size("seq")
    local_heads = HEADS // groups
    sequence = block_input.reshape(tokens, model_width)
    query_full, key_full, value_full, out_full = (
        lax.all_gather(query_weight, "fsdp", axis=0, tiled=True),
        lax.all_gather(key_weight, "fsdp", axis=0, tiled=True),
        lax.all_gather(value_weight, "fsdp", axis=0, tiled=True),
        lax.all_gather(out_weight, "fsdp", axis=0, tiled=True),
    )
    query_raw = jnp.dot(sequence, query_full, preferred_element_type=jnp.float32)
    key_raw = jnp.dot(sequence, key_full, preferred_element_type=jnp.float32)
    value_raw = jnp.dot(sequence, value_full, preferred_element_type=jnp.float32)
    query_factor = norm_factor(query_raw)
    key_factor = norm_factor(key_raw)
    cosine, sine_table = rotary_tables(tokens, lax.axis_index("seq") * tokens, head_size)
    query_rot = rotate(
        (query_raw * query_factor * query_gain).reshape(tokens, HEADS, head_size),
        cosine,
        sine_table,
        1.0,
    )
    key_rot = rotate(
        (key_raw * key_factor * key_gain).reshape(tokens, HEADS, head_size), cosine, sine_table, 1.0
    )
    stacked = jnp.stack(
        [
            query_rot.reshape(tokens, model_width).astype(jnp.bfloat16),
            key_rot.reshape(tokens, model_width).astype(jnp.bfloat16),
            value_raw.astype(jnp.bfloat16),
        ]
    )
    grouped = lax.all_to_all(stacked, "seq", split_axis=2, concat_axis=1, tiled=True)
    length = grouped.shape[1]
    head_queries = grouped[0].reshape(length, local_heads, head_size)
    head_keys = grouped[1].reshape(length, local_heads, head_size)
    head_values = grouped[2].reshape(length, local_heads, head_size)
    attended_heads, log_total = attention_forward(head_queries, head_keys, head_values)
    attended = lax.all_to_all(attended_heads, "seq", split_axis=0, concat_axis=1, tiled=True)
    branch = jnp.dot(attended, out_full, preferred_element_type=jnp.float32)
    branch_factor = norm_factor(branch)
    residual = sequence.astype(jnp.float32) + branch * branch_factor * attention_gain
    residual_low = residual.astype(jnp.bfloat16)
    gate_full, up_full, down_full = (
        lax.all_gather(gate_weight, "fsdp", axis=0, tiled=True),
        lax.all_gather(up_weight, "fsdp", axis=0, tiled=True),
        lax.all_gather(down_weight, "fsdp", axis=0, tiled=True),
    )
    gate_value = jnp.dot(residual_low, gate_full, preferred_element_type=jnp.float32)
    upward = jnp.dot(residual_low, up_full, preferred_element_type=jnp.float32)
    sigmoid_gate = jax.nn.sigmoid(gate_value)
    activated = gate_value * sigmoid_gate
    hidden = (activated * upward).astype(jnp.bfloat16)
    mixed_out = jnp.dot(hidden, down_full, preferred_element_type=jnp.float32)
    mixed_factor = norm_factor(mixed_out)
    output = residual + mixed_out * mixed_factor * swiglu_gain
    upstream = cotangent.reshape(tokens, model_width).astype(jnp.float32)
    mixed_float, swiglu_gain_grad = norm_backward(mixed_out, mixed_factor, swiglu_gain, upstream)
    mixed_grad = mixed_float.astype(jnp.bfloat16)
    gate_back, up_back, down_back = (
        lax.all_gather(gate_weight, "fsdp", axis=0, tiled=True),
        lax.all_gather(up_weight, "fsdp", axis=0, tiled=True),
        lax.all_gather(down_weight, "fsdp", axis=0, tiled=True),
    )
    hidden_grad = times_transposed(mixed_grad, down_back)
    gate_grad = (
        hidden_grad * upward * sigmoid_gate * (1.0 + gate_value * (1.0 - sigmoid_gate))
    ).astype(jnp.bfloat16)
    up_grad = (hidden_grad * activated).astype(jnp.bfloat16)
    residual_grad = (
        upstream + times_transposed(gate_grad, gate_back) + times_transposed(up_grad, up_back)
    )
    joined = jnp.concatenate([gate_grad, up_grad], axis=1)
    branch_float, attention_gain_grad = norm_backward(
        branch, branch_factor, attention_gain, residual_grad
    )
    branch_grad = branch_float.astype(jnp.bfloat16)
    query_back, key_back, value_back, out_back = (
        lax.all_gather(query_weight, "fsdp", axis=0, tiled=True),
        lax.all_gather(key_weight, "fsdp", axis=0, tiled=True),
        lax.all_gather(value_weight, "fsdp", axis=0, tiled=True),
        lax.all_gather(out_weight, "fsdp", axis=0, tiled=True),
    )
    attended_grad = times_transposed(branch_grad, out_back).astype(jnp.bfloat16)
    head_grad = lax.all_to_all(attended_grad, "seq", split_axis=1, concat_axis=0, tiled=True)
    query_grads, key_grads, value_grads = attention_backward(
        head_queries,
        head_keys,
        head_values,
        head_grad.reshape(length, local_heads, head_size),
        log_total,
    )
    back_stack = jnp.stack([query_grads, key_grads, value_grads]).reshape(
        3, length, local_heads * head_size
    )
    token_grads = lax.all_to_all(back_stack, "seq", split_axis=1, concat_axis=2, tiled=True)
    query_norm_grad = rotate(
        token_grads[0].astype(jnp.float32).reshape(tokens, HEADS, head_size),
        cosine,
        sine_table,
        -1.0,
    )
    key_norm_grad = rotate(
        token_grads[1].astype(jnp.float32).reshape(tokens, HEADS, head_size),
        cosine,
        sine_table,
        -1.0,
    )
    query_float, query_gain_grad = norm_backward(
        query_raw, query_factor, query_gain, query_norm_grad.reshape(tokens, model_width)
    )
    key_float, key_gain_grad = norm_backward(
        key_raw, key_factor, key_gain, key_norm_grad.reshape(tokens, model_width)
    )
    query_raw_grad = query_float.astype(jnp.bfloat16)
    key_raw_grad = key_float.astype(jnp.bfloat16)
    value_tokens = token_grads[2]
    input_grad = (
        residual_grad
        + times_transposed(query_raw_grad, query_back)
        + times_transposed(key_raw_grad, key_back)
        + times_transposed(value_tokens, value_back)
    )
    projected = jnp.concatenate([query_raw_grad, key_raw_grad, value_tokens], axis=1)
    hidden_width = gate_weight.shape[1]
    columns = hidden
    down_shard = lax.psum_scatter(
        transposed_times(columns, mixed_grad).astype(jnp.bfloat16),
        "fsdp",
        scatter_dimension=0,
        tiled=True,
    )
    columns = residual_low
    gate_up_shard = lax.psum_scatter(
        transposed_times(columns, joined).astype(jnp.bfloat16),
        "fsdp",
        scatter_dimension=0,
        tiled=True,
    )
    attention_shard = lax.psum_scatter(
        jnp.concatenate(
            [transposed_times(sequence, projected), transposed_times(attended, branch_grad)], axis=1
        ).astype(jnp.bfloat16),
        "fsdp",
        scatter_dimension=0,
        tiled=True,
    )
    attention_total, gate_up_total, down_total = (
        lax.psum(attention_shard, "seq").astype(jnp.float32),
        lax.psum(gate_up_shard, "seq").astype(jnp.float32),
        lax.psum(down_shard, "seq").astype(jnp.float32),
    )
    gain_totals = lax.psum(
        jnp.stack([query_gain_grad, key_gain_grad, attention_gain_grad, swiglu_gain_grad]),
        ("seq", "fsdp"),
    )
    return (
        output.reshape(1, tokens, model_width),
        input_grad.reshape(1, tokens, model_width),
        attention_total[:, :model_width],
        attention_total[:, model_width : 2 * model_width],
        attention_total[:, 2 * model_width : 3 * model_width],
        attention_total[:, 3 * model_width :],
        gate_up_total[:, :hidden_width],
        gate_up_total[:, hidden_width:],
        down_total,
        gain_totals[0],
        gain_totals[1],
        gain_totals[2],
        gain_totals[3],
    )


def solution(mesh):
    placed = (
        P("fsdp", "seq", None),
        P("fsdp", None),
        P("fsdp", None),
        P("fsdp", None),
        P("fsdp", None),
        P("fsdp", None),
        P("fsdp", None),
        P("fsdp", None),
        P(),
        P(),
        P(),
        P(),
        P("fsdp", "seq", None),
    )
    return jax.shard_map(
        local,
        mesh=mesh,
        in_specs=placed,
        out_specs=(
            P("fsdp", "seq", None),
            P("fsdp", "seq", None),
            P("fsdp", None),
            P("fsdp", None),
            P("fsdp", None),
            P("fsdp", None),
            P("fsdp", None),
            P("fsdp", None),
            P("fsdp", None),
            P(),
            P(),
            P(),
            P(),
        ),
        check_vma=False,
    )
```

profile of v0, /device:TPU:0, one launch (start us, length us, event | category | flops | bytes accessed | tf_op | source)
XLA Modules:
  0.0 2293.0 jit_solution(11662893380696936753)
XLA Ops:
  12.9 54.2 %all-gather.8.cloned.1.call-done = bf16[2048,2048]{1,0:T(8,128)(2,1)} async-done(((bf16[256,2048]{1,0:T(8,128)(2,1)}), bf16[2048,2048]{1,0:T(8,128)(2,1)}) %all-gather.8.cloned.1.call-update) | async-done | bytes 8388624 | tf_op jit(solution)/shard_map/all_gather | solution.py:161
  77.9 45.4 %all-gather.10.cloned.1.call-done = bf16[2048,2048]{1,0:T(8,128)(2,1)} async-done(((bf16[256,2048]{1,0:T(8,128)(2,1)}), bf16[2048,2048]{1,0:T(8,128)(2,1)}) %all-gather.10.cloned.1.call-update) | async-done | bytes 8388624 | tf_op jit(solution)/shard_map/all_gather | solution.py:162
  140.4 39.3 %all-gather.12.cloned.1.call-done = bf16[2048,2048]{1,0:T(8,128)(2,1)} async-done(((bf16[256,2048]{1,0:T(8,128)(2,1)}), bf16[2048,2048]{1,0:T(8,128)(2,1)}) %all-gather.12.cloned.1.call-update) | async-done | bytes 8388624 | tf_op jit(solution)/shard_map/all_gather | solution.py:163
  196.0 93.4 %all-to-all-done = bf16[3,256,2048]{1,0,2:T(4,128)(2,1)} async-done(((bf16[3,256,2048]{1,0,2:T(4,128)(2,1)}), bf16[3,256,2048]{1,0,2:T(4,128)(2,1)}, u32[]{:S(2)}, u32[]{:S(2)}) %all-to-all-start) | async-done | bytes 3145760 | tf_op jit(solution)/shard_map/all_to_all | solution.py:188
  304.6 20.3 while.27
  327.9 29.9 %all_to_all.65 = bf16[4,256,512]{2,1,0:T(8,128)(2,1)} all-to-all(bf16[4,256,512]{2,1,0:T(8,128)(2,1)} %all_to_all.51), channel_id=1, replica_groups=mesh['seq'=4,'fsdp'=8] {'seq'}, dimensions={0} | all-to-all | bytes 2097152 | tf_op jit(solution)/shard_map/all_to_all | solution.py:194
  368.3 30.1 %all-gather.16.cloned.1.call-done = bf16[2048,8192]{1,0:T(8,128)(2,1)} async-done(((bf16[256,8192]{1,0:T(8,128)(2,1)}), bf16[2048,8192]{1,0:T(8,128)(2,1)}) %all-gather.16.cloned.1.call-update) | async-done | bytes 33554448 | tf_op jit(solution)/shard_map/all_gather | solution.py:200
  398.4 20.2 fusion.65
  418.6 142.3 %all-gather.18.cloned.1.call-done = bf16[2048,8192]{1,0:T(8,128)(2,1)} async-done(((bf16[256,8192]{1,0:T(8,128)(2,1)}), bf16[2048,8192]{1,0:T(8,128)(2,1)}) %all-gather.18.cloned.1.call-update) | async-done | bytes 33554448 | tf_op jit(solution)/shard_map/all_gather | solution.py:201
  560.9 26.0 %multiply_convert_fusion.3 = (bf16[256,8192]{1,0:T(8,128)(2,1)}, f32[256,8192]{1,0:T(8,128)}) fusion(f32[256,8192]{1,0:T(8,128)} %fusion.65, bf16[256,2048]{1,0:T(8,128)(2,1)S(1)} %fusion.49, bf16[2048,8192]{1,0:T(8,128)(2,1)} %all-gather.18.cloned.1.call-done), kind=kOutput, calls=%fused_computation.55 | convolution fusion | flops 8602517504 | bytes 55574528 | tf_op jit(solution)/shard_map/dot_general | solution.py:205
  586.9 136.7 %all-gather.20.cloned.1.call-done = bf16[8192,2048]{1,0:T(8,128)(2,1)} async-done(((bf16[1024,2048]{1,0:T(8,128)(2,1)}), bf16[8192,2048]{1,0:T(8,128)(2,1)}) %all-gather.20.cloned.1.call-update) | async-done | bytes 33554448 | tf_op jit(solution)/shard_map/all_gather | solution.py:202
  723.7 16.6 multiply_reduce_fusion.7
  758.0 28.1 %multiply_convert_fusion.1 = (bf16[256,8192]{1,0:T(8,128)(2,1)}, bf16[256,8192]{1,0:T(8,128)(2,1)}) fusion(f32[256,8192]{1,0:T(8,128)} %fusion.65, f32[256,8192]{1,0:T(8,128)} %get-tuple-element.337, bf16[8192,2048]{1,0:T(8,128)(2,1)} %all-gather.20.cloned.1.call-done, f32[256,2048]{1,0:T(8,128)S(1)} %get-tuple-element.339, ...), kind=kOutput, calls=%fused_computation.53 | convolution fusion | flops 8621916160 | bytes 61876224 | tf_op jit(solution)/shard_map/dot_general | solution.py:45
  786.1 23.9 %convert_add_fusion = f32[256,2048]{1,0:T(8,128)} fusion(bf16[256,8192]{1,0:T(8,128)(2,1)} %get-tuple-element.296, bf16[2048,8192]{1,0:T(8,128)(2,1)} %all-gather.16.cloned.1.call-done, bf16[1,256,2048]{2,1,0:T(8,128)(2,1)S(1)} %copy-done.31), kind=kOutput, calls=%fused_computation.67 | convolution fusion | flops 8590983168 | bytes 40894464 | tf_op jit(solution)/shard_map/dot_general | solution.py:45
  810.0 18.3 multiply_reduce_fusion.1
  842.7 26.4 %all-to-all-done.2 = bf16[256,4,512]{2,0,1:T(8,128)(2,1)} async-done(((bf16[256,4,512]{2,0,1:T(8,128)(2,1)}), bf16[256,4,512]{2,0,1:T(8,128)(2,1)}, u32[]{:S(2)}, u32[]{:S(2)}) %all-to-all-start.2) | async-done | bytes 1048608 | tf_op jit(solution)/shard_map/all_to_all | solution.py:240
  872.6 46.9 %while.28 = (s32[]{:T(128)}, f32[1024,4,128]{0,2,1:T(8,128)S(1)}, f32[1024,4,128]{0,2,1:T(8,128)}, bf16[2,512,4,128]{3,2,1,0:T(4,128)(2,1)}, s32[2]{0:T(128)S(1)...) while((s32[]{:T(128)}, f32[1024,4,128]{0,2,1:T(8,128)S(1)}, ...), condition=%wide.region_12.13_spmd.clone, body=%wide.region_10.12_spmd.clone.sunk | while | flops 2719480320 | bytes 190378560 | solution.py:129
  941.4 86.9 %all-to-all-done.3 = bf16[3,1024,512]{2,0,1:T(4,128)(2,1)} async-done(((bf16[3,1024,512]{2,0,1:T(4,128)(2,1)}), bf16[3,1024,512]{2,0,1:T(4,128)(2,1)}, u32[]{:S(2)}, u32[]{:S(2)}) %all-to-all-start.3) | async-done | bytes 3145760 | tf_op jit(solution)/shard_map/all_to_all | solution.py:251
  1071.4 24.0 %pad_maximum_fusion = bf16[2048,8192]{0,1:T(8,128)(2,1)} fusion(bf16[2048,2048]{0,1:T(8,128)(2,1)} %convolution_convert_fusion.2, bf16[2048,6144]{0,1:T(8,128)(2,1)} %convert_bitcast_fusion), kind=kLoop, calls=%fused_computation.47 | loop fusion | flops 67108864 | bytes 67108864 | tf_op jit(solution)/shard_map/concatenate | solution.py:296
  1096.6 42.3 %convolution_convert_fusion = bf16[2048,16384]{1,0:T(8,128)(2,1)} fusion(bf16[256,2048]{1,0:T(8,128)(2,1)S(1)} %copy-done.27, bf16[256,8192]{1,0:T(8,128)(2,1)} %get-tuple-element.295, bf16[256,8192]{1,0:T(8,128)(2,1)} %get-tuple-element.296), kind=kOutput, calls=%fused_computation.46 | convolution fusion | flops 17230200832 | bytes 76546048 | tf_op jit(solution)/shard_map/dot_general | solution.py:51
  1138.9 159.8 %reduce-scatter.4.cloned.1.call-done = bf16[256,8192]{0,1:T(8,128)(2,1)} async-done(((bf16[2048,8192]{0,1:T(8,128)(2,1)}), bf16[256,8192]{0,1:T(8,128)(2,1)}) %reduce-scatter.4.cloned.1.call-update) | async-done | bytes 4194320 | tf_op jit(solution)/shard_map/reduce_scatter | solution.py:295
  1298.8 387.2 %reduce-scatter.6.cloned.1.call-done = bf16[256,16384]{1,0:T(8,128)(2,1)} async-done(((bf16[2048,16384]{1,0:T(8,128)(2,1)}), bf16[256,16384]{1,0:T(8,128)(2,1)}) %reduce-scatter.6.cloned.1.call-update) | async-done | bytes 8388624 | tf_op jit(solution)/shard_map/reduce_scatter | solution.py:289
  1686.7 45.5 %psum.31 = f32[4,2048]{1,0:T(4,128)S(1)} all-reduce(f32[4,2048]{1,0:T(4,128)S(1)} %pad_maximum_fusion.7), channel_id=1, replica_groups=mesh['seq'=4,'fsdp'=8] {'seq','fsdp'}, use_global_device_ids=true, to_apply=%region_25.26 | all-reduce | flops 8192 | bytes 65536 | tf_op jit(solution)/shard_map/psum | solution.py:308
  1749.3 505.1 %all-reduce.3.cloned.1.call-done = (bf16[256,8192]{0,1:T(8,128)(2,1)}, bf16[256,16384]{1,0:T(8,128)(2,1)}, bf16[1024,2048]{1,0:T(8,128)(2,1)}) async-done(((bf16[256,8192]{0,1:T(8,128)(2,1)}, bf16[256,16384]{1,0:T(8,128)(2,1)}, bf16[1024,2048]{1,0:T(8,128)(2,1)}), (bf16[256,8192]{0,1:T(8,128)(2,1)}, bf16[256,16384]{1,0:T(8,128)(2,1)}, bf16[1024,2048]{1,0:T(8,128)(2,1)})) %all-reduce.3.cloned.1.call-update) | async-done | bytes 16777232 | tf_op jit(solution)/shard_map/psum | solution.py:304
  (289 shorter events, 293.7 us)
Async XLA Ops:
  7.2 59.8 %all-gather.8.cloned.1.call-start = ((), (), s32[]{:S(2)}) async-start(), calls=%async_computation.7 | async-start | bytes 9437184 | tf_op jit(solution)/shard_map/all_gather | solution.py:161
  7.9 115.4 %all-gather.10.cloned.1.call-start = ((), (), s32[]{:S(2)}) async-start(), calls=%async_computation.8 | async-start | bytes 9437184 | tf_op jit(solution)/shard_map/all_gather | solution.py:162
  8.7 171.0 %all-gather.12.cloned.1.call-start = ((), (), s32[]{:S(2)}) async-start(), calls=%async_computation.9 | async-start | bytes 9437184 | tf_op jit(solution)/shard_map/all_gather | solution.py:163
  9.4 350.7 %all-gather.14.cloned.1.call-start = ((), (), s32[]{:S(2)}) async-start(), calls=%async_computation.10 | async-start | bytes 9437184 | tf_op jit(solution)/shard_map/all_gather | solution.py:164
  10.0 388.4 %all-gather.16.cloned.1.call-start = ((), (), s32[]{:S(2)}) async-start(), calls=%async_computation.11 | async-start | bytes 37748736 | tf_op jit(solution)/shard_map/all_gather | solution.py:200
  10.6 550.4 %all-gather.18.cloned.1.call-start = ((), (), s32[]{:S(2)}) async-start(), calls=%async_computation.12 | async-start | bytes 37748736 | tf_op jit(solution)/shard_map/all_gather | solution.py:201
  11.1 55.9 %copy-start.22 = (bf16[1,256,2048]{2,1,0:T(8,128)(2,1)S(1)}, bf16[1,256,2048]{2,1,0:T(8,128)(2,1)}, u32[]{:S(2)}) copy-start(bf16[1,256,2048]{2,1,0:T(8,128)(2,1)} %param.17) | copy-start | bytes 3145732
  11.1 712.5 %all-gather.20.cloned.1.call-start = ((), (), s32[]{:S(2)}) async-start(), calls=%async_computation.13 | async-start | bytes 37748736 | tf_op jit(solution)/shard_map/all_gather | solution.py:202
  12.9 122.3 %copy-start.38 = (f32[256,64]{0,1:T(8,128)}, f32[256,64]{0,1:T(8,128)S(1)}, u32[]{:S(2)}) copy-start(f32[256,64]{0,1:T(8,128)S(1)} %get-tuple-element.329) | copy-start | bytes 196612
  12.9 61.3 %copy-start.46 = (f32[2048]{0:T(1024)S(1)}, f32[2048]{0:T(1024)}, u32[]{:S(2)}) copy-start(f32[2048]{0:T(1024)} %param.25) | copy-start | bytes 24580
  77.9 52.6 %copy-start.44 = (f32[2048]{0:T(1024)S(1)}, f32[2048]{0:T(1024)}, u32[]{:S(2)}) copy-start(f32[2048]{0:T(1024)} %param.26) | copy-start | bytes 24580
  190.6 98.8 %all-to-all-start = ((bf16[3,256,2048]{1,0,2:T(4,128)(2,1)}), bf16[3,256,2048]{1,0,2:T(4,128)(2,1)}, u32[]{:S(2)}, u32[]{:S(2)}) async-start(bf16[3,256,2048]{1,0,2:T(4,128)(2,1)} %copy.92), calls=%async_computation | async-start | bytes 8388608 | tf_op jit(solution)/shard_map/all_to_all | solution.py:188
  195.5 943.4 %reduce-scatter.8.cloned.1.call-start = ((), (), s32[]{:S(2)}) async-start(), calls=%async_computation.16 | async-start | bytes 37748736 | tf_op jit(solution)/shard_map/reduce_scatter | solution.py:282
  324.9 35.1 %copy-start.3 = (bf16[1024,4,128]{2,0,1:T(8,128)(2,1)}, bf16[1024,4,128]{2,0,1:T(8,128)(2,1)S(1)}, u32[]{:S(2)}) copy-start(bf16[1024,4,128]{2,0,1:T(8,128)(2,1)S(1)} %get-tuple-element.550) | copy-start | bytes 3145732
  324.9 35.1 %copy-start.7 = (bf16[1024,4,128]{2,0,1:T(8,128)(2,1)}, bf16[1024,4,128]{2,0,1:T(8,128)(2,1)S(1)}, u32[]{:S(2)}) copy-start(bf16[1024,4,128]{2,0,1:T(8,128)(2,1)S(1)} %get-tuple-element.551) | copy-start | bytes 3145732
  324.9 35.1 %copy-start.10 = (bf16[1024,4,128]{2,0,1:T(8,128)(2,1)}, bf16[1024,4,128]{2,0,1:T(8,128)(2,1)S(1)}, u32[]{:S(2)}) copy-start(bf16[1024,4,128]{2,0,1:T(8,128)(2,1)S(1)} %get-tuple-element.552) | copy-start | bytes 3145732
  324.9 35.1 %copy-start.41 = (f32[2,4,512]{2,1,0:T(4,128)}, f32[2,4,512]{2,1,0:T(4,128)S(1)}, u32[]{:S(2)}) copy-start(f32[2,4,512]{2,1,0:T(4,128)S(1)} %get-tuple-element.495) | copy-start | bytes 49156
  368.2 192.7 %copy-start.26 = (bf16[256,2048]{1,0:T(8,128)(2,1)}, bf16[256,2048]{1,0:T(8,128)(2,1)S(1)}, u32[]{:S(2)}) copy-start(bf16[256,2048]{1,0:T(8,128)(2,1)S(1)} %fusion.49) | copy-start | bytes 3145732
  837.9 34.6 %copy-start.42 = (f32[2,4,512]{2,1,0:T(4,128)S(1)}, f32[2,4,512]{2,1,0:T(4,128)}, u32[]{:S(2)}) copy-start(f32[2,4,512]{2,1,0:T(4,128)} %copy-done.41) | copy-start | bytes 49156
  837.9 31.2 %all-to-all-start.2 = ((bf16[256,4,512]{2,0,1:T(8,128)(2,1)}), bf16[256,4,512]{2,0,1:T(8,128)(2,1)}, u32[]{:S(2)}, u32[]{:S(2)}) async-start(bf16[256,4,512]{2,0,1:T(8,128)(2,1)} %bitcast.123), calls=%async_computation.2 | async-start | bytes 2097152 | tf_op jit(solution)/shard_map/all_to_all | solution.py:240
  930.5 97.8 %all-to-all-start.3 = ((bf16[3,1024,512]{2,0,1:T(4,128)(2,1)}), bf16[3,1024,512]{2,0,1:T(4,128)(2,1)}, u32[]{:S(2)}, u32[]{:S(2)}) async-start(bf16[3,1024,512]{2,0,1:T(4,128)(2,1)} %copy.107), calls=%async_computation.3 | async-start | bytes 8388608 | tf_op jit(solution)/shard_map/all_to_all | solution.py:251
  935.6 363.2 %reduce-scatter.4.cloned.1.call-start = ((), (), s32[]{:S(2)}) async-start(), calls=%async_computation.14 | async-start | bytes 37748736 | tf_op jit(solution)/shard_map/reduce_scatter | solution.py:295
  1095.4 590.6 %reduce-scatter.6.cloned.1.call-start = ((), (), s32[]{:S(2)}) async-start(), calls=%async_computation.15 | async-start | bytes 75497472 | tf_op jit(solution)/shard_map/reduce_scatter | solution.py:289
  1138.9 1115.5 %all-reduce.3.cloned.1.call-start = ((), (), s32[]{:S(2)}) async-start(), calls=%async_computation.17 | async-start | bytes 33554432 | tf_op jit(solution)/shard_map/psum | solution.py:304
  (58 other events, 300.2 us)
Sparse Core Ops, SparseCore 0:
  9.9 57.0 all-gather.7
  68.9 54.3 all-gather.9
  125.2 54.3 all-gather.11
  181.4 54.3 all-gather.13
  237.5 160.7 all-gather.15
  400.1 160.7 all-gather.17
  562.8 160.7 all-gather.19
  758.1 205.2 reduce-scatter.7
  1095.5 203.2 reduce-scatter.3
  1302.2 383.7 reduce-scatter.5
  1689.1 565.2 all-reduce.2
where the time goes:
time: 2300 us; the launch traced here: 2290 us
  waiting for transfers between devices  1710 us (74%)
  matrix products  298 us (13%)
  local copies, waits for them, and re-layouts  103 us (4%)
  blocking collectives  75.4 us (3%)
  other arithmetic  72.2 us (3%)
    psum x1, waiting for transfers between devices, local(): lax.psum(attention_shard, 'seq').astype(jnp.float32)  505 us
    reduce_scatter x1, waiting for transfers between devices, local(): lax.psum_scatter(transposed_times(columns, joined).astype(jnp.bfloat16),...  387 us
    reduce_scatter x1, waiting for transfers between devices, local(): lax.psum_scatter(jnp.concatenate([transposed_times(sequence, projected),...  160 us
    all_gather x1, waiting for transfers between devices, local(): lax.all_gather(up_weight, 'fsdp', axis=0, tiled=True)  142 us
    all_gather x1, waiting for transfers between devices, local(): lax.all_gather(down_weight, 'fsdp', axis=0, tiled=True)  137 us
    all_to_all x1, waiting for transfers between devices, local(): lax.all_to_all(stacked, 'seq', split_axis=2, concat_axis=1, tiled=True)  93.4 us
    dot_general x7, matrix products, times_transposed(): lax.dot_general(operand, matrix, (((1,), (1,)), ((), ())), preferred_elem...  92.9 us
    all_to_all x1, waiting for transfers between devices, local(): lax.all_to_all(back_stack, 'seq', split_axis=1, concat_axis=2, tiled=True)  86.9 us
  transfers between devices with their start and end apart: 14, of which 12 were waited for; matrix products, arithmetic and copies ran while one was open for 17% of the time, Pallas kernels for 0%

commit v1 on v0

--- a/solution.py
+++ b/solution.py
@@ -1,6 +1,8 @@
 import jax
 import jax.numpy as jnp
 from jax import lax
+from jax.experimental import pallas as pl
+from jax.experimental.pallas import tpu as pltpu
 from jax.sharding import PartitionSpec as P
 
 HEADS = 16
@@ -326,6 +328,1175 @@
     )
 
 
+MESH = pl.DeviceIdType.MESH
+VMEM_LIMIT = 48 * 1024 * 1024
+
+
+def flip(value, bit):
+    return value + bit - 2 * bit * lax.rem(lax.div(value, bit), 2)
+
+
+def flip_mask(value, mask):
+    for bit in (1, 2, 4):
+        if mask & bit:
+            value = flip(value, bit)
+    return value
+
+
+def place():
+    seq, shard = lax.axis_index("seq"), lax.axis_index("fsdp")
+    return seq, shard
+
+
+def greet(targets):
+    barrier = pltpu.get_barrier_semaphore()
+    for target in targets:
+        pl.semaphore_signal(barrier, inc=1, device_id=target, device_id_type=MESH)
+    pl.semaphore_wait(barrier, len(targets))
+
+
+def remote(source, target_ref, send, receive, device):
+    return pltpu.make_async_remote_copy(
+        src_ref=source,
+        dst_ref=target_ref,
+        send_sem=send,
+        recv_sem=receive,
+        device_id=device,
+        device_id_type=MESH,
+    )
+
+
+def column_others(seq, shard):
+    mate = flip(shard, 1)
+    others = [(lax.rem(seq + step, 4), shard) for step in (1, 2, 3)]
+    return others + [(lax.rem(seq + step, 4), mate) for step in (0, 1, 2, 3)]
+
+
+def ordered(kernel, inputs, after):
+    count, extra = len(inputs), len(after)
+    return lambda *refs: kernel(*refs[:count], *refs[count + extra :])
+
+
+def comm_call(kernel, out_shape, inputs, in_specs, out_specs, scratch, name, number, after=()):
+    return pl.pallas_call(
+        ordered(kernel, inputs, after),
+        out_shape=out_shape,
+        in_specs=list(in_specs) + [ANY] * len(after),
+        out_specs=out_specs,
+        scratch_shapes=scratch,
+        name=name,
+        compiler_params=pltpu.CompilerParams(
+            collective_id=number, has_side_effects=True, vmem_limit_bytes=VMEM_LIMIT
+        ),
+    )(*inputs, *after)
+
+
+def keep_kernel(x, out):
+    out[...] = x[...]
+
+
+def keep_number(x, out):
+    out[0] = x[0]
+
+
+def keep(x, after, space=pltpu.VMEM):
+    return pl.pallas_call(
+        ordered(keep_number if space == pltpu.SMEM else keep_kernel, (x,), after),
+        out_shape=jax.ShapeDtypeStruct(x.shape, x.dtype),
+        in_specs=[pl.BlockSpec(memory_space=space)] + [ANY] * len(after),
+        out_specs=pl.BlockSpec(memory_space=space),
+        name="keep",
+    )(x, *after)
+
+
+ANY = pl.BlockSpec(memory_space=pl.ANY)
+VM = pl.BlockSpec(memory_space=pltpu.VMEM)
+DMA = pltpu.SemaphoreType.DMA
+
+
+def entry_kernel(
+    x, wq, wk, wv, xo, wo, local, x_send, x_recv, fwd_send, w_send, w_recv
+):
+    seq, shard = place()
+    core, half = lax.rem(shard, 2), lax.div(seq, 2)
+    quarter = lax.rem(seq, 2)
+    rows, width = wq.shape[0], wo.shape[1] // 3
+    weights = (wq, wk, wv)
+    greet(
+        [(seq, flip_mask(shard, mask)) for mask in range(1, 8)]
+        + [(lax.rem(seq + step, 4), shard) for step in (1, 2, 3)]
+    )
+    mine = pl.ds(pl.multiple_of(shard * rows, rows), rows)
+
+    def columns(index):
+        return slice(index * width, (index + 1) * width)
+
+    def block(index, target):
+        group = 2 * quarter + lax.rem(target, 2)
+        return weights[index].at[:, pl.ds(pl.multiple_of(group * width, width), width)]
+
+    x_copies = []
+    for which in (0, 1):
+        target = 2 * core + which
+        copy = remote(x, xo.at[seq], x_send.at[which], x_recv.at[seq], (target, shard))
+
+        @pl.when(target != seq)
+        def _():
+            copy.start()
+
+        @pl.when(target == seq)
+        def _():
+            pltpu.make_async_copy(x, xo.at[seq], local.at[3]).start()
+
+        x_copies.append((target, copy))
+    copies = []
+    for index in range(3):
+        for mask in (2, 4, 3, 5, 1):
+            target = flip_mask(shard, mask)
+            copy = remote(
+                block(index, target),
+                wo.at[mine, columns(index)],
+                w_send.at[index, mask - 1],
+                w_recv.at[index, mask - 1],
+                (seq, target),
+            )
+            copy.start()
+            copies.append(copy)
+    own = [
+        pltpu.make_async_copy(block(index, shard), wo.at[mine, columns(index)], local.at[index])
+        for index in range(3)
+    ]
+    for copy in own:
+        copy.start()
+
+    mate = (seq, flip(shard, 1))
+    for turn in range(4):
+        source = lax.rem(seq + turn, 4)
+        forward = remote(
+            xo.at[source], xo.at[source], fwd_send.at[turn], x_recv.at[source], mate
+        )
+
+        @pl.when(core == half)
+        def _():
+            if turn == 0:
+                pltpu.make_async_copy(x, xo.at[seq], local.at[3]).wait()
+            else:
+                forward.wait_recv()
+            forward.start()
+
+    for turn in range(4):
+        source = lax.rem(seq + turn, 4)
+        forward = remote(
+            xo.at[source], xo.at[source], fwd_send.at[turn], x_recv.at[source], mate
+        )
+
+        @pl.when(core == half)
+        def _():
+            forward.wait_send()
+
+        @pl.when(core != half)
+        def _():
+            forward.wait_recv()
+
+    def arrival(index, origin, mask):
+        spot = wo.at[pl.ds(pl.multiple_of(origin * rows, rows), rows), columns(index)]
+        return remote(spot, spot, w_send.at[index, 0], w_recv.at[index, mask - 1], mate)
+
+    base = shard - core
+    side, above = flip(base, 2), flip(base, 4)
+    onward = []
+    for index in range(3):
+        for origin, mask, slot, target in (
+            (side, 2 + core, 6 + core, flip(shard, 4)),
+            (above + 1, 5 - core, 7 - core, flip(shard, 2)),
+        ):
+            arrival(index, origin, mask).wait_recv()
+            spot = wo.at[pl.ds(pl.multiple_of(origin * rows, rows), rows), columns(index)]
+            copy = remote(
+                spot,
+                spot,
+                w_send.at[index, 5 + len(onward) % 2],
+                w_recv.at[index, slot - 1],
+                (seq, target),
+            )
+            copy.start()
+            onward.append(copy)
+    for target, copy in x_copies:
+
+        @pl.when(target != seq)
+        def _():
+            copy.wait_send()
+
+    for copy in own:
+        copy.wait()
+    for copy in copies + onward:
+        copy.wait_send()
+    far = flip_mask(base, 6)
+    for index in range(3):
+        arrival(index, flip(shard, 1), 1).wait_recv()
+        arrival(index, side + 1, 3 - core).wait_recv()
+        arrival(index, above, 4 + core).wait_recv()
+        arrival(index, far, 6 + core).wait_recv()
+        arrival(index, far + 1, 7 - core).wait_recv()
+
+
+def entry(x, wq, wk, wv, number):
+    rows, width = wq.shape
+    group = width // 4
+    return comm_call(
+        entry_kernel,
+        (
+            jax.ShapeDtypeStruct((4,) + x.shape, x.dtype),
+            jax.ShapeDtypeStruct((8 * rows, 3 * group), wq.dtype),
+        ),
+        (x, wq, wk, wv),
+        [ANY] * 4,
+        (ANY, ANY),
+        [DMA((4,)), DMA((2,)), DMA((4,)), DMA((4,)), DMA((3, 7)), DMA((3, 7))],
+        "entry",
+        number,
+    )
+
+
+def stats_kernel(part, total, held, send, receive):
+    seq, shard = place()
+    partners = [
+        (seq, flip(shard, 1)),
+        (flip(seq, 1), shard),
+        (flip(seq, 1), flip(shard, 1)),
+    ]
+    greet(partners)
+    copies = [
+        remote(part, held.at[index], send.at[index], receive.at[index], partner)
+        for index, partner in enumerate(partners)
+    ]
+    for copy in copies:
+        copy.start()
+    for copy in copies:
+        copy.wait()
+    total[...] = (part[...] + held[0]) + (held[1] + held[2])
+
+
+def stats_sum(part, number, after=()):
+    return comm_call(
+        stats_kernel,
+        jax.ShapeDtypeStruct(part.shape, part.dtype),
+        (part,),
+        [VM],
+        VM,
+        [pltpu.VMEM((3,) + part.shape, part.dtype), DMA((3,)), DMA((3,))],
+        "stats",
+        number,
+        after,
+    )
+
+
+def to_tokens_kernel(heads, tokens, local, send, receive):
+    seq, shard = place()
+    core, half = lax.rem(shard, 2), lax.div(seq, 2)
+    base = shard - core
+    width = heads.shape[2]
+    group = 2 * lax.rem(seq, 2) + core
+    greet(column_others(seq, shard))
+    mine = tokens.at[:, pl.ds(pl.multiple_of(group * width, width), width)]
+    steps = []
+    for turn in range(4):
+        target = lax.rem(seq + turn, 4)
+        remote_copy = remote(
+            heads.at[target], mine, send.at[turn], receive.at[group], (target, base + half)
+        )
+        if turn == 0:
+            here = core == half
+            own = pltpu.make_async_copy(heads.at[target], mine, local)
+
+            @pl.when(here)
+            def _():
+                own.start()
+
+            @pl.when(jnp.logical_not(here))
+            def _():
+                remote_copy.start()
+
+        else:
+            remote_copy.start()
+        steps.append(remote_copy)
+    for turn in range(4):
+        if turn == 0:
+
+            @pl.when(here)
+            def _():
+                own.wait()
+
+            @pl.when(jnp.logical_not(here))
+            def _():
+                steps[0].wait_send()
+
+        else:
+            steps[turn].wait_send()
+    for source in range(4):
+        slot = tokens.at[:, source * width : (source + 1) * width]
+        arrival = remote(heads.at[0], slot, send.at[0], receive.at[source], (seq, shard))
+
+        @pl.when(jnp.logical_not(jnp.logical_and(here, group == source)))
+        def _():
+            arrival.wait_recv()
+
+
+def to_tokens(heads, number, after=()):
+    blocks, rows, width = heads.shape
+    return comm_call(
+        to_tokens_kernel,
+        jax.ShapeDtypeStruct((rows, 4 * width), heads.dtype),
+        (heads,),
+        [ANY],
+        ANY,
+        [DMA, DMA((4,)), DMA((4,))],
+        "to_tokens",
+        number,
+        after,
+    )
+
+
+def to_heads_kernel(tokens, heads, local, send, receive):
+    seq, shard = place()
+    core, half = lax.rem(shard, 2), lax.div(seq, 2)
+    base = shard - core
+    width = heads.shape[2]
+    greet(column_others(seq, shard))
+    here = core == half
+    mine = 2 * lax.rem(seq, 2) + core
+    copies = []
+    for group in range(4):
+        target = (2 * core + group // 2, base + group % 2)
+        source = tokens.at[:, group * width : (group + 1) * width]
+        copy = remote(source, heads.at[seq], send.at[group], receive.at[seq], target)
+        own = pltpu.make_async_copy(source, heads.at[seq], local)
+        self_copy = jnp.logical_and(here, mine == group)
+
+        @pl.when(self_copy)
+        def _():
+            own.start()
+
+        @pl.when(jnp.logical_not(self_copy))
+        def _():
+            copy.start()
+
+        copies.append((self_copy, own, copy))
+    for self_copy, own, copy in copies:
+
+        @pl.when(self_copy)
+        def _():
+            own.wait()
+
+        @pl.when(jnp.logical_not(self_copy))
+        def _():
+            copy.wait_send()
+
+    for source in range(4):
+        arrival = remote(
+            tokens.at[:, 0:width], heads.at[source], send.at[0], receive.at[source], (seq, shard)
+        )
+
+        @pl.when(jnp.logical_not(jnp.logical_and(here, seq == source)))
+        def _():
+            arrival.wait_recv()
+
+
+def to_heads(tokens, number, after=()):
+    rows, width = tokens.shape
+    return comm_call(
+        to_heads_kernel,
+        jax.ShapeDtypeStruct((4, rows, width // 4), tokens.dtype),
+        (tokens,),
+        [ANY],
+        ANY,
+        [DMA, DMA((4,)), DMA((4,))],
+        "to_heads",
+        number,
+        after,
+    )
+
+
+def plane_gather_kernel(x, out, local, send, receive):
+    seq, shard = place()
+    core = lax.rem(shard, 2)
+    near = [(seq, flip(shard, bit)) for bit in (2, 4, 1)]
+    greet(near)
+    own = pltpu.make_async_copy(x, out.at[shard], local)
+    own.start()
+    firsts = [
+        remote(x, out.at[shard], send.at[index], receive.at[index], device)
+        for index, device in enumerate(near)
+    ]
+    for copy in firsts:
+        copy.start()
+    mate = near[2]
+
+    def pass_on(slot, index, device):
+        return remote(out.at[slot], out.at[slot], send.at[index], receive.at[index], device)
+
+    first_bit = 2 + 2 * core
+    second_bit = 4 - 2 * core
+    first, second = flip_bit(shard, first_bit), flip_bit(shard, second_bit)
+    diagonal = flip_mask(shard, 6)
+
+    def arrival(slot, index):
+        return remote(out.at[slot], out.at[slot], send.at[0], receive.at[index], mate)
+
+    arrival(first, core).wait_recv()
+    across = pass_on(first, 3, (seq, second))
+    across.start()
+    one = remote(out.at[first], out.at[first], send.at[4], receive.at[4 + core], mate)
+    one.start()
+    arrival(second, 1 - core).wait_recv()
+    two = remote(out.at[second], out.at[second], send.at[5], receive.at[5 - core], mate)
+    two.start()
+    arrival(diagonal, 3).wait_recv()
+    three = pass_on(diagonal, 6, mate)
+    three.start()
+    own.wait()
+    for copy in firsts:
+        copy.wait_send()
+    for copy in (across, one, two, three):
+        copy.wait_send()
+    mate_shard = flip(shard, 1)
+    arrival(mate_shard, 2).wait_recv()
+    arrival(flip(mate_shard, 2), 4).wait_recv()
+    arrival(flip(mate_shard, 4), 5).wait_recv()
+    arrival(flip_mask(mate_shard, 6), 6).wait_recv()
+
+
+def flip_bit(value, bit):
+    return value + bit - 2 * bit * lax.rem(lax.div(value, bit), 2)
+
+
+def plane_gather(x, number, after=()):
+    return comm_call(
+        plane_gather_kernel,
+        jax.ShapeDtypeStruct((8,) + x.shape, x.dtype),
+        (x,),
+        [ANY],
+        ANY,
+        [DMA, DMA((7,)), DMA((7,))],
+        "plane_gather",
+        number,
+        after,
+    )
+
+
+PIECES = 2
+
+
+def add_rows(rows, body):
+    step = 32
+
+    def one(index, carry):
+        body(pl.ds(pl.multiple_of(index * step, step), step))
+        return carry
+
+    lax.fori_loop(0, rows // step, one, 0)
+
+
+def plane_scatter_kernel(part, out, mated, first_in, second_in, sums, sem_s, sem_r):
+    seq, shard = place()
+    core, chip = lax.rem(shard, 2), lax.div(shard, 2)
+    rows = out.shape[0] // PIECES
+    mate = (seq, flip(shard, 1))
+    bit = 1 + core
+    first, second = flip_bit(chip, bit), flip_bit(chip, 3 - bit)
+    diagonal = 3 - chip
+    first_device, second_device = (seq, 2 * first + core), (seq, 2 * second + core)
+    greet([mate, first_device, second_device])
+
+    def piece(index):
+        return pl.ds(index * rows, rows)
+
+    order = (diagonal, first, second, chip)
+    swaps = {}
+    for slot, target in enumerate(order):
+        for index in range(PIECES):
+            copy = remote(
+                part.at[2 * target + 1 - core, piece(index)],
+                mated.at[target, piece(index)],
+                sem_s.at[0, slot, index],
+                sem_r.at[0, target, index],
+                mate,
+            )
+            copy.start()
+            swaps[slot, index] = copy
+
+    def came(target, index):
+        remote(
+            part.at[0, piece(index)],
+            mated.at[target, piece(index)],
+            sem_s.at[0, 0, index],
+            sem_r.at[0, target, index],
+            mate,
+        ).wait_recv()
+
+    sends = []
+    for index in range(PIECES):
+        for slot, target in ((0, diagonal), (1, first)):
+            came(target, index)
+
+            def add(span, slot=slot, target=target, index=index):
+                span = pl.ds(span.start + index * rows, span.size)
+                sums[slot, span] = (
+                    part[2 * target + core, span].astype(jnp.float32)
+                    + mated[target, span].astype(jnp.float32)
+                ).astype(jnp.bfloat16)
+
+            add_rows(rows, add)
+            copy = remote(
+                sums.at[slot, piece(index)],
+                first_in.at[slot, piece(index)],
+                sem_s.at[1, slot, index],
+                sem_r.at[1, slot, index],
+                first_device,
+            )
+            copy.start()
+            sends.append(copy)
+    finals = []
+    for index in range(PIECES):
+        came(second, index)
+        sends[2 * index].wait_recv()
+
+        def add(span, index=index):
+            span = pl.ds(span.start + index * rows, span.size)
+            sums[2, span] = (
+                part[2 * second + core, span].astype(jnp.float32)
+                + mated[second, span].astype(jnp.float32)
+                + first_in[0, span].astype(jnp.float32)
+            ).astype(jnp.bfloat16)
+
+        add_rows(rows, add)
+        copy = remote(
+            sums.at[2, piece(index)],
+            second_in.at[piece(index)],
+            sem_s.at[2, 0, index],
+            sem_r.at[2, 0, index],
+            second_device,
+        )
+        copy.start()
+        finals.append(copy)
+    for index in range(PIECES):
+        came(chip, index)
+        sends[2 * index + 1].wait_recv()
+        finals[index].wait_recv()
+
+        def add(span, index=index):
+            span = pl.ds(span.start + index * rows, span.size)
+            out[span] = (
+                part[shard, span].astype(jnp.float32) + mated[chip, span].astype(jnp.float32)
+            ) + (first_in[1, span].astype(jnp.float32) + second_in[span].astype(jnp.float32))
+
+        add_rows(rows, add)
+    for copy in list(swaps.values()) + sends + finals:
+        copy.wait_send()
+
+
+def plane_scatter(part, number, after=()):
+    _, rows, width = part.shape
+    low = part.dtype
+    return comm_call(
+        plane_scatter_kernel,
+        jax.ShapeDtypeStruct((rows, width), jnp.float32),
+        (part,),
+        [VM],
+        VM,
+        [
+            pltpu.VMEM((4, rows, width), low),
+            pltpu.VMEM((2, rows, width), low),
+            pltpu.VMEM((rows, width), low),
+            pltpu.VMEM((3, rows, width), low),
+            DMA((3, 4, PIECES)),
+            DMA((3, 4, PIECES)),
+        ],
+        "plane_scatter",
+        number,
+        after,
+    )
+
+
+def finish_kernel(
+    part, grads, out_grad, out, placed,
+    mated, sums, landed, first_in, second_in, onward, total, swapped,
+    local, sem_s, sem_r, grad_s, grad_r
+):
+    seq, shard = place()
+    core, half, quarter = lax.rem(shard, 2), lax.div(seq, 2), lax.rem(seq, 2)
+    chip = lax.div(shard, 2)
+    base = shard - core
+    rows = out.shape[0] // 2
+    mate = (seq, flip(shard, 1))
+    bit = 1 + core
+    first, second, diagonal = flip_bit(chip, bit), flip_bit(chip, 3 - bit), 3 - chip
+    first_device, second_device = (seq, 2 * first + core), (seq, 2 * second + core)
+    greet(column_others(seq, shard) + [first_device, second_device])
+    mine = pl.ds(pl.multiple_of(core * rows, rows), rows)
+    other = pl.ds(pl.multiple_of((1 - core) * rows, rows), rows)
+    here = core == half
+    order = [2 * (1 - half) + 1 - quarter, 2 * (1 - half) + quarter, flip(seq, 1), seq]
+    swaps = []
+    for slot, block in enumerate(order):
+        copy = remote(
+            part.at[block, other], mated.at[slot], sem_s.at[0, slot], sem_r.at[0, slot], mate
+        )
+        copy.start()
+        swaps.append(copy)
+    long = grads.shape[1] // 2
+    firsts = []
+    for index in range(2):
+        span = slice(index * long, (index + 1) * long)
+        for slot, target in ((0, diagonal), (1, first)):
+            copy = remote(
+                grads.at[target, span],
+                first_in.at[slot, span],
+                grad_s.at[slot, index],
+                grad_r.at[slot, index],
+                first_device,
+            )
+            copy.start()
+            firsts.append(copy)
+    placed[...] = jnp.zeros_like(placed)
+    width = out_grad.shape[1]
+    placed[:, 3 * width :] = out_grad[...]
+
+    sends = []
+    for slot, block in enumerate(order):
+        swaps[slot].wait_recv()
+
+        def add(span, slot=slot, block=block):
+            source = pl.ds(pl.multiple_of(span.start + core * rows, 32), span.size)
+            sums[slot, span] = (
+                part[block, source].astype(jnp.float32) + mated[slot, span].astype(jnp.float32)
+            ).astype(jnp.bfloat16)
+
+        add_rows(rows, add)
+        copy = remote(
+            sums.at[slot],
+            landed.at[quarter, core],
+            sem_s.at[1, slot],
+            sem_r.at[1, 2 * quarter + core],
+            (block, base + half),
+        )
+        if slot < 3:
+            copy.start()
+        else:
+            own = pltpu.make_async_copy(sums.at[slot], landed.at[quarter, core], local)
+
+            @pl.when(here)
+            def _():
+                own.start()
+
+            @pl.when(jnp.logical_not(here))
+            def _():
+                copy.start()
+
+        sends.append(copy)
+
+    seconds = []
+    for index in range(2):
+        firsts[2 * index].wait_recv()
+
+        def add(span, index=index):
+            span = pl.ds(span.start + index * long, span.size)
+            onward[span] = (
+                grads[second, span].astype(jnp.float32) + first_in[0, span].astype(jnp.float32)
+            ).astype(jnp.bfloat16)
+
+        add_rows(long, add)
+        span = slice(index * long, (index + 1) * long)
+        copy = remote(
+            onward.at[span], second_in.at[span], grad_s.at[2, index], grad_r.at[2, index],
+            second_device,
+        )
+        copy.start()
+        seconds.append(copy)
+    for turn in range(2):
+        start = pl.multiple_of((1 - core if turn == 0 else core) * long, long)
+        if turn == 0:
+            for copy in (firsts[1], firsts[3], seconds[0], seconds[1]):
+                copy.wait_recv()
+
+        def add(span, start=start):
+            span = pl.ds(pl.multiple_of(span.start + start, 32), span.size)
+            total[span] = (
+                (grads[chip, span].astype(jnp.float32) + first_in[1, span].astype(jnp.float32))
+                + second_in[span].astype(jnp.float32)
+            ).astype(jnp.bfloat16)
+
+        add_rows(long, add)
+        if turn == 0:
+            swap = remote(
+                total.at[pl.ds(start, long)], swapped, grad_s.at[3, 0], grad_r.at[3, 0], mate
+            )
+            swap.start()
+    group = 2 * quarter + core
+    part_width = width // 4
+    own_rows = pl.ds(pl.multiple_of(core * long, long), long)
+    for index in range(3):
+        spot = pl.multiple_of(index * width + group * part_width, part_width)
+        placed[:, pl.ds(spot, part_width)] = total[
+            own_rows, index * part_width : (index + 1) * part_width
+        ]
+    swap.wait_recv()
+    for index in range(3):
+        spot = pl.multiple_of(
+            index * width + (2 * quarter + 1 - core) * part_width, part_width
+        )
+        placed[:, pl.ds(spot, part_width)] = swapped[
+            :, index * part_width : (index + 1) * part_width
+        ]
+
+    for slot in range(3):
+        sends[slot].wait_send()
+
+    @pl.when(here)
+    def _():
+        own.wait()
+
+    @pl.when(jnp.logical_not(here))
+    def _():
+        sends[3].wait_send()
+
+    for source in range(4):
+        arrival = remote(
+            sums.at[0],
+            landed.at[source // 2, source % 2],
+            sem_s.at[1, 0],
+            sem_r.at[1, source],
+            mate,
+        )
+
+        @pl.when(jnp.logical_not(jnp.logical_and(here, 2 * quarter + core == source)))
+        def _():
+            arrival.wait_recv()
+
+    for side in range(2):
+
+        def add(span, side=side):
+            target = pl.ds(span.start + side * rows, span.size)
+            out[target] = landed[0, side, span].astype(jnp.float32) + landed[
+                1, side, span
+            ].astype(jnp.float32)
+
+        add_rows(rows, add)
+    for copy in swaps + firsts + seconds + [swap]:
+        copy.wait_send()
+
+
+def finish(part, grads, out_grad, number, after=()):
+    _, rows, width = part.shape
+    _, long, joined = grads.shape
+    low = part.dtype
+    return comm_call(
+        finish_kernel,
+        (
+            jax.ShapeDtypeStruct((rows, width), jnp.float32),
+            jax.ShapeDtypeStruct((long // 2, 4 * width), low),
+        ),
+        (part, grads, out_grad),
+        [VM] * 3,
+        (VM, VM),
+        [
+            pltpu.VMEM((4, rows // 2, width), low),
+            pltpu.VMEM((4, rows // 2, width), low),
+            pltpu.VMEM((2, 2, rows // 2, width), low),
+            pltpu.VMEM((2, long, joined), low),
+            pltpu.VMEM((long, joined), low),
+            pltpu.VMEM((long, joined), low),
+            pltpu.VMEM((long, joined), low),
+            pltpu.VMEM((long // 2, joined), low),
+            DMA,
+            DMA((2, 4)),
+            DMA((2, 4)),
+            DMA((4, 2)),
+            DMA((4, 2)),
+        ],
+        "finish",
+        number,
+        after,
+    )
+
+
+def turn_heads(values, cosine, signed):
+    middle = values.shape[-1] // 2
+    return values * cosine + jnp.concatenate(
+        [values[:, middle:], values[:, :middle]], axis=1
+    ) * signed
+
+
+def dot_nt(a, b):
+    return lax.dot_general(a, b, (((1,), (1,)), ((), ())), preferred_element_type=jnp.float32)
+
+
+def dot_tn(a, b):
+    return lax.dot_general(a, b, (((0,), (0,)), ((), ())), preferred_element_type=jnp.float32)
+
+
+def dot_nn(a, b):
+    return jnp.dot(a, b, preferred_element_type=jnp.float32)
+
+
+ATTENTION_ROWS = 256
+
+
+def causal(scores, start):
+    query = start + lax.broadcasted_iota(jnp.int32, scores.shape, 0)
+    key = lax.broadcasted_iota(jnp.int32, scores.shape, 1)
+    return jnp.where(key <= query, scores, masked_value)
+
+
+def attend_kernel(
+    q_raw, k_raw, v_raw, q_factor, k_factor, q_gain, k_gain, cosine, signed,
+    q_out, k_out, v_out, attended, log_total
+):
+    length, size = q_raw.shape
+    scale = size ** (-0.5)
+    cos, sin = cosine[...], signed[...]
+    q_out[...] = turn_heads(
+        q_raw[...] * q_factor[...] * q_gain[...], cos, sin
+    ).astype(jnp.bfloat16)
+    k_out[...] = turn_heads(
+        k_raw[...] * k_factor[...] * k_gain[...], cos, sin
+    ).astype(jnp.bfloat16)
+    v_out[...] = v_raw[...].astype(jnp.bfloat16)
+    rows = min(ATTENTION_ROWS, length)
+    for start in range(0, length, rows):
+        stop = start + rows
+        scores = dot_nt(q_out[start:stop], k_out[:stop]) * scale
+        scores = causal(scores, start)
+        maximum = jnp.max(scores, axis=-1, keepdims=True)
+        exponent = jnp.exp(scores - maximum)
+        total = jnp.sum(exponent, axis=-1, keepdims=True)
+        weights = (exponent * (1.0 / total)).astype(jnp.bfloat16)
+        attended[start:stop] = dot_nn(weights, v_out[:stop]).astype(jnp.bfloat16)
+        log_total[0, start:stop] = maximum + jnp.log(total)
+
+
+def attend(raw, q_factor, k_factor, q_gain, k_gain, cosine, signed, size, after=()):
+    length, width = raw.shape[0], raw.shape[1] // 3
+    heads = width // size
+    by_head = pl.BlockSpec((length, size), lambda h: (0, h))
+    parts = [
+        pl.BlockSpec((length, size), lambda h, start=index * heads: (0, start + h))
+        for index in range(3)
+    ]
+    fixed = pl.BlockSpec((length, size), lambda h: (0, 0))
+    factor = pl.BlockSpec((length, 1), lambda h: (0, 0))
+    gain = pl.BlockSpec((1, size), lambda h: (0, h))
+    low = jax.ShapeDtypeStruct((length, width), jnp.bfloat16)
+    flops = heads * length * length * size * 2
+    inputs = (raw, raw, raw, q_factor, k_factor, q_gain, k_gain, cosine, signed)
+    return pl.pallas_call(
+        ordered(attend_kernel, inputs, after),
+        grid=(heads,),
+        out_shape=(low, low, low, low, jax.ShapeDtypeStruct((heads, length, 1), jnp.float32)),
+        in_specs=parts + [factor] * 2 + [gain] * 2 + [fixed] * 2 + [ANY] * len(after),
+        out_specs=[by_head] * 4 + [pl.BlockSpec((1, length, 1), lambda h: (h, 0, 0))],
+        name="attend",
+        compiler_params=pltpu.CompilerParams(vmem_limit_bytes=VMEM_LIMIT),
+        cost_estimate=pl.CostEstimate(
+            flops=flops, bytes_accessed=20 * length * width, transcendentals=flops // (4 * size)
+        ),
+    )(*inputs, *after)
+
+
+def attend_back_kernel(
+    queries, keys, values, grads, log_total, cosine, signed, q_grad, k_grad, v_grad, k_sum, v_sum
+):
+    length, size = queries.shape
+    scale = size ** (-0.5)
+    rows = min(ATTENTION_ROWS, length)
+    k_sum[...] = jnp.zeros_like(k_sum)
+    v_sum[...] = jnp.zeros_like(v_sum)
+    for start in range(0, length, rows):
+        stop = start + rows
+        query, grad = queries[start:stop], grads[start:stop]
+        scores = causal(dot_nt(query, keys[:stop]) * scale, start)
+        weights = jnp.exp(scores - log_total[0, start:stop])
+        v_sum[:stop] += dot_tn(weights.astype(jnp.bfloat16), grad)
+        weight_grad = dot_nt(grad, values[:stop])
+        inner = jnp.sum(weights * weight_grad, axis=-1, keepdims=True)
+        score_grad = (weights * (weight_grad - inner)).astype(jnp.bfloat16)
+        q_low = (dot_nn(score_grad, keys[:stop]) * scale).astype(jnp.bfloat16)
+        q_grad[start:stop] = turn_heads(
+            q_low.astype(jnp.float32), cosine[start:stop], -signed[start:stop]
+        )
+        k_sum[:stop] += dot_tn(score_grad, query)
+    k_low = (k_sum[...] * scale).astype(jnp.bfloat16)
+    k_grad[...] = turn_heads(k_low.astype(jnp.float32), cosine[...], -signed[...])
+    v_grad[...] = v_sum[...].astype(jnp.bfloat16)
+
+
+def attend_back(queries, keys, values, grads, log_total, cosine, signed, size, after=()):
+    length, width = queries.shape
+    heads = width // size
+    by_head = pl.BlockSpec((length, size), lambda h: (0, h))
+    fixed = pl.BlockSpec((length, size), lambda h: (0, 0))
+    wide = jax.ShapeDtypeStruct((length, width), jnp.float32)
+    flops = heads * length * length * size * 5
+    inputs = (queries, keys, values, grads, log_total, cosine, signed)
+    return pl.pallas_call(
+        ordered(attend_back_kernel, inputs, after),
+        grid=(heads,),
+        out_shape=(wide, wide, jax.ShapeDtypeStruct((length, width), jnp.bfloat16)),
+        in_specs=[by_head] * 4
+        + [pl.BlockSpec((1, length, 1), lambda h: (h, 0, 0))]
+        + [fixed] * 2
+        + [ANY] * len(after),
+        out_specs=[by_head] * 3,
+        scratch_shapes=[pltpu.VMEM((length, size), jnp.float32)] * 2,
+        name="attend_back",
+        compiler_params=pltpu.CompilerParams(vmem_limit_bytes=VMEM_LIMIT),
+        cost_estimate=pl.CostEstimate(
+            flops=flops, bytes_accessed=20 * length * width, transcendentals=flops // (10 * size)
+        ),
+    )(*inputs, *after)
+
+
+class LineGather:
+    def __init__(self, block):
+        self.seq = lax.axis_index("seq")
+        self.block = block
+        self.up, self.down = [block], [block]
+
+    def step(self):
+        done = len(self.up)
+        up = [(i, i + 1) for i in range(done - 1, 3)]
+        down = [(3 - i, 3 - j) for i, j in up]
+        self.up.append(lax.ppermute(self.up[-1], "seq", up))
+        self.down.append(lax.ppermute(self.down[-1], "seq", down))
+        return (self.up[-1], self.down[-1])
+
+    def blocks(self):
+        while len(self.up) < 4:
+            self.step()
+        seq = self.seq
+        found = [(seq, self.block)]
+        for back in (1, 2, 3):
+            came = jnp.where(seq >= back, self.up[back], self.down[4 - back])
+            found.append((lax.rem(seq + 4 - back, 4), came))
+        return found
+
+
+def line_total(part):
+    for route in ([(0, 1), (3, 2)], [(1, 2), (2, 1)]):
+        part = part + lax.ppermute(part, "seq", route)
+    seq = lax.axis_index("seq")
+    inner = jnp.logical_or(seq == 1, seq == 2)
+    return jnp.where(inner, part, lax.ppermute(part, "seq", [(1, 0), (2, 3)]))
+
+
+def gain_sums(part):
+    for mask in (1, 2, 4):
+        part = part + lax.ppermute(part, "fsdp", [(i, i ^ mask) for i in range(8)])
+    return line_total(part)
+
+
+def split_layer(
+    block_input, query_weight, key_weight, value_weight, out_weight, gate_weight, up_weight,
+    down_weight, query_gain, key_gain, attention_gain, swiglu_gain, cotangent
+):
+    tokens, width = block_input.shape[1:]
+    head_size = width // HEADS
+    seq, shard = lax.axis_index("seq"), lax.axis_index("fsdp")
+    core, chip = lax.rem(shard, 2), lax.div(shard, 2)
+    half, quarter = lax.div(seq, 2), lax.rem(seq, 2)
+    rows = query_weight.shape[0]
+    hidden_width = gate_weight.shape[1] // 8
+    group_width = width // 4
+    group = 2 * quarter + core
+    length = 4 * tokens
+    low = jnp.bfloat16
+    sequence = block_input.reshape(tokens, width)
+
+    whole, qkv = entry(sequence, query_weight, key_weight, value_weight, 1)
+    whole = whole.reshape(length, width)
+    out_full = lax.all_gather(
+        keep(out_weight, (qkv,)), "fsdp", axis=0, tiled=True
+    )
+    shard_later = keep(shard.reshape(1), (qkv,), pltpu.SMEM)[0]
+
+    def columns_of(weight):
+        pieces = {}
+        for mask in (1, 2, 4, 3, 5, 6, 7, 0):
+            partner = flip_mask(shard_later, mask)
+            piece = lax.dynamic_slice_in_dim(weight, partner * hidden_width, hidden_width, 1)
+            if mask:
+                piece = lax.ppermute(piece, "fsdp", [(i, i ^ mask) for i in range(8)])
+            pieces[mask] = piece
+        return pieces
+
+    def joined_columns(pieces):
+        cols = jnp.zeros((8, rows, hidden_width), low)
+        for mask, piece in pieces.items():
+            cols = lax.dynamic_update_index_in_dim(cols, piece, flip_mask(shard, mask), 0)
+        return cols.reshape(width, hidden_width)
+
+    gate_pieces, up_pieces = columns_of(gate_weight), columns_of(up_weight)
+    gate_cols, up_cols = joined_columns(gate_pieces), joined_columns(up_pieces)
+
+    raw = dot_nn(whole, qkv)
+    q_raw, k_raw = raw[:, :group_width], raw[:, group_width : 2 * group_width]
+
+    def reduced(first, second, number, after=()):
+        part = jnp.stack([first, second]).reshape(2 * length // 128, 128)
+        total = stats_sum(part, number, after).reshape(2, length, 1)
+        return total[0] / width, total[1] / width
+
+    q_mean, k_mean = reduced(
+        jnp.sum(q_raw * q_raw, axis=-1), jnp.sum(k_raw * k_raw, axis=-1), 2
+    )
+    q_factor, k_factor = lax.rsqrt(q_mean + epsilon), lax.rsqrt(k_mean + epsilon)
+    cosine, sine = rotary_tables(length, 0, head_size)
+    cosine = jnp.concatenate([cosine[:, 0], cosine[:, 0]], axis=1)
+    signed = jnp.concatenate([-sine[:, 0], sine[:, 0]], axis=1)
+    q_gain_part = lax.dynamic_slice_in_dim(query_gain, group * group_width, group_width)[None]
+    k_gain_part = lax.dynamic_slice_in_dim(key_gain, group * group_width, group_width)[None]
+    queries, keys, values, attended_heads, log_total = attend(
+        raw, q_factor, k_factor, q_gain_part, k_gain_part, cosine, signed, head_size,
+        tuple(gate_pieces[mask] for mask in (1, 2, 4, 3)),
+    )
+    attended = to_tokens(
+        attended_heads.reshape(4, tokens, group_width),
+        3,
+        tuple(gate_pieces[mask] for mask in (5, 6, 7)) + (up_pieces[1], up_pieces[2]),
+    )
+    branch = dot_nn(attended, out_full)
+    branch_factor = norm_factor(branch)
+    residual = sequence.astype(jnp.float32) + branch * branch_factor * attention_gain
+
+    plane = plane_gather(
+        residual.astype(low), 4, tuple(up_pieces[mask] for mask in (4, 3, 5, 6, 7))
+    ).reshape(8 * tokens, width)
+    gate_value = dot_nn(plane, gate_cols)
+    upward = dot_nn(plane, up_cols)
+    sigmoid_gate = jax.nn.sigmoid(gate_value)
+    hidden = (gate_value * sigmoid_gate * upward).astype(low)
+    mixed_part = dot_nn(hidden, down_weight).astype(low)
+    mixed_out = plane_scatter(mixed_part.reshape(8, tokens, width), 5)
+    mixed_factor = norm_factor(mixed_out)
+    output = residual + mixed_out * mixed_factor * swiglu_gain
+    upstream = cotangent.reshape(tokens, width).astype(jnp.float32)
+    mixed_float, swiglu_gain_grad = norm_backward(mixed_out, mixed_factor, swiglu_gain, upstream)
+    mixed_plane = plane_gather(mixed_float.astype(low), 6).reshape(8 * tokens, width)
+    down_grad = transposed_times(hidden, mixed_plane).astype(low)
+    down_block = lax.psum_scatter(down_grad, "seq", scatter_dimension=0, tiled=True)
+    hidden_grad = times_transposed(mixed_plane, down_weight)
+    gate_grad = (
+        hidden_grad * upward * sigmoid_gate * (1.0 + gate_value * (1.0 - sigmoid_gate))
+    ).astype(low)
+    up_grad = (hidden_grad * (gate_value * sigmoid_gate)).astype(low)
+    residual_part = (
+        times_transposed(gate_grad, gate_cols) + times_transposed(up_grad, up_cols)
+    ).astype(low)
+    gate_sum = transposed_times(plane, gate_grad).astype(low).reshape(8, rows, hidden_width)
+    gate_block = lax.psum_scatter(gate_sum, "seq", scatter_dimension=1, tiled=True)
+    up_sum = transposed_times(plane, up_grad).astype(low).reshape(8, rows, hidden_width)
+    up_block = lax.psum_scatter(up_sum, "seq", scatter_dimension=1, tiled=True)
+    residual_grad = upstream + plane_scatter(
+        residual_part.reshape(8, tokens, width), 7, (down_block, gate_sum, up_sum)
+    )
+
+    down_line = LineGather(down_block)
+
+    branch_float, attention_gain_grad = norm_backward(
+        branch, branch_factor, attention_gain, residual_grad
+    )
+    branch_grad = branch_float.astype(low)
+    attended_grad = times_transposed(branch_grad, out_full).astype(low)
+    head_grad = to_heads(attended_grad, 8).reshape(length, group_width)
+    out_grad = lax.psum_scatter(
+        transposed_times(attended, branch_grad).astype(low), "fsdp", scatter_dimension=0, tiled=True
+    )
+    q_norm_grad, k_norm_grad, value_grad = attend_back(
+        queries, keys, values, head_grad, log_total, cosine, signed, head_size,
+        (gate_block,),
+    )
+    q_scaled, k_scaled = q_norm_grad * q_gain_part, k_norm_grad * k_gain_part
+    q_inner, k_inner = reduced(
+        jnp.sum(q_scaled * q_raw, axis=-1), jnp.sum(k_scaled * k_raw, axis=-1), 9
+    )
+    q_gain_sum = jnp.sum(q_norm_grad * q_raw * q_factor, axis=0)
+    k_gain_sum = jnp.sum(k_norm_grad * k_raw * k_factor, axis=0)
+    q_raw_grad = (q_factor * q_scaled - q_raw * (q_factor * q_factor * q_factor * q_inner)).astype(low)
+    k_raw_grad = (k_factor * k_scaled - k_raw * (k_factor * k_factor * k_factor * k_inner)).astype(low)
+    joined = jnp.concatenate([q_raw_grad, k_raw_grad, value_grad], axis=1)
+    input_part = times_transposed(joined, qkv).astype(low)
+    qkv_grad = transposed_times(whole, joined).astype(low)
+    input_sum, attention_part = finish(
+        input_part.reshape(4, tokens, width),
+        qkv_grad.reshape(4, 2 * rows, 3 * group_width),
+        out_grad,
+        10,
+        (up_block,) + down_line.step() + down_line.step() + down_line.step(),
+    )
+    input_grad = residual_grad + input_sum
+
+    share = rows // 4
+
+    def owned(block):
+        full = jnp.zeros((share, 8 * hidden_width), low)
+        for mask in (1, 2, 4, 3, 5, 6, 7, 0):
+            partner = flip_mask(shard, mask)
+            piece = lax.dynamic_index_in_dim(block, partner, 0, keepdims=False)
+            if mask:
+                piece = lax.ppermute(piece, "fsdp", [(i, i ^ mask) for i in range(8)])
+            full = lax.dynamic_update_slice(full, piece, (0, partner * hidden_width))
+        return full
+
+    gate_line, up_line = LineGather(owned(gate_block)), LineGather(owned(up_block))
+    attention_line = LineGather(
+        lax.psum_scatter(attention_part, "seq", scatter_dimension=0, tiled=True)
+    )
+
+    def whole_line(line):
+        blocks = line.blocks()
+        count, columns = line.block.shape
+        total = jnp.zeros((4 * count, columns), jnp.float32)
+        for slot, block in blocks:
+            total = lax.dynamic_update_slice(
+                total, block.astype(jnp.float32), (slot * count, 0)
+            )
+        return total
+
+    down_total, gate_total, up_total = map(whole_line, (down_line, gate_line, up_line))
+    attention_total = whole_line(attention_line)
+    query_total, key_total, value_total, out_total = (
+        attention_total[:, index * width : (index + 1) * width] for index in range(4)
+    )
+
+    def widen(part):
+        return lax.dynamic_update_slice(
+            jnp.zeros((width,), jnp.float32), part, (group * group_width,)
+        )
+
+    gain_totals = gain_sums(
+        jnp.stack([widen(q_gain_sum), widen(k_gain_sum), attention_gain_grad, swiglu_gain_grad])
+    )
+    return (
+        output.reshape(1, tokens, width),
+        input_grad.reshape(1, tokens, width),
+        query_total,
+        key_total,
+        value_total,
+        out_total,
+        gate_total,
+        up_total,
+        down_total,
+        gain_totals[0],
+        gain_totals[1],
+        gain_totals[2],
+        gain_totals[3],
+    )
+
+
+def fits(mesh):
+    return mesh.shape["seq"] == 4 and mesh.shape["fsdp"] == 8
+
+
 def solution(mesh):
     placed = (
         P("fsdp", "seq", None),
@@ -343,7 +1514,7 @@
         P("fsdp", "seq", None),
     )
     return jax.shard_map(
-        local,
+        split_layer if fits(mesh) else local,
         mesh=mesh,
         in_specs=placed,
         out_specs=(

time: 2300 us -> 1210 us (0.53)
  waiting for transfers between devices: 1710 us -> 323 us
  Pallas kernels: 0 us -> 485 us
  matrix products: 298 us -> 180 us
  blocking collectives: 75.4 us -> 0 us
  starting transfers between devices: 15.6 us -> 81.7 us
  local copies, waits for them, and re-layouts: 103 us -> 66.2 us
  other arithmetic: 72.2 us -> 44.5 us
    psum x1 -> x0, waiting for transfers between devices: 505 us -> none  [local(): lax.psum(attention_shard, 'seq').astype(jnp.float32)]
    pallas_call x0 -> x14, Pallas kernels: none -> 485 us  [the longest x10 450 us: comm_call(): pl.pallas_call(ordered(kernel, inputs, after), out_shape=out_shape, in_sp...]
    reduce_scatter x3 -> x5, waiting for transfers between devices: 547 us -> 67.5 us  [the longest x1 67.5 us: split_layer(): lax.psum_scatter(attention_part, 'seq', scatter_dimension=0, tiled=True)]
    all_gather x7 -> x1, waiting for transfers between devices: 448 us -> 0.01 us  [split_layer(): lax.all_gather(keep(out_weight, (qkv,)), 'fsdp', axis=0, tiled=True)]
    ppermute x0 -> x58, waiting for transfers between devices: none -> 255 us  [the longest x12 129 us: step(): self.down.append(lax.ppermute(self.down[-1], 'seq', down))]
    all_to_all x3 -> x0, waiting for transfers between devices: 207 us -> none  [the longest x1 93.4 us: local(): lax.all_to_all(stacked, 'seq', split_axis=2, concat_axis=1, tiled=True)]
    ppermute x0 -> x58, starting transfers between devices: none -> 80.9 us  [the longest x12 29.4 us: step(): self.up.append(lax.ppermute(self.up[-1], 'seq', up))]
    dot_general x21 -> x5, matrix products: 128 us -> 56.6 us  [dot_nn(): return jnp.dot(a, b, preferred_element_type=jnp.float32)]
  transfers between devices with their start and end apart: 14 -> 64, of which waited for: 12 -> 22; matrix products, arithmetic and copies ran while one was open for 17% -> 17% of each run, Pallas kernels for 0% -> 22%
where the time goes in v1:
time: 1210 us; the launch traced here: 1200 us
  Pallas kernels  485 us (40%)
  waiting for transfers between devices  323 us (27%)
  matrix products  180 us (15%)
  starting transfers between devices  81.7 us (7%)
  local copies, waits for them, and re-layouts  66.2 us (5%)
  other arithmetic  44.5 us (4%)
  between operations  21.1 us (2%)
    pallas_call x10, Pallas kernels, comm_call(): pl.pallas_call(ordered(kernel, inputs, after), out_shape=out_shape, in_sp...  450 us
    ppermute x12, waiting for transfers between devices, step(): self.down.append(lax.ppermute(self.down[-1], 'seq', down))  129 us
    reduce_scatter x1, waiting for transfers between devices, split_layer(): lax.psum_scatter(attention_part, 'seq', scatter_dimension=0, tiled=True)  67.5 us
    dot_general x5, matrix products, times_transposed(): lax.dot_general(operand, matrix, (((1,), (1,)), ((), ())), preferred_elem...  66.8 us
    dot_general x5, matrix products, dot_nn(): return jnp.dot(a, b, preferred_element_type=jnp.float32)  56.6 us
    dot_general x5, matrix products, transposed_times(): lax.dot_general(operand, matrix, (((0,), (0,)), ((), ())), preferred_elem...  56.1 us
    ppermute x14, waiting for transfers between devices, columns_of(): piece = lax.ppermute(piece, 'fsdp', [(i, i ^ mask) for i in range(8)])  54 us
    ppermute x12, starting transfers between devices, step(): self.up.append(lax.ppermute(self.up[-1], 'seq', up))  29.4 us
  transfers between devices with their start and end apart: 64, of which 22 were waited for; matrix products, arithmetic and copies ran while one was open for 17% of the time, Pallas kernels for 22%

profile of v1, /device:TPU:0, one launch (start us, length us, event | category | flops | bytes accessed | tf_op | source)
XLA Modules:
  0.0 1200.8 jit_solution(15331270853944034932)
XLA Ops:
  12.1 67.0 %entry.1 = (bf16[4,256,2048]{2,1,0:T(8,128)(2,1)}, bf16[2048,1536]{1,0:T(8,128)(2,1)}) custom-call(bf16[256,2048]{1,0:T(8,128)(2,1)S(1)} %bitcast.154, bf16[256,2048]{1,0:T(8,128)(2,1)S(1)} %copy-done.28, bf16[256,2048]{1,0:T(8,128)(2,1)S(1)} %copy-done.29, bf16[256,2048]{1,0:T(8,128)(2,1)S(1)} %copy-done.30), custom_call_target="tpu_custom_call" | custom-call | tf_op jit(solution)/shard_map/entry/pallas_call | solution.py:381
  106.6 17.7 %stats.2 = f32[16,128]{1,0:T(8,128)S(1)} custom-call(f32[16,128]{1,0:T(8,128)S(1)} %reshape.237.refs_0_), custom_call_target="tpu_custom_call" | custom-call | tf_op jit(solution)/shard_map/stats/pallas_call | solution.py:381
  139.9 16.3 %collective-permute-done.8.refs_5_ = bf16[256,1024]{1,0:T(8,128)(2,1)S(1)} collective-permute-done((bf16[256,1024]{1,0:T(8,128)(2,1)}, bf16[256,1024]{1,0:T(8,128)(2,1)S(1)}, u32[]{:S(2)}, u32[]{:S(2)}) %collective-permute-start.8) | collective-permute-done | bytes 524320 | tf_op jit(solution)/shard_map/ppermute | solution.py:1328
  161.0 26.2 %collective-permute-done.9.refs_1_ = bf16[256,1024]{1,0:T(8,128)(2,1)S(1)} collective-permute-done((bf16[256,1024]{1,0:T(8,128)(2,1)S(1)}, bf16[256,1024]{1,0:T(8,128)(2,1)S(1)}, u32[]{:S(2)}, u32[]{:S(2)}) %collective-permute-start.9) | collective-permute-done | bytes 524320 | tf_op jit(solution)/shard_map/ppermute | solution.py:1328
  197.3 15.7 %attend.1 = (bf16[1024,512]{1,0:T(8,128)(2,1)S(1)}, bf16[1024,512]{1,0:T(8,128)(2,1)}, bf16[1024,512]{1,0:T(8,128)(2,1)}, bf16[1024,512]{1,0:T(8,128)(2,1)}, f32[4,1024,1]{2,1,0:T(8,128)}) custom-call(f32[1024,1536]{1,0:T(8,128)} %copy-done.40, f32[1024,1536]{1,0:T(8,128)} %copy-done.40, f32[1024,1536]{1,0:T(8,128)} %copy-done.40, ...), custom_call_target="tpu_custom_call" | custom-call | flops 1073741824 | bytes 10485760 | tf_op jit(solution)/shard_map/attend/pallas_call | solution.py:1192
  225.8 26.8 %to_tokens.1 = bf16[256,2048]{1,0:T(8,128)(2,1)S(1)} custom-call(bf16[4,256,512]{2,1,0:T(8,128)(2,1)S(1)} %bitcast.156, bf16[256,1024]{1,0:T(8,128)(2,1)S(1)} %collective-permute-done.4.refs_1_, bf16[256,1024]{1,0:T(8,128)(2,1)S(1)} %collective-permute-done.5.refs_2_, bf16[256,1024]{1,0:T(8,128)(2,1)S(1)} %collective-permute-done.6.refs_3_, ...), custom_call_target="tpu_custom_call" | custom-call | tf_op jit(solution)/shard_map/to_tokens/pallas_call | solution.py:381
  267.0 54.5 %plane_gather.2 = bf16[8,256,2048]{2,1,0:T(8,128)(2,1)} custom-call(bf16[256,2048]{1,0:T(8,128)(2,1)S(1)} %fusion.8.refs_0_, bf16[256,1024]{1,0:T(8,128)(2,1)S(1)} %copy-done.19, bf16[256,1024]{1,0:T(8,128)(2,1)S(1)} %copy-done.21, bf16[256,1024]{1,0:T(8,128)(2,1)S(1)} %copy-done.23, bf16[256,1024]{1,0:T(8,128)(2,1)S(1)} %copy-done.25, ...), custom_call_target="tpu_custom_call" | custom-call | tf_op jit(solution)/shard_map/plane_gather/pallas_call | solution.py:381
  363.4 48.4 %plane_scatter.2 = f32[256,2048]{1,0:T(8,128)S(1)} custom-call(bf16[8,256,2048]{2,1,0:T(8,128)(2,1)} %bitcast.163), custom_call_target="tpu_custom_call" | custom-call | tf_op jit(solution)/shard_map/plane_scatter/pallas_call | solution.py:381
  413.4 47.7 %plane_gather.3 = bf16[8,256,2048]{2,1,0:T(8,128)(2,1)} custom-call(bf16[256,2048]{1,0:T(8,128)(2,1)S(1)} %fusion.4.refs_0_), custom_call_target="tpu_custom_call" | custom-call | tf_op jit(solution)/shard_map/plane_gather/pallas_call | solution.py:381
  474.1 22.4 %multiply_convert_fusion.1 = (bf16[2048,1024]{1,0:T(8,128)(2,1)S(1)}, bf16[2048,1024]{1,0:T(8,128)(2,1)}) fusion(f32[2048,1024]{1,0:T(8,128)} %fusion.20, f32[2048,1024]{1,0:T(8,128)} %get-tuple-element.103, bf16[2048,2048]{1,0:T(8,128)(2,1)} %bitcast.165, bf16[1024,2048]{1,0:T(8,128)(2,1)} %param.20), kind=kOutput, calls=%fused_computation.2 | convolution fusion | flops 8617197568 | bytes 37748736 | tf_op jit(solution)/shard_map/dot_general | solution.py:47
  525.5 15.4 %fusion.21 = f32[2048,2048]{1,0:T(8,128)} fusion(bf16[2048,1024]{1,0:T(8,128)(2,1)} %get-tuple-element.50, bf16[2048,1024]{1,0:T(8,128)(2,1)} %bitcast.172), kind=kOutput, calls=%fused_computation.150 | convolution fusion | flops 8589934592 | bytes 25165824 | tf_op jit(solution)/shard_map/dot_general | solution.py:47
  540.9 15.3 %add_convert_fusion = bf16[2048,2048]{1,0:T(8,128)(2,1)} fusion(f32[2048,2048]{1,0:T(8,128)} %fusion.21, bf16[2048,1024]{1,0:T(8,128)(2,1)S(1)} %copy-done.85, bf16[2048,1024]{1,0:T(8,128)(2,1)} %bitcast.20), kind=kOutput, calls=%fused_computation | convolution fusion | flops 8598323200 | bytes 33554432 | tf_op jit(solution)/shard_map/dot_general | solution.py:47
  557.5 48.6 %plane_scatter.3 = f32[256,2048]{1,0:T(8,128)S(1)} custom-call(bf16[8,256,2048]{2,1,0:T(8,128)(2,1)} %bitcast.170, bf16[256,2048]{1,0:T(8,128)(2,1)S(1)} %copy-done.8, bf16[8,256,1024]{2,1,0:T(8,128)(2,1)} %bitcast.162, bf16[8,256,1024]{2,1,0:T(8,128)(2,1)} %bitcast.160), custom_call_target="tpu_custom_call" | custom-call | tf_op jit(solution)/shard_map/plane_scatter/pallas_call | solution.py:381
  614.0 29.9 %to_heads.1 = bf16[4,256,512]{2,1,0:T(8,128)(2,1)S(1)} custom-call(bf16[256,2048]{1,0:T(8,128)(2,1)S(1)} %convolution_convert_fusion.7.refs_0_), custom_call_target="tpu_custom_call" | custom-call | tf_op jit(solution)/shard_map/to_heads/pallas_call | solution.py:381
  646.2 16.4 %attend_back.1 = (f32[1024,512]{1,0:T(8,128)}, f32[1024,512]{1,0:T(8,128)}, bf16[1024,512]{1,0:T(8,128)(2,1)S(1)}) custom-call(bf16[1024,512]{1,0:T(8,128)(2,1)S(1)} %copy-done.35, bf16[1024,512]{1,0:T(8,128)(2,1)S(1)} %copy-done.36, bf16[1024,512]{1,0:T(8,128)(2,1)S(1)} %copy-done.37, bf16[1024,512]{1,0:T(8,128)(2,1)} %bitcast.155, ...), custom_call_target="tpu_custom_call" | custom-call | flops 2684354560 | bytes 10485760 | tf_op jit(solution)/shard_map/attend_back/pallas_call | solution.py:1241
  670.1 20.5 %stats.3 = f32[16,128]{1,0:T(8,128)S(1)} custom-call(f32[16,128]{1,0:T(8,128)S(1)} %reshape.250.refs_0_), custom_call_target="tpu_custom_call" | custom-call | tf_op jit(solution)/shard_map/stats/pallas_call | solution.py:381
  752.6 19.7 %collective-permute-done.55 = f32[4,2048]{1,0:T(4,128)S(1)} collective-permute-done((f32[4,2048]{1,0:T(4,128)S(1)}, f32[4,2048]{1,0:T(4,128)S(1)}, u32[]{:S(2)}, u32[]{:S(2)}) %collective-permute-start.55) | collective-permute-done | bytes 32800 | tf_op jit(solution)/shard_map/ppermute | solution.py:1286
  890.4 18.9 %collective-permute-done.35 = bf16[64,8192]{1,0:T(8,128)(2,1)} collective-permute-done((bf16[64,8192]{1,0:T(8,128)(2,1)S(1)}, bf16[64,8192]{1,0:T(8,128)(2,1)}, u32[]{:S(2)}, u32[]{:S(2)}) %collective-permute-start.35) | collective-permute-done | bytes 1048608 | tf_op jit(solution)/shard_map/ppermute | solution.py:1270
  912.3 19.4 %collective-permute-done.19.refs_9_ = bf16[256,2048]{1,0:T(8,128)(2,1)S(1)} collective-permute-done((bf16[256,2048]{1,0:T(8,128)(2,1)S(1)}, bf16[256,2048]{1,0:T(8,128)(2,1)S(1)}, u32[]{:S(2)}, u32[]{:S(2)}) %collective-permute-start.19) | collective-permute-done | bytes 1048608 | tf_op jit(solution)/shard_map/ppermute | solution.py:1270
  937.5 89.2 %finish.1 = (f32[256,2048]{1,0:T(8,128)}, bf16[256,8192]{1,0:T(8,128)(2,1)}) custom-call(bf16[4,256,2048]{2,1,0:T(8,128)(2,1)} %bitcast.174, bf16[4,512,1536]{2,1,0:T(8,128)(2,1)} %bitcast.171, bf16[256,2048]{1,0:T(8,128)(2,1)S(1)} %copy-done.26, bf16[8,64,1024]{2,1,0:T(8,128)(2,1)S(1)} %copy-done.7, bf16[256,2048]{1,0:T(8,128)(2,1)S(1)} %collective-permute-done.14.refs_4_, ...), custom_call_target="tpu_custom_call" | custom-call | tf_op jit(solution)/shard_map/finish/pallas_call | solution.py:381
  1042.6 67.5 %reduce-scatter.14.cloned.1.call-done = bf16[64,8192]{1,0:T(8,128)(2,1)} async-done(((bf16[256,8192]{1,0:T(8,128)(2,1)}), bf16[64,8192]{1,0:T(8,128)(2,1)}) %reduce-scatter.14.cloned.1.call-update) | async-done | bytes 1048592 | tf_op jit(solution)/shard_map/reduce_scatter | solution.py:1452
  1119.0 18.3 %collective-permute-done.21 = bf16[64,8192]{1,0:T(8,128)(2,1)S(1)} collective-permute-done((bf16[64,8192]{1,0:T(8,128)(2,1)}, bf16[64,8192]{1,0:T(8,128)(2,1)S(1)}, u32[]{:S(2)}, u32[]{:S(2)}) %collective-permute-start.21) | collective-permute-done | bytes 1048608 | tf_op jit(solution)/shard_map/ppermute | solution.py:1270
  1144.1 19.5 %collective-permute-done.22 = bf16[64,8192]{1,0:T(8,128)(2,1)S(1)} collective-permute-done((bf16[64,8192]{1,0:T(8,128)(2,1)S(1)}, bf16[64,8192]{1,0:T(8,128)(2,1)S(1)}, u32[]{:S(2)}, u32[]{:S(2)}) %collective-permute-start.22) | collective-permute-done | bytes 1048608 | tf_op jit(solution)/shard_map/ppermute | solution.py:1270
  1166.8 22.3 %collective-permute-done.23 = bf16[64,8192]{1,0:T(8,128)(2,1)S(1)} collective-permute-done((bf16[64,8192]{1,0:T(8,128)(2,1)S(1)}, bf16[64,8192]{1,0:T(8,128)(2,1)S(1)}, u32[]{:S(2)}, u32[]{:S(2)}) %collective-permute-start.23) | collective-permute-done | bytes 1048608 | tf_op jit(solution)/shard_map/ppermute | solution.py:1270
  (416 shorter events, 416.0 us)
Async XLA Ops:
  7.2 251.6 %all-gather.2.cloned.1.call-start = ((), (), s32[]{:S(2)}) async-start(), calls=%async_computation.5 | async-start | bytes 9437184 | tf_op jit(solution)/shard_map/all_gather | solution.py:1317
  81.4 474.8 %reduce-scatter.6.cloned.1.call-start = ((), (), s32[]{:S(2)}) async-start(), calls=%async_computation.6 | async-start | bytes 5242880 | tf_op jit(solution)/shard_map/reduce_scatter | solution.py:1386
  91.0 68.0 %collective-permute-start.2 = (bf16[256,1024]{1,0:T(8,128)(2,1)}, bf16[256,1024]{1,0:T(8,128)(2,1)}, u32[]{:S(2)}, u32[]{:S(2)}) collective-permute-start(bf16[256,1024]{1,0:T(8,128)(2,1)} %get-tuple-element.68), channel_id=1, source_target_pairs={{0,4},{1,5},{2,6},{3,7},{4,0},{5,1},{6,2},{7,3},{8,12},{9,13},{10,... | collective-permute-start | bytes 1572872 | tf_op jit(solution)/shard_map/ppermute | solution.py:1328
  92.2 95.0 %collective-permute-start.3 = (bf16[256,1024]{1,0:T(8,128)(2,1)}, bf16[256,1024]{1,0:T(8,128)(2,1)}, u32[]{:S(2)}, u32[]{:S(2)}) collective-permute-start(bf16[256,1024]{1,0:T(8,128)(2,1)} %get-tuple-element.67), channel_id=1, source_target_pairs={{0,3},{1,2},{2,1},{3,0},{4,7},{5,6},{6,5},{7,4},{8,11},{9,10},{10,... | collective-permute-start | bytes 1572872 | tf_op jit(solution)/shard_map/ppermute | solution.py:1328
  135.4 56.6 %collective-permute-start.4 = (bf16[256,1024]{1,0:T(8,128)(2,1)S(1)}, bf16[256,1024]{1,0:T(8,128)(2,1)S(1)}, u32[]{:S(2)}, u32[]{:S(2)}) collective-permute-start(bf16[256,1024]{1,0:T(8,128)(2,1)S(1)} %copy-done.70), channel_id=1, source_target_pairs={{0,5},{1,4},{2,7},{3,6},{4,1},{5,0},{6,3},{7,2},{8,13},{9,12},{10,... | collective-permute-start | bytes 1572872 | tf_op jit(solution)/shard_map/ppermute | solution.py:1328
  138.4 48.7 %collective-permute-start.9 = (bf16[256,1024]{1,0:T(8,128)(2,1)S(1)}, bf16[256,1024]{1,0:T(8,128)(2,1)S(1)}, u32[]{:S(2)}, u32[]{:S(2)}) collective-permute-start(bf16[256,1024]{1,0:T(8,128)(2,1)S(1)} %copy-done.72), channel_id=1, source_target_pairs={{0,4},{1,5},{2,6},{3,7},{4,0},{5,1},{6,2},{7,3},{8,12},{9,13},{10,... | collective-permute-start | bytes 1572872 | tf_op jit(solution)/shard_map/ppermute | solution.py:1328
  187.1 65.5 %collective-permute-start.11 = (bf16[256,1024]{1,0:T(8,128)(2,1)S(1)}, bf16[256,1024]{1,0:T(8,128)(2,1)S(1)}, u32[]{:S(2)}, u32[]{:S(2)}) collective-permute-start(bf16[256,1024]{1,0:T(8,128)(2,1)S(1)} %copy-done.68), channel_id=1, source_target_pairs={{0,5},{1,4},{2,7},{3,6},{4,1},{5,0},{6,3},{7,2},{8,13},{9,12},{10,... | collective-permute-start | bytes 1572872 | tf_op jit(solution)/shard_map/ppermute | solution.py:1328
  187.2 65.5 %collective-permute-start.12 = (bf16[256,1024]{1,0:T(8,128)(2,1)S(1)}, bf16[256,1024]{1,0:T(8,128)(2,1)S(1)}, u32[]{:S(2)}, u32[]{:S(2)}) collective-permute-start(bf16[256,1024]{1,0:T(8,128)(2,1)S(1)} %copy-done.67), channel_id=1, source_target_pairs={{0,6},{1,7},{2,4},{3,5},{4,2},{5,3},{6,0},{7,1},{8,14},{9,15},{10,... | collective-permute-start | bytes 1572872 | tf_op jit(solution)/shard_map/ppermute | solution.py:1328
  191.7 61.1 %collective-permute-start.13 = (bf16[256,1024]{1,0:T(8,128)(2,1)S(1)}, bf16[256,1024]{1,0:T(8,128)(2,1)S(1)}, u32[]{:S(2)}, u32[]{:S(2)}) collective-permute-start(bf16[256,1024]{1,0:T(8,128)(2,1)S(1)} %copy-done.66), channel_id=1, source_target_pairs={{0,7},{1,6},{2,5},{3,4},{4,3},{5,2},{6,1},{7,0},{8,15},{9,14},{10,... | collective-permute-start | bytes 1572872 | tf_op jit(solution)/shard_map/ppermute | solution.py:1328
  474.0 170.9 %reduce-scatter.8.cloned.1.call-start = ((), (), s32[]{:S(2)}) async-start(), calls=%async_computation.7 | async-start | bytes 5242880 | tf_op jit(solution)/shard_map/reduce_scatter | solution.py:1396
  510.8 212.6 %reduce-scatter.12.cloned.1.call-start = ((), (), s32[]{:S(2)}) async-start(), calls=%async_computation.9 | async-start | bytes 5242880 | tf_op jit(solution)/shard_map/reduce_scatter | solution.py:1398
  525.3 409.7 %reduce-scatter.10.cloned.1.call-start = ((), (), s32[]{:S(2)}) async-start(), calls=%async_computation.8 | async-start | bytes 9437184 | tf_op jit(solution)/shard_map/reduce_scatter | solution.py:1411
  667.3 54.7 %collective-permute-start.52 = (f32[4,2048]{1,0:T(4,128)S(1)}, f32[4,2048]{1,0:T(4,128)S(1)}, u32[]{:S(2)}, u32[]{:S(2)}) collective-permute-start(f32[4,2048]{1,0:T(4,128)S(1)} %pad_maximum_fusion.5), channel_id=1, source_target_pairs={{0,1},{1,0},{2,3},{3,2},{4,5},{5,4},{6,7},{7,6},{8,9},{9,8},{10,11... | collective-permute-start | bytes 98312 | tf_op jit(solution)/shard_map/ppermute | solution.py:1294
  696.5 413.7 %reduce-scatter.14.cloned.1.call-start = ((), (), s32[]{:S(2)}) async-start(), calls=%async_computation.10 | async-start | bytes 5242880 | tf_op jit(solution)/shard_map/reduce_scatter | solution.py:1452
  743.4 73.1 %collective-permute-start.15 = (bf16[256,2048]{1,0:T(8,128)(2,1)S(1)}, bf16[256,2048]{1,0:T(8,128)(2,1)S(1)}, u32[]{:S(2)}, u32[]{:S(2)}) collective-permute-start(bf16[256,2048]{1,0:T(8,128)(2,1)S(1)} %copy-done.9), channel_id=1, source_target_pairs={{24,16},{16,8},{8,0},{25,17},{17,9},{9,1},{26,18},{18,10},{10,2},{... | collective-permute-start | bytes 3145736 | tf_op jit(solution)/shard_map/ppermute | solution.py:1270
  744.7 76.4 %collective-permute-start.14 = (bf16[256,2048]{1,0:T(8,128)(2,1)S(1)}, bf16[256,2048]{1,0:T(8,128)(2,1)S(1)}, u32[]{:S(2)}, u32[]{:S(2)}) collective-permute-start(bf16[256,2048]{1,0:T(8,128)(2,1)S(1)} %copy-done.9), channel_id=1, source_target_pairs={{0,8},{8,16},{16,24},{1,9},{9,17},{17,25},{2,10},{10,18},{18,26},{... | collective-permute-start | bytes 3145736 | tf_op jit(solution)/shard_map/ppermute | solution.py:1269
  772.3 50.1 %collective-permute-start.47 = (bf16[64,8192]{1,0:T(8,128)(2,1)S(1)}, bf16[64,8192]{1,0:T(8,128)(2,1)S(1)}, u32[]{:S(2)}, u32[]{:S(2)}) collective-permute-start(bf16[64,8192]{1,0:T(8,128)(2,1)S(1)} %bitcast_dynamic-update-slice_fusion.16), channel_id=1, source_target_pairs={{24,16},{16,8},{8,0},{25,17},{17,9},{9,1},{26,18},{18,10},{10,2},{... | collective-permute-start | bytes 3145736 | tf_op jit(solution)/shard_map/ppermute | solution.py:1270
  832.8 54.0 %collective-permute-start.48 = (bf16[64,8192]{1,0:T(8,128)(2,1)S(1)}, bf16[64,8192]{1,0:T(8,128)(2,1)}, u32[]{:S(2)}, u32[]{:S(2)}) collective-permute-start(bf16[64,8192]{1,0:T(8,128)(2,1)S(1)} %collective-permute-done.47), channel_id=1, source_target_pairs={{16,8},{8,0},{17,9},{9,1},{18,10},{10,2},{19,11},{11,3},{20,12},{1... | collective-permute-start | bytes 3145736 | tf_op jit(solution)/shard_map/ppermute | solution.py:1270
  854.0 55.3 %collective-permute-start.35 = (bf16[64,8192]{1,0:T(8,128)(2,1)S(1)}, bf16[64,8192]{1,0:T(8,128)(2,1)}, u32[]{:S(2)}, u32[]{:S(2)}) collective-permute-start(bf16[64,8192]{1,0:T(8,128)(2,1)S(1)} %collective-permute-done.34), channel_id=1, source_target_pairs={{16,8},{8,0},{17,9},{9,1},{18,10},{10,2},{19,11},{11,3},{20,12},{1... | collective-permute-start | bytes 3145736 | tf_op jit(solution)/shard_map/ppermute | solution.py:1270
  866.2 65.5 %collective-permute-start.19 = (bf16[256,2048]{1,0:T(8,128)(2,1)S(1)}, bf16[256,2048]{1,0:T(8,128)(2,1)S(1)}, u32[]{:S(2)}, u32[]{:S(2)}) collective-permute-start(bf16[256,2048]{1,0:T(8,128)(2,1)S(1)} %collective-permute-done.17.refs_7_), channel_id=1, source_target_pairs={{8,0},{9,1},{10,2},{11,3},{12,4},{13,5},{14,6},{15,7}} | collective-permute-start | bytes 3145736 | tf_op jit(solution)/shard_map/ppermute | solution.py:1270
  889.1 142.2 %collective-permute-start.49 = (bf16[64,8192]{1,0:T(8,128)(2,1)}, bf16[64,8192]{1,0:T(8,128)(2,1)}, u32[]{:S(2)}, u32[]{:S(2)}) collective-permute-start(bf16[64,8192]{1,0:T(8,128)(2,1)} %collective-permute-done.48), channel_id=1, source_target_pairs={{8,0},{9,1},{10,2},{11,3},{12,4},{13,5},{14,6},{15,7}} | collective-permute-start | bytes 3145736 | tf_op jit(solution)/shard_map/ppermute | solution.py:1270
  909.3 202.3 %collective-permute-start.51 = (bf16[64,8192]{1,0:T(8,128)(2,1)}, bf16[64,8192]{1,0:T(8,128)(2,1)}, u32[]{:S(2)}, u32[]{:S(2)}) collective-permute-start(bf16[64,8192]{1,0:T(8,128)(2,1)} %collective-permute-done.50), channel_id=1, source_target_pairs={{16,24},{17,25},{18,26},{19,27},{20,28},{21,29},{22,30},{23,31}} | collective-permute-start | bytes 3145736 | tf_op jit(solution)/shard_map/ppermute | solution.py:1269
  911.0 126.0 %collective-permute-start.36 = (bf16[64,8192]{1,0:T(8,128)(2,1)}, bf16[64,8192]{1,0:T(8,128)(2,1)}, u32[]{:S(2)}, u32[]{:S(2)}) collective-permute-start(bf16[64,8192]{1,0:T(8,128)(2,1)} %collective-permute-done.35), channel_id=1, source_target_pairs={{8,0},{9,1},{10,2},{11,3},{12,4},{13,5},{14,6},{15,7}} | collective-permute-start | bytes 3145736 | tf_op jit(solution)/shard_map/ppermute | solution.py:1270
  931.7 206.9 %collective-permute-start.38 = (bf16[64,8192]{1,0:T(8,128)(2,1)}, bf16[64,8192]{1,0:T(8,128)(2,1)}, u32[]{:S(2)}, u32[]{:S(2)}) collective-permute-start(bf16[64,8192]{1,0:T(8,128)(2,1)} %collective-permute-done.37), channel_id=1, source_target_pairs={{16,24},{17,25},{18,26},{19,27},{20,28},{21,29},{22,30},{23,31}} | collective-permute-start | bytes 3145736 | tf_op jit(solution)/shard_map/ppermute | solution.py:1269
  (128 other events, 3034.3 us)
Sparse Core Ops, SparseCore 0:
  81.6 100.1 all-gather.1
  474.1 76.7 reduce-scatter.5
  553.9 88.7 reduce-scatter.7
  644.8 75.2 reduce-scatter.11
  723.8 79.0 reduce-scatter.9
  1026.9 83.2 reduce-scatter.13

commit v2 on v1

--- a/solution.py
+++ b/solution.py
@@ -329,7 +329,10 @@
 
 
 MESH = pl.DeviceIdType.MESH
-VMEM_LIMIT = 48 * 1024 * 1024
+ANY = pl.BlockSpec(memory_space=pl.ANY)
+VM = pl.BlockSpec(memory_space=pltpu.VMEM)
+DMA = pltpu.SemaphoreType.DMA
+VMEM_LIMIT = 56 * 1024 * 1024
 
 
 def flip(value, bit):
@@ -388,6 +391,7 @@
         compiler_params=pltpu.CompilerParams(
             collective_id=number, has_side_effects=True, vmem_limit_bytes=VMEM_LIMIT
         ),
+        cost_estimate=pl.CostEstimate(flops=1, bytes_accessed=1, transcendentals=0),
     )(*inputs, *after)
 
 
@@ -395,23 +399,29 @@
     out[...] = x[...]
 
 
-def keep_number(x, out):
-    out[0] = x[0]
-
-
-def keep(x, after, space=pltpu.VMEM):
+def hold_kernel(x, out):
+    pass
+
+
+def hold(x, after):
     return pl.pallas_call(
-        ordered(keep_number if space == pltpu.SMEM else keep_kernel, (x,), after),
+        ordered(hold_kernel, (x,), after),
         out_shape=jax.ShapeDtypeStruct(x.shape, x.dtype),
-        in_specs=[pl.BlockSpec(memory_space=space)] + [ANY] * len(after),
-        out_specs=pl.BlockSpec(memory_space=space),
+        in_specs=[ANY] * (1 + len(after)),
+        out_specs=ANY,
+        input_output_aliases={0: 0},
+        name="hold",
+    )(x, *after)
+
+
+def keep(x, after):
+    return pl.pallas_call(
+        ordered(keep_kernel, (x,), after),
+        out_shape=jax.ShapeDtypeStruct(x.shape, x.dtype),
+        in_specs=[VM] + [ANY] * len(after),
+        out_specs=VM,
         name="keep",
     )(x, *after)
-
-
-ANY = pl.BlockSpec(memory_space=pl.ANY)
-VM = pl.BlockSpec(memory_space=pltpu.VMEM)
-DMA = pltpu.SemaphoreType.DMA
 
 
 def entry_kernel(
@@ -591,13 +601,60 @@
     )
 
 
-def to_tokens_kernel(heads, tokens, local, send, receive):
+def plane_others(seq, shard):
+    return [(seq, flip_mask(shard, mask)) for mask in range(1, 8)]
+
+
+class ColumnExchange:
+    def __init__(self, weight, cols, local, send, receive):
+        self.parts = (weight, cols, local, send, receive)
+        self.seq, self.shard = place()
+        self.width = cols.shape[2]
+
+    def block(self, target):
+        weight = self.parts[0]
+        return weight.at[:, pl.ds(pl.multiple_of(target * self.width, self.width), self.width)]
+
+    def copies(self):
+        _, cols, local, send, receive = self.parts
+        spot = cols.at[self.shard]
+        for mask in (2, 4, 3, 5, 6, 7, 1):
+            target = flip_mask(self.shard, mask)
+            yield remote(
+                self.block(target), spot, send.at[mask], receive.at[mask], (self.seq, target)
+            )
+
+    def start(self):
+        _, cols, local, _, _ = self.parts
+        self.started = list(self.copies())
+        for copy in self.started:
+            copy.start()
+        self.own = pltpu.make_async_copy(self.block(self.shard), cols.at[self.shard], local)
+        self.own.start()
+
+    def wait(self):
+        self.own.wait()
+        for copy in self.started:
+            copy.wait()
+
+
+EXCHANGE = [DMA, DMA((8,)), DMA((8,))]
+
+
+def columns_shape(weight):
+    rows, width = weight.shape
+    return jax.ShapeDtypeStruct((8, rows, width // 8), weight.dtype)
+
+
+def to_tokens_kernel(
+    heads, weight, tokens, cols, local, send, receive, cols_local, cols_send, cols_receive
+):
     seq, shard = place()
     core, half = lax.rem(shard, 2), lax.div(seq, 2)
     base = shard - core
     width = heads.shape[2]
     group = 2 * lax.rem(seq, 2) + core
-    greet(column_others(seq, shard))
+    greet(column_others(seq, shard) + plane_others(seq, shard)[1:])
     mine = tokens.at[:, pl.ds(pl.multiple_of(group * width, width), width)]
     steps = []
     for turn in range(4):
@@ -620,6 +677,8 @@
         else:
             remote_copy.start()
         steps.append(remote_copy)
+    exchange = ColumnExchange(weight, cols, cols_local, cols_send, cols_receive)
+    exchange.start()
     for turn in range(4):
         if turn == 0:
 
@@ -641,16 +700,18 @@
         def _():
             arrival.wait_recv()
 
-
-def to_tokens(heads, number, after=()):
+    exchange.wait()
+
+
+def to_tokens(heads, weight, number, after=()):
     blocks, rows, width = heads.shape
     return comm_call(
         to_tokens_kernel,
-        jax.ShapeDtypeStruct((rows, 4 * width), heads.dtype),
-        (heads,),
-        [ANY],
-        ANY,
-        [DMA, DMA((4,)), DMA((4,))],
+        (jax.ShapeDtypeStruct((rows, 4 * width), heads.dtype), columns_shape(weight)),
+        (heads, weight),
+        [ANY] * 2,
+        (ANY, ANY),
+        [DMA, DMA((4,)), DMA((4,))] + EXCHANGE,
         "to_tokens",
         number,
         after,
@@ -717,11 +778,11 @@
     )
 
 
-def plane_gather_kernel(x, out, local, send, receive):
+def gather_plane(x, out, local, send, receive, ready, exchange=None):
     seq, shard = place()
     core = lax.rem(shard, 2)
     near = [(seq, flip(shard, bit)) for bit in (2, 4, 1)]
-    greet(near)
+    greet(plane_others(seq, shard) if exchange else near)
     own = pltpu.make_async_copy(x, out.at[shard], local)
     own.start()
     firsts = [
@@ -730,7 +791,10 @@
     ]
     for copy in firsts:
         copy.start()
+    if exchange:
+        exchange.start()
     mate = near[2]
+    mate_shard = flip(shard, 1)
 
     def pass_on(slot, index, device):
         return remote(out.at[slot], out.at[slot], send.at[index], receive.at[index], device)
@@ -743,6 +807,10 @@
     def arrival(slot, index):
         return remote(out.at[slot], out.at[slot], send.at[0], receive.at[index], mate)
 
+    own.wait()
+    ready(shard)
+    arrival(mate_shard, 2).wait_recv()
+    ready(mate_shard)
     arrival(first, core).wait_recv()
     across = pass_on(first, 3, (seq, second))
     across.start()
@@ -751,37 +819,172 @@
     arrival(second, 1 - core).wait_recv()
     two = remote(out.at[second], out.at[second], send.at[5], receive.at[5 - core], mate)
     two.start()
+    ready(first)
+    ready(second)
+    arrival(flip(mate_shard, 2), 4).wait_recv()
+    ready(flip(mate_shard, 2))
     arrival(diagonal, 3).wait_recv()
     three = pass_on(diagonal, 6, mate)
     three.start()
-    own.wait()
-    for copy in firsts:
+    arrival(flip(mate_shard, 4), 5).wait_recv()
+    ready(flip(mate_shard, 4))
+    ready(diagonal)
+    arrival(flip_mask(mate_shard, 6), 6).wait_recv()
+    ready(flip_mask(mate_shard, 6))
+    for copy in firsts + [across, one, two, three]:
         copy.wait_send()
-    for copy in (across, one, two, three):
-        copy.wait_send()
-    mate_shard = flip(shard, 1)
-    arrival(mate_shard, 2).wait_recv()
-    arrival(flip(mate_shard, 2), 4).wait_recv()
-    arrival(flip(mate_shard, 4), 5).wait_recv()
-    arrival(flip_mask(mate_shard, 6), 6).wait_recv()
+
+
+class Stores:
+    def __init__(self, pairs, sems):
+        self.pairs, self.sems = pairs, sems
+
+    def copies(self, slot):
+        return [
+            pltpu.make_async_copy(source.at[slot], target.at[slot], self.sems.at[index, slot])
+            for index, (source, target) in enumerate(self.pairs)
+        ]
+
+    def start(self, slot):
+        for copy in self.copies(slot):
+            copy.start()
+
+    def wait(self):
+        def one(slot, carry):
+            for copy in self.copies(slot):
+                copy.wait()
+            return carry
+
+        lax.fori_loop(0, 8, one, 0)
+
+
+TILE = 512
+
+
+def tiles(width, body):
+    def one(index, carry):
+        body(pl.ds(pl.multiple_of(index * TILE, TILE), TILE))
+        return carry
+
+    lax.fori_loop(0, width // TILE, one, 0)
+
+
+def hidden_kernel(
+    x, weight, gate_cols, plane, up_cols, gate, upward, hidden,
+    plane_in, up_in, gate_wide, gate_low, up_low, hidden_low, local, send, receive, store,
+    up_store, cols_local, cols_send, cols_receive
+):
+    exchange = ColumnExchange(weight, up_in, cols_local, cols_send, cols_receive)
+    width = gate_wide.shape[2]
+    early = Stores([(plane_in, plane), (gate_low, gate)], store.at[0])
+    late = Stores([(up_low, upward), (hidden_low, hidden)], store.at[1])
+
+    def ready(slot):
+        def tile(at):
+            value = dot_nn(plane_in[slot], gate_cols[:, at])
+            gate_wide[slot, :, at] = value
+            gate_low[slot, :, at] = value.astype(jnp.bfloat16)
+
+        tiles(width, tile)
+        early.start(slot)
+
+    gather_plane(x, plane_in, local, send, receive, ready, exchange)
+    exchange.wait()
+    kept = pltpu.make_async_copy(up_in, up_cols, up_store)
+    kept.start()
+
+    def last(slot, carry):
+        def tile(at):
+            value = dot_nn(plane_in[slot], up_in[:, :, at].reshape(-1, TILE))
+            gated = gate_wide[slot, :, at]
+            up_low[slot, :, at] = value.astype(jnp.bfloat16)
+            hidden_low[slot, :, at] = (
+                gated * (1.0 / (1.0 + jnp.exp(-gated))) * value
+            ).astype(jnp.bfloat16)
+
+        tiles(width, tile)
+        late.start(slot)
+        return carry
+
+    lax.fori_loop(0, 8, last, 0)
+    early.wait()
+    late.wait()
+    kept.wait()
+
+
+def gather_hidden(x, gate_cols, weight, number, after=()):
+    rows, wide = x.shape
+    width = weight.shape[1] // 8
+    low = x.dtype
+    narrow = (8, rows, width)
+    result = jax.ShapeDtypeStruct(narrow, low)
+    return comm_call(
+        hidden_kernel,
+        (jax.ShapeDtypeStruct((8, rows, wide), low), columns_shape(weight)) + (result,) * 3,
+        (x, weight, gate_cols),
+        [VM, ANY, VM],
+        (ANY,) * 5,
+        [
+            pltpu.VMEM((8, rows, wide), low),
+            pltpu.VMEM(columns_shape(weight).shape, low),
+            pltpu.VMEM(narrow, jnp.float32),
+        ]
+        + [pltpu.VMEM(narrow, low)] * 3
+        + [DMA, DMA((7,)), DMA((7,)), DMA((2, 2, 8)), DMA]
+        + EXCHANGE,
+        "gather_hidden",
+        number,
+        after,
+    )
+
+
+def hidden_grad_kernel(
+    x, down, gate, upward, plane, gate_grad, up_grad,
+    plane_in, gate_low, up_low, local, send, receive, store
+):
+    width = gate.shape[2]
+    stores = Stores([(plane_in, plane), (gate_low, gate_grad), (up_low, up_grad)], store)
+
+    def ready(slot):
+        def tile(at):
+            grad = dot_nt(plane_in[slot], down[at])
+            gated = gate[slot, :, at].astype(jnp.float32)
+            sigmoid = 1.0 / (1.0 + jnp.exp(-gated))
+            part = grad * sigmoid
+            gate_low[slot, :, at] = (
+                part * upward[slot, :, at].astype(jnp.float32) * (1.0 + gated * (1.0 - sigmoid))
+            ).astype(jnp.bfloat16)
+            up_low[slot, :, at] = (part * gated).astype(jnp.bfloat16)
+
+        tiles(width, tile)
+        stores.start(slot)
+
+    gather_plane(x, plane_in, local, send, receive, ready)
+    stores.wait()
+
+
+def gather_hidden_grad(x, down, gate, upward, number, after=()):
+    rows, wide = x.shape
+    low = x.dtype
+    narrow = gate.shape
+    result = jax.ShapeDtypeStruct(narrow, low)
+    return comm_call(
+        hidden_grad_kernel,
+        (jax.ShapeDtypeStruct((8, rows, wide), low), result, result),
+        (x, down, gate, upward),
+        [VM] * 4,
+        (ANY,) * 3,
+        [pltpu.VMEM((8, rows, wide), low)]
+        + [pltpu.VMEM(narrow, low)] * 2
+        + [DMA, DMA((7,)), DMA((7,)), DMA((3, 8))],
+        "gather_hidden_grad",
+        number,
+        after,
+    )
 
 
 def flip_bit(value, bit):
     return value + bit - 2 * bit * lax.rem(lax.div(value, bit), 2)
-
-
-def plane_gather(x, number, after=()):
-    return comm_call(
-        plane_gather_kernel,
-        jax.ShapeDtypeStruct((8,) + x.shape, x.dtype),
-        (x,),
-        [ANY],
-        ANY,
-        [DMA, DMA((7,)), DMA((7,))],
-        "plane_gather",
-        number,
-        after,
-    )
 
 
 PIECES = 2
@@ -797,7 +1000,7 @@
     lax.fori_loop(0, rows // step, one, 0)
 
 
-def plane_scatter_kernel(part, out, mated, first_in, second_in, sums, sem_s, sem_r):
+def scatter_products(produce, part, out, mated, first_in, second_in, sums, sem_s, sem_r):
     seq, shard = place()
     core, chip = lax.rem(shard, 2), lax.div(shard, 2)
     rows = out.shape[0] // PIECES
@@ -811,9 +1014,12 @@
     def piece(index):
         return pl.ds(index * rows, rows)
 
-    order = (diagonal, first, second, chip)
+    order, mate_order = (diagonal, first, second, chip), (diagonal, second, first, chip)
     swaps = {}
-    for slot, target in enumerate(order):
+
+    def make(slot):
+        target = mate_order[slot]
+        produce(2 * target + 1 - core)
         for index in range(PIECES):
             copy = remote(
                 part.at[2 * target + 1 - core, piece(index)],
@@ -824,6 +1030,10 @@
             )
             copy.start()
             swaps[slot, index] = copy
+        produce(2 * order[slot] + core)
+
+    make(0)
+    make(1)
 
     def came(target, index):
         remote(
@@ -856,6 +1066,8 @@
             )
             copy.start()
             sends.append(copy)
+    make(2)
+    make(3)
     finals = []
     for index in range(PIECES):
         came(second, index)
@@ -895,16 +1107,38 @@
         copy.wait_send()
 
 
-def plane_scatter(part, number, after=()):
-    _, rows, width = part.shape
-    low = part.dtype
+def out_scatter_kernel(hidden, down, out, part, *scratch):
+    def produce(block):
+        def tile(at):
+            part[block, :, at] = dot_nn(hidden[block], down[:, at]).astype(jnp.bfloat16)
+
+        tiles(down.shape[1], tile)
+
+    scatter_products(produce, part, out, *scratch)
+
+
+def back_scatter_kernel(gate_grad, up_grad, gate_cols, up_cols, out, part, *scratch):
+    def produce(block):
+        def tile(at):
+            part[block, :, at] = (
+                dot_nt(gate_grad[block], gate_cols[at]) + dot_nt(up_grad[block], up_cols[at])
+            ).astype(jnp.bfloat16)
+
+        tiles(gate_cols.shape[0], tile)
+
+    scatter_products(produce, part, out, *scratch)
+
+
+def plane_scatter(kernel, inputs, rows, width, name, number, after=()):
+    low = jnp.bfloat16
     return comm_call(
-        plane_scatter_kernel,
+        kernel,
         jax.ShapeDtypeStruct((rows, width), jnp.float32),
-        (part,),
-        [VM],
+        inputs,
+        [VM] * len(inputs),
         VM,
         [
+            pltpu.VMEM((8, rows, width), low),
             pltpu.VMEM((4, rows, width), low),
             pltpu.VMEM((2, rows, width), low),
             pltpu.VMEM((rows, width), low),
@@ -912,14 +1146,14 @@
             DMA((3, 4, PIECES)),
             DMA((3, 4, PIECES)),
         ],
-        "plane_scatter",
+        name,
         number,
         after,
     )
 
 
 def finish_kernel(
-    part, grads, out_grad, out, placed,
+    part, grads, out, placed,
     mated, sums, landed, first_in, second_in, onward, total, swapped,
     local, sem_s, sem_r, grad_s, grad_r
 ):
@@ -959,8 +1193,6 @@
             copy.start()
             firsts.append(copy)
     placed[...] = jnp.zeros_like(placed)
-    width = out_grad.shape[1]
-    placed[:, 3 * width :] = out_grad[...]
 
     sends = []
     for slot, block in enumerate(order):
@@ -1033,19 +1265,17 @@
             )
             swap.start()
     group = 2 * quarter + core
-    part_width = width // 4
+    part_width = out.shape[1] // 4
     own_rows = pl.ds(pl.multiple_of(core * long, long), long)
     for index in range(3):
-        spot = pl.multiple_of(index * width + group * part_width, part_width)
-        placed[:, pl.ds(spot, part_width)] = total[
+        spot = pl.multiple_of(group * part_width, part_width)
+        placed[index, :, pl.ds(spot, part_width)] = total[
             own_rows, index * part_width : (index + 1) * part_width
         ]
     swap.wait_recv()
     for index in range(3):
-        spot = pl.multiple_of(
-            index * width + (2 * quarter + 1 - core) * part_width, part_width
-        )
-        placed[:, pl.ds(spot, part_width)] = swapped[
+        spot = pl.multiple_of((2 * quarter + 1 - core) * part_width, part_width)
+        placed[index, :, pl.ds(spot, part_width)] = swapped[
             :, index * part_width : (index + 1) * part_width
         ]
 
@@ -1086,7 +1316,7 @@
         copy.wait_send()
 
 
-def finish(part, grads, out_grad, number, after=()):
+def finish(part, grads, number, after=()):
     _, rows, width = part.shape
     _, long, joined = grads.shape
     low = part.dtype
@@ -1094,10 +1324,10 @@
         finish_kernel,
         (
             jax.ShapeDtypeStruct((rows, width), jnp.float32),
-            jax.ShapeDtypeStruct((long // 2, 4 * width), low),
+            jax.ShapeDtypeStruct((3, long // 2, width), low),
         ),
-        (part, grads, out_grad),
-        [VM] * 3,
+        (part, grads),
+        [VM] * 2,
         (VM, VM),
         [
             pltpu.VMEM((4, rows // 2, width), low),
@@ -1256,29 +1486,266 @@
     )(*inputs, *after)
 
 
-class LineGather:
-    def __init__(self, block):
-        self.seq = lax.axis_index("seq")
-        self.block = block
-        self.up, self.down = [block], [block]
-
-    def step(self):
-        done = len(self.up)
-        up = [(i, i + 1) for i in range(done - 1, 3)]
-        down = [(3 - i, 3 - j) for i, j in up]
-        self.up.append(lax.ppermute(self.up[-1], "seq", up))
-        self.down.append(lax.ppermute(self.down[-1], "seq", down))
-        return (self.up[-1], self.down[-1])
-
-    def blocks(self):
-        while len(self.up) < 4:
-            self.step()
-        seq = self.seq
-        found = [(seq, self.block)]
-        for back in (1, 2, 3):
-            came = jnp.where(seq >= back, self.up[back], self.down[4 - back])
-            found.append((lax.rem(seq + 4 - back, 4), came))
-        return found
+LINE_ROWS = 128
+
+
+def flip_by(value, mask):
+    for bit in (1, 2, 4):
+        here, there = lax.rem(lax.div(value, bit), 2), lax.rem(lax.div(mask, bit), 2)
+        value = value + bit * (lax.rem(here + there, 2) - here)
+    return value
+
+
+def line_kernel(
+    gate, up, out_part, rest, gate_rows, up_rows, out,
+    first, second, held, total, load_sem, send, receive, spread_send, spread_receive
+):
+    seq, shard = place()
+    inner = jnp.logical_or(seq == 1, seq == 2)
+    outer = jnp.logical_not(inner)
+    beside = (seq + 1 - 2 * lax.rem(seq, 2), shard)
+    across = (3 - seq, shard)
+    greet([beside, across] + plane_others(seq, shard))
+    rows, width = gate_rows.shape[0], gate.shape[1]
+    cuts = rows // LINE_ROWS
+    early = 8 * cuts
+    late = [
+        part.at[start : start + LINE_ROWS]
+        for part in (out_part, rest)
+        for start in range(0, part.shape[0], LINE_ROWS)
+    ]
+    count = early + len(late)
+
+    def owner(index):
+        return flip_by(shard, 7 - lax.div(index, cuts))
+
+    def sources(index):
+        start = owner(index) * rows + lax.rem(index, cuts) * LINE_ROWS
+        span = pl.ds(pl.multiple_of(start, LINE_ROWS), LINE_ROWS)
+        return gate.at[span], up.at[span]
+
+    halves = (slice(0, width), slice(width, 2 * width))
+
+    def inward(index, side, source):
+        return remote(
+            source,
+            first.at[index, :, halves[side]],
+            send.at[side, index],
+            receive.at[side, index],
+            beside,
+        )
+
+    def inward_late(index, source):
+        return remote(source, first.at[index], send.at[0, index], receive.at[0, index], beside)
+
+    def swap(index):
+        return remote(
+            first.at[index], second.at[index], send.at[2, index], receive.at[2, index], across
+        )
+
+    def outward(index):
+        return remote(
+            total.at[index], total.at[index], send.at[3, index], receive.at[3, index], beside
+        )
+
+    def outward_late(index, place_in_out):
+        here = out.at[place_in_out * LINE_ROWS : (place_in_out + 1) * LINE_ROWS]
+        return remote(here, here, send.at[3, index], receive.at[3, index], beside)
+
+    def spread(index, side, away=True):
+        target = (gate_rows, up_rows)[side]
+        down = pl.ds(pl.multiple_of(lax.rem(index, cuts) * LINE_ROWS, LINE_ROWS), LINE_ROWS)
+        along = pl.ds(pl.multiple_of(shard * width, width), width)
+        source, spot = total.at[index, :, halves[side]], target.at[down, along]
+        if not away:
+            return pltpu.make_async_copy(source, spot, spread_send.at[side, index])
+        return remote(
+            source,
+            spot,
+            spread_send.at[side, index],
+            spread_receive.at[side, index],
+            (seq, owner(index)),
+        )
+
+    away = 7 * cuts
+
+    def each(start, stop, body):
+        def one(index, carry):
+            body(index)
+            return carry
+
+        lax.fori_loop(start, stop, one, 0)
+
+    def spread_start(index):
+        for side in range(2):
+
+            @pl.when(index < away)
+            def _():
+                spread(index, side).start()
+
+            @pl.when(index >= away)
+            def _():
+                spread(index, side, False).start()
+
+    @pl.when(outer)
+    def _():
+        def start(index):
+            for side, source in enumerate(sources(index)):
+                inward(index, side, source).start()
+
+        each(0, early, start)
+        for spot, part in enumerate(late):
+            inward_late(early + spot, part).start()
+
+        def finish_one(index):
+            outward(index).wait_recv()
+            spread_start(index)
+
+        each(0, early, finish_one)
+        for spot in range(len(late)):
+            outward_late(early + spot, spot).wait_recv()
+
+        def sent(index):
+            for side, source in enumerate(sources(index)):
+                inward(index, side, source).wait_send()
+
+        each(0, early, sent)
+        for spot, part in enumerate(late):
+            inward_late(early + spot, part).wait_send()
+
+    @pl.when(inner)
+    def _():
+        def loads(index):
+            slot = lax.rem(index, 2)
+            for side, source in enumerate(sources(index)):
+                yield pltpu.make_async_copy(
+                    source, held.at[slot, :, halves[side]], load_sem.at[slot, side]
+                )
+
+        def load(index):
+            for copy in loads(index):
+                copy.start()
+
+        def add_in(index, own):
+            def add(at):
+                first[index, at] = (
+                    first[index, at].astype(jnp.float32) + own(at).astype(jnp.float32)
+                ).astype(jnp.bfloat16)
+
+            add_rows(LINE_ROWS, add)
+            swap(index).start()
+
+        def add_up(index, store):
+            swap(index).wait_recv()
+
+            def add(at):
+                store(
+                    at,
+                    (
+                        first[index, at].astype(jnp.float32)
+                        + second[index, at].astype(jnp.float32)
+                    ).astype(jnp.bfloat16),
+                )
+
+            add_rows(LINE_ROWS, add)
+
+        def total_store(index):
+            def store(at, value):
+                total[index, at] = value
+
+            return store
+
+        def close(index):
+            add_up(index, total_store(index))
+            outward(index).start()
+            spread_start(index)
+
+        def step(index):
+            @pl.when(index + 1 < early)
+            def _():
+                load(index + 1)
+
+            for copy in loads(index):
+                copy.wait()
+            for side, source in enumerate(sources(index)):
+                inward(index, side, source).wait_recv()
+            slot = lax.rem(index, 2)
+            add_in(index, lambda at: held[slot, at])
+
+            @pl.when(index > 0)
+            def _():
+                close(index - 1)
+
+        load(0)
+        each(0, early, step)
+
+        def close_late(spot):
+            def store(at, value):
+                out[pl.ds(at.start + spot * LINE_ROWS, at.size)] = value
+
+            add_up(early + spot, store)
+            outward_late(early + spot, spot).start()
+
+        for spot, part in enumerate(late):
+            inward_late(early + spot, part).wait_recv()
+            add_in(early + spot, lambda at, part=part: part[at])
+            if spot:
+                close_late(spot - 1)
+            else:
+                close(early - 1)
+        close_late(len(late) - 1)
+
+        def sent(index):
+            swap(index).wait_send()
+            outward(index).wait_send()
+
+        each(0, early, sent)
+        for spot in range(len(late)):
+            swap(early + spot).wait_send()
+            outward_late(early + spot, spot).wait_send()
+
+    def spread_wait(index):
+        for side in range(2):
+
+            @pl.when(index < away)
+            def _():
+                spread(index, side).wait()
+
+            @pl.when(index >= away)
+            def _():
+                spread(index, side, False).wait()
+
+    each(0, early, spread_wait)
+
+
+def line_sums(gate, up, out_part, rest, number, after=()):
+    rows, width = gate.shape[0] // 8, gate.shape[1]
+    low = gate.dtype
+    tail = (out_part.shape[0] + rest.shape[0], rest.shape[1])
+    early, late = gate.shape[0] // LINE_ROWS, tail[0] // LINE_ROWS
+    block = (LINE_ROWS, 2 * width)
+    owned = jax.ShapeDtypeStruct((rows, 8 * width), low)
+    return comm_call(
+        line_kernel,
+        (owned, owned, jax.ShapeDtypeStruct(tail, low)),
+        (gate, up, out_part, rest),
+        [ANY, ANY, VM, VM],
+        (ANY, ANY, VM),
+        [
+            pltpu.VMEM((early + late,) + block, low),
+            pltpu.VMEM((early + late,) + block, low),
+            pltpu.VMEM((2,) + block, low),
+            pltpu.VMEM((early,) + block, low),
+            DMA((2, 2)),
+            DMA((4, early + late)),
+            DMA((4, early + late)),
+            DMA((2, early)),
+            DMA((2, early)),
+        ],
+        "line_sums",
+        number,
+        after,
+    )
 
 
 def line_total(part):
@@ -1317,27 +1784,6 @@
     out_full = lax.all_gather(
         keep(out_weight, (qkv,)), "fsdp", axis=0, tiled=True
     )
-    shard_later = keep(shard.reshape(1), (qkv,), pltpu.SMEM)[0]
-
-    def columns_of(weight):
-        pieces = {}
-        for mask in (1, 2, 4, 3, 5, 6, 7, 0):
-            partner = flip_mask(shard_later, mask)
-            piece = lax.dynamic_slice_in_dim(weight, partner * hidden_width, hidden_width, 1)
-            if mask:
-                piece = lax.ppermute(piece, "fsdp", [(i, i ^ mask) for i in range(8)])
-            pieces[mask] = piece
-        return pieces
-
-    def joined_columns(pieces):
-        cols = jnp.zeros((8, rows, hidden_width), low)
-        for mask, piece in pieces.items():
-            cols = lax.dynamic_update_index_in_dim(cols, piece, flip_mask(shard, mask), 0)
-        return cols.reshape(width, hidden_width)
-
-    gate_pieces, up_pieces = columns_of(gate_weight), columns_of(up_weight)
-    gate_cols, up_cols = joined_columns(gate_pieces), joined_columns(up_pieces)
-
     raw = dot_nn(whole, qkv)
     q_raw, k_raw = raw[:, :group_width], raw[:, group_width : 2 * group_width]
 
@@ -1356,51 +1802,47 @@
     q_gain_part = lax.dynamic_slice_in_dim(query_gain, group * group_width, group_width)[None]
     k_gain_part = lax.dynamic_slice_in_dim(key_gain, group * group_width, group_width)[None]
     queries, keys, values, attended_heads, log_total = attend(
-        raw, q_factor, k_factor, q_gain_part, k_gain_part, cosine, signed, head_size,
-        tuple(gate_pieces[mask] for mask in (1, 2, 4, 3)),
-    )
-    attended = to_tokens(
-        attended_heads.reshape(4, tokens, group_width),
-        3,
-        tuple(gate_pieces[mask] for mask in (5, 6, 7)) + (up_pieces[1], up_pieces[2]),
-    )
+        raw, q_factor, k_factor, q_gain_part, k_gain_part, cosine, signed, head_size
+    )
+    attended, gate_cols = to_tokens(
+        attended_heads.reshape(4, tokens, group_width), gate_weight, 3
+    )
+    gate_cols = gate_cols.reshape(width, hidden_width)
     branch = dot_nn(attended, out_full)
     branch_factor = norm_factor(branch)
     residual = sequence.astype(jnp.float32) + branch * branch_factor * attention_gain
 
-    plane = plane_gather(
-        residual.astype(low), 4, tuple(up_pieces[mask] for mask in (4, 3, 5, 6, 7))
-    ).reshape(8 * tokens, width)
-    gate_value = dot_nn(plane, gate_cols)
-    upward = dot_nn(plane, up_cols)
-    sigmoid_gate = jax.nn.sigmoid(gate_value)
-    hidden = (gate_value * sigmoid_gate * upward).astype(low)
-    mixed_part = dot_nn(hidden, down_weight).astype(low)
-    mixed_out = plane_scatter(mixed_part.reshape(8, tokens, width), 5)
+    plane, up_cols, gate, upward, hidden = gather_hidden(
+        residual.astype(low), gate_cols, up_weight, 4
+    )
+    plane, up_cols = plane.reshape(8 * tokens, width), up_cols.reshape(width, hidden_width)
+    mixed_out = plane_scatter(
+        out_scatter_kernel, (hidden, down_weight), tokens, width, "out_scatter", 5
+    )
     mixed_factor = norm_factor(mixed_out)
     output = residual + mixed_out * mixed_factor * swiglu_gain
     upstream = cotangent.reshape(tokens, width).astype(jnp.float32)
     mixed_float, swiglu_gain_grad = norm_backward(mixed_out, mixed_factor, swiglu_gain, upstream)
-    mixed_plane = plane_gather(mixed_float.astype(low), 6).reshape(8 * tokens, width)
-    down_grad = transposed_times(hidden, mixed_plane).astype(low)
-    down_block = lax.psum_scatter(down_grad, "seq", scatter_dimension=0, tiled=True)
-    hidden_grad = times_transposed(mixed_plane, down_weight)
-    gate_grad = (
-        hidden_grad * upward * sigmoid_gate * (1.0 + gate_value * (1.0 - sigmoid_gate))
+    mixed_plane, gate_grad, up_grad = gather_hidden_grad(
+        mixed_float.astype(low), down_weight, gate, upward, 6
+    )
+    mixed_plane = mixed_plane.reshape(8 * tokens, width)
+    down_grad = transposed_times(
+        hidden.reshape(8 * tokens, hidden_width), mixed_plane
     ).astype(low)
-    up_grad = (hidden_grad * (gate_value * sigmoid_gate)).astype(low)
-    residual_part = (
-        times_transposed(gate_grad, gate_cols) + times_transposed(up_grad, up_cols)
-    ).astype(low)
-    gate_sum = transposed_times(plane, gate_grad).astype(low).reshape(8, rows, hidden_width)
-    gate_block = lax.psum_scatter(gate_sum, "seq", scatter_dimension=1, tiled=True)
-    up_sum = transposed_times(plane, up_grad).astype(low).reshape(8, rows, hidden_width)
-    up_block = lax.psum_scatter(up_sum, "seq", scatter_dimension=1, tiled=True)
+    down_sum = lax.psum(down_grad, "seq")
+    gate_sum = transposed_times(plane, gate_grad.reshape(8 * tokens, hidden_width)).astype(low)
+    up_sum = transposed_times(plane, up_grad.reshape(8 * tokens, hidden_width)).astype(low)
+
     residual_grad = upstream + plane_scatter(
-        residual_part.reshape(8, tokens, width), 7, (down_block, gate_sum, up_sum)
-    )
-
-    down_line = LineGather(down_block)
+        back_scatter_kernel,
+        (gate_grad, up_grad, gate_cols, up_cols),
+        tokens,
+        width,
+        "back_scatter",
+        7,
+        (gate_sum, up_sum),
+    )
 
     branch_float, attention_gain_grad = norm_backward(
         branch, branch_factor, attention_gain, residual_grad
@@ -1412,8 +1854,7 @@
         transposed_times(attended, branch_grad).astype(low), "fsdp", scatter_dimension=0, tiled=True
     )
     q_norm_grad, k_norm_grad, value_grad = attend_back(
-        queries, keys, values, head_grad, log_total, cosine, signed, head_size,
-        (gate_block,),
+        queries, keys, values, head_grad, log_total, cosine, signed, head_size, (down_sum,)
     )
     q_scaled, k_scaled = q_norm_grad * q_gain_part, k_norm_grad * k_gain_part
     q_inner, k_inner = reduced(
@@ -1429,43 +1870,17 @@
     input_sum, attention_part = finish(
         input_part.reshape(4, tokens, width),
         qkv_grad.reshape(4, 2 * rows, 3 * group_width),
-        out_grad,
         10,
-        (up_block,) + down_line.step() + down_line.step() + down_line.step(),
     )
     input_grad = residual_grad + input_sum
 
-    share = rows // 4
-
-    def owned(block):
-        full = jnp.zeros((share, 8 * hidden_width), low)
-        for mask in (1, 2, 4, 3, 5, 6, 7, 0):
-            partner = flip_mask(shard, mask)
-            piece = lax.dynamic_index_in_dim(block, partner, 0, keepdims=False)
-            if mask:
-                piece = lax.ppermute(piece, "fsdp", [(i, i ^ mask) for i in range(8)])
-            full = lax.dynamic_update_slice(full, piece, (0, partner * hidden_width))
-        return full
-
-    gate_line, up_line = LineGather(owned(gate_block)), LineGather(owned(up_block))
-    attention_line = LineGather(
-        lax.psum_scatter(attention_part, "seq", scatter_dimension=0, tiled=True)
-    )
-
-    def whole_line(line):
-        blocks = line.blocks()
-        count, columns = line.block.shape
-        total = jnp.zeros((4 * count, columns), jnp.float32)
-        for slot, block in blocks:
-            total = lax.dynamic_update_slice(
-                total, block.astype(jnp.float32), (slot * count, 0)
-            )
-        return total
-
-    down_total, gate_total, up_total = map(whole_line, (down_line, gate_line, up_line))
-    attention_total = whole_line(attention_line)
-    query_total, key_total, value_total, out_total = (
-        attention_total[:, index * width : (index + 1) * width] for index in range(4)
+    gate_rows, up_rows, late = line_sums(
+        gate_sum, up_sum, out_grad, attention_part.reshape(3 * rows, width), 11
+    )
+    down_total = down_sum.astype(jnp.float32)
+    gate_total, up_total = gate_rows.astype(jnp.float32), up_rows.astype(jnp.float32)
+    out_total, query_total, key_total, value_total = (
+        late[index * rows : (index + 1) * rows].astype(jnp.float32) for index in range(4)
     )
 
     def widen(part):

time: 1210 us -> 1070 us (0.88)
  Pallas kernels: 485 us -> 845 us
  waiting for transfers between devices: 323 us -> 43 us
  matrix products: 180 us -> 89.1 us
  starting transfers between devices: 81.7 us -> 7.55 us
  local copies, waits for them, and re-layouts: 66.2 us -> 12 us
    pallas_call x10 -> x11, Pallas kernels: 450 us -> 809 us  [comm_call(): pl.pallas_call(ordered(kernel, inputs, after), out_shape=out_shape, in_sp...]
    ppermute x52 -> x0, waiting for transfers between devices: 228 us -> none  [the longest x12 129 us: step(): self.down.append(lax.ppermute(self.down[-1], 'seq', down))]
    ppermute x52 -> x0, starting transfers between devices: 71.6 us -> none  [the longest x12 29.4 us: step(): self.up.append(lax.ppermute(self.up[-1], 'seq', up))]
    reduce_scatter x4 -> x0, waiting for transfers between devices: 67.5 us -> none  [the longest x1 67.5 us: split_layer(): lax.psum_scatter(attention_part, 'seq', scatter_dimension=0, tiled=True)]
    dot_general x5 -> x2, matrix products: 66.8 us -> 18 us  [times_transposed(): lax.dot_general(operand, matrix, (((1,), (1,)), ((), ())), preferred_elem...]
    psum x0 -> x1, waiting for transfers between devices: none -> 41.4 us  [split_layer(): down_sum = lax.psum(down_grad, 'seq')]
    dot_general x5 -> x2, matrix products: 56.6 us -> 16.2 us  [dot_nn(): return jnp.dot(a, b, preferred_element_type=jnp.float32)]
    dynamic_update_slice x16 -> x0, other arithmetic: 26.2 us -> none  [whole_line(): lax.dynamic_update_slice(total, block.astype(jnp.float32), (slot * count,...]
  transfers between devices with their start and end apart: 64 -> 9, of which waited for: 22 -> 2; matrix products, arithmetic and copies ran while one was open for 17% -> 10% of each run, Pallas kernels for 22% -> 25%
where the time goes in v2:
time: 1070 us; the launch traced here: 1060 us
  Pallas kernels  845 us (79%)
  matrix products  89.1 us (8%)
  other arithmetic  47 us (4%)
  waiting for transfers between devices  43 us (4%)
  between operations  14.5 us (1%)
  local copies, waits for them, and re-layouts  12 us (1%)
    pallas_call x11, Pallas kernels, comm_call(): pl.pallas_call(ordered(kernel, inputs, after), out_shape=out_shape, in_sp...  809 us
    dot_general x5, matrix products, transposed_times(): lax.dot_general(operand, matrix, (((0,), (0,)), ((), ())), preferred_elem...  54.9 us
    psum x1, waiting for transfers between devices, split_layer(): down_sum = lax.psum(down_grad, 'seq')  41.4 us
  transfers between devices with their start and end apart: 9, of which 2 were waited for; matrix products, arithmetic and copies ran while one was open for 10% of the time, Pallas kernels for 25%

profile of v2, /device:TPU:0, one launch (start us, length us, event | category | flops | bytes accessed | tf_op | source)
XLA Modules:
  0.0 1058.0 jit_solution(13001803518861313313)
XLA Ops:
  7.2 67.3 %entry.1 = (bf16[4,256,2048]{2,1,0:T(8,128)(2,1)}, bf16[2048,1536]{1,0:T(8,128)(2,1)}) custom-call(bf16[256,2048]{1,0:T(8,128)(2,1)} %bitcast.81, bf16[256,2048]{1,0:T(8,128)(2,1)} %refs_1_.5, bf16[256,2048]{1,0:T(8,128)(2,1)} %refs_2_.1, bf16[256,2048]{1,0:T(8,128)(2,1)} %refs_3_.1), custom_call_target="tpu_custom_call" | custom-call | flops 1 | bytes 1 | tf_op jit(solution)/shard_map/entry/pallas_call | solution.py:384
  76.9 10.0 fusion.17.refs_0_.refs_1_.refs_2_
  90.6 14.8 %stats.2 = f32[16,128]{1,0:T(8,128)} custom-call(f32[16,128]{1,0:T(8,128)} %reshape.224.refs_0_), custom_call_target="tpu_custom_call" | custom-call | flops 1 | bytes 1 | tf_op jit(solution)/shard_map/stats/pallas_call | solution.py:384
  114.1 16.4 %attend.1 = (bf16[1024,512]{1,0:T(8,128)(2,1)}, bf16[1024,512]{1,0:T(8,128)(2,1)}, bf16[1024,512]{1,0:T(8,128)(2,1)}, bf16[1024,512]{1,0:T(8,128)(2,1)}, f32[4,1024,1]{2,1,0:T(8,128)}) custom-call(f32[1024,1536]{1,0:T(8,128)} %copy-done, f32[1024,1536]{1,0:T(8,128)} %copy-done, f32[1024,1536]{1,0:T(8,128)} %copy-done, f32[1024,1]{1,0:T(8,128)} %copy.26.refs_3_, ...), custom_call_target="tpu_custom_call" | custom-call | flops 1073741824 | bytes 10485760 | tf_op jit(solution)/shard_map/attend/pallas_call | solution.py:1422
  130.5 53.4 %to_tokens.1 = (bf16[256,2048]{1,0:T(8,128)(2,1)}, bf16[8,256,1024]{2,1,0:T(8,128)(2,1)}) custom-call(bf16[4,256,512]{2,1,0:T(8,128)(2,1)} %bitcast.87, bf16[256,8192]{1,0:T(8,128)(2,1)} %refs_1_.6), custom_call_target="tpu_custom_call" | custom-call | flops 1 | bytes 1 | tf_op jit(solution)/shard_map/to_tokens/pallas_call | solution.py:384
  183.9 6.2 multiply_reduce_fusion.7
  191.8 102.0 %gather_hidden.1 = (bf16[8,256,2048]{2,1,0:T(8,128)(2,1)}, bf16[8,256,1024]{2,1,0:T(8,128)(2,1)}, bf16[8,256,1024]{2,1,0:T(8,128)(2,1)}, bf16[8,256,1024]{2,1,0:T(8,128)(2,1)}, bf16[8,256,1024]{2,1,0:T(8,128)(2,1)}) custom-call(bf16[256,2048]{1,0:T(8,128)(2,1)} %fusion.7.refs_0_, bf16[256,8192]{1,0:T(8,128)(2,1)} %refs_1_.7, bf16[2048,1024]{1,0:T(8,128)(2,1)} %bitcast.79), custom_call_target="tpu_custom_call" | custom-call | flops 1 | bytes 1 | tf_op jit(solution)/shard_map/gather_hidden/pallas_call | solution.py:384
  293.8 49.2 %out_scatter.1 = f32[256,2048]{1,0:T(8,128)} custom-call(bf16[8,256,1024]{2,1,0:T(8,128)(2,1)} %get-tuple-element.43.refs_0_, bf16[1024,2048]{1,0:T(8,128)(2,1)} %refs_1_.9), custom_call_target="tpu_custom_call" | custom-call | flops 1 | bytes 1 | tf_op jit(solution)/shard_map/out_scatter/pallas_call | solution.py:384
  347.6 51.7 %gather_hidden_grad.1 = (bf16[8,256,2048]{2,1,0:T(8,128)(2,1)}, bf16[8,256,1024]{2,1,0:T(8,128)(2,1)}, bf16[8,256,1024]{2,1,0:T(8,128)(2,1)}) custom-call(bf16[256,2048]{1,0:T(8,128)(2,1)} %fusion.3.refs_0_, bf16[1024,2048]{1,0:T(8,128)(2,1)} %refs_1_.9, bf16[8,256,1024]{2,1,0:T(8,128)(2,1)} %get-tuple-element.44.refs_2_, ...), custom_call_target="tpu_custom_call" | custom-call | flops 1 | bytes 1 | tf_op jit(solution)/shard_map/gather_hidden_grad/pallas_call | solution.py:384
  399.3 12.8 %bitcast_convert_fusion = bf16[1024,2048]{1,0:T(8,128)(2,1)} fusion(bf16[8,256,1024]{2,1,0:T(8,128)(2,1)S(1)} %copy-done.14, bf16[8,256,2048]{2,1,0:T(8,128)(2,1)} %get-tuple-element.54), kind=kOutput, calls=%fused_computation | convolution fusion | flops 8592031744 | bytes 16777216 | tf_op jit(solution)/shard_map/dot_general | solution.py:53
  412.2 14.3 %bitcast_convert_fusion.1.refs_5_.refs_1_ = bf16[2048,1024]{1,0:T(8,128)(2,1)} fusion(bf16[8,256,2048]{2,1,0:T(8,128)(2,1)} %get-tuple-element.49, bf16[8,256,1024]{2,1,0:T(8,128)(2,1)} %get-tuple-element.47.refs_1_), kind=kOutput, calls=%fused_computation.1 | convolution fusion | flops 8592031744 | bytes 16777216 | tf_op jit(solution)/shard_map/dot_general | solution.py:53
  426.5 12.9 %bitcast_convert_fusion.2.refs_4_.refs_0_ = bf16[2048,1024]{1,0:T(8,128)(2,1)} fusion(bf16[8,256,2048]{2,1,0:T(8,128)(2,1)} %get-tuple-element.49, bf16[8,256,1024]{2,1,0:T(8,128)(2,1)S(1)} %copy-done.15), kind=kOutput, calls=%fused_computation.2 | convolution fusion | flops 8592031744 | bytes 16777216 | tf_op jit(solution)/shard_map/dot_general | solution.py:53
  439.4 57.3 %back_scatter.1 = f32[256,2048]{1,0:T(8,128)} custom-call(bf16[8,256,1024]{2,1,0:T(8,128)(2,1)} %get-tuple-element.46.refs_0_, bf16[8,256,1024]{2,1,0:T(8,128)(2,1)} %get-tuple-element.47.refs_1_, bf16[2048,1024]{1,0:T(8,128)(2,1)} %bitcast.80, bf16[2048,1024]{1,0:T(8,128)(2,1)} %bitcast.84, bf16[2048,1024]{1,0:T(8,128)(2,1)} %bitcast_convert_fusion.2.refs_4_.refs_0_, ...), custom_call_target="tpu_custom_call" | custom-call | flops 1 | bytes 1 | tf_op jit(solution)/shard_map/back_scatter/pallas_call | solution.py:384
  502.8 5.8 convolution_convert_fusion
  509.8 6.8 convolution_convert_fusion.3.refs_0_
  516.5 31.5 %to_heads.1 = bf16[4,256,512]{2,1,0:T(8,128)(2,1)} custom-call(bf16[256,2048]{1,0:T(8,128)(2,1)} %convolution_convert_fusion.3.refs_0_), custom_call_target="tpu_custom_call" | custom-call | flops 1 | bytes 1 | tf_op jit(solution)/shard_map/to_heads/pallas_call | solution.py:384
  548.0 41.4 %all-reduce.2.cloned.1.call-done.refs_7_ = bf16[1024,2048]{1,0:T(8,128)(2,1)} async-done(((bf16[1024,2048]{1,0:T(8,128)(2,1)}), bf16[1024,2048]{1,0:T(8,128)(2,1)}) %all-reduce.2.cloned.1.call-update) | async-done | bytes 4194320 | tf_op jit(solution)/shard_map/psum | solution.py:1833
  589.4 16.7 %attend_back.1 = (f32[1024,512]{1,0:T(8,128)}, f32[1024,512]{1,0:T(8,128)}, bf16[1024,512]{1,0:T(8,128)(2,1)}) custom-call(bf16[1024,512]{1,0:T(8,128)(2,1)} %get-tuple-element.50.refs_0_, bf16[1024,512]{1,0:T(8,128)(2,1)} %get-tuple-element.51.refs_1_, bf16[1024,512]{1,0:T(8,128)(2,1)} %get-tuple-element.52.refs_2_, bf16[1024,512]{1,0:T(8,128)(2,1)} %bitcast.85, ...), custom_call_target="tpu_custom_call" | custom-call | flops 2684354560 | bytes 10485760 | tf_op jit(solution)/shard_map/attend_back/pallas_call | solution.py:1471
  610.8 5.1 stats.3
  628.1 11.2 %convolution_convert_fusion.2 = bf16[1024,2048]{1,0:T(8,128)(2,1)} fusion(bf16[2048,1536]{1,0:T(8,128)(2,1)} %get-tuple-element.39.refs_1_, bf16[1024,512]{1,0:T(8,128)(2,1)S(1)} %copy-done.23, bf16[1024,512]{1,0:T(8,128)(2,1)S(1)} %get-tuple-element.76, bf16[1024,512]{1,0:T(8,128)(2,1)S(1)} %get-tuple-element.75), kind=kOutput, calls=%fused_computation.5 | convolution fusion | flops 6453985280 | bytes 13631488 | tf_op jit(solution)/shard_map/dot_general | solution.py:47
  640.0 9.2 convolution_convert_fusion.1
  649.1 69.8 %finish.1 = (f32[256,2048]{1,0:T(8,128)}, bf16[3,256,2048]{2,1,0:T(8,128)(2,1)}) custom-call(bf16[4,256,2048]{2,1,0:T(8,128)(2,1)} %bitcast.83, bf16[4,512,1536]{2,1,0:T(8,128)(2,1)} %bitcast.82), custom_call_target="tpu_custom_call" | custom-call | flops 1 | bytes 1 | tf_op jit(solution)/shard_map/finish/pallas_call | solution.py:384
  729.1 307.3 %line_sums.1 = (bf16[256,8192]{1,0:T(8,128)(2,1)}, bf16[256,8192]{1,0:T(8,128)(2,1)}, bf16[1024,2048]{1,0:T(8,128)(2,1)}) custom-call(bf16[2048,1024]{1,0:T(8,128)(2,1)} %bitcast_convert_fusion.2.refs_4_.refs_0_, bf16[2048,1024]{1,0:T(8,128)(2,1)} %bitcast_convert_fusion.1.refs_5_.refs_1_, bf16[256,2048]{1,0:T(8,128)(2,1)} %reduce-scatter.2.cloned.1.call-done.refs_2_, ...), custom_call_target="tpu_custom_call" | custom-call | flops 1 | bytes 1 | tf_op jit(solution)/shard_map/line_sums/pallas_call | solution.py:384
  1036.4 6.1 slice_convert_fusion
  (117 shorter events, 64.4 us)
Async XLA Ops:
  7.2 176.7 %all-gather.2.cloned.1.call-start = ((), (), s32[]{:S(2)}) async-start(), calls=%async_computation.1 | async-start | bytes 9437184 | tf_op jit(solution)/shard_map/all_gather | solution.py:1784
  76.8 512.5 %all-reduce.2.cloned.1.call-start = ((), (), s32[]{:S(2)}) async-start(), calls=%async_computation.2 | async-start | bytes 8388608 | tf_op jit(solution)/shard_map/psum | solution.py:1833
  183.9 6.3 copy-start.8
  183.9 6.2 copy-start.17
  293.8 51.2 %copy-start.4 = (bf16[1,256,2048]{2,1,0:T(8,128)(2,1)S(1)}, bf16[1,256,2048]{2,1,0:T(8,128)(2,1)}, u32[]{:S(2)}) copy-start(bf16[1,256,2048]{2,1,0:T(8,128)(2,1)} %param.25) | copy-start | bytes 3145732
  293.8 51.2 %copy-start.18 = (f32[2048]{0:T(1024)S(1)}, f32[2048]{0:T(1024)}, u32[]{:S(2)}) copy-start(f32[2048]{0:T(1024)} %param.24) | copy-start | bytes 24580
  347.6 51.7 %copy-start.14 = (bf16[8,256,1024]{2,1,0:T(8,128)(2,1)S(1)}, bf16[8,256,1024]{2,1,0:T(8,128)(2,1)}, u32[]{:S(2)}) copy-start(bf16[8,256,1024]{2,1,0:T(8,128)(2,1)} %get-tuple-element.43.refs_0_) | copy-start | bytes 12582916
  412.1 317.0 %reduce-scatter.2.cloned.1.call-start = ((), (), s32[]{:S(2)}) async-start(), calls=%async_computation.3 | async-start | bytes 9437184 | tf_op jit(solution)/shard_map/reduce_scatter | solution.py:1853
  412.2 14.3 %copy-start.15 = (bf16[8,256,1024]{2,1,0:T(8,128)(2,1)S(1)}, bf16[8,256,1024]{2,1,0:T(8,128)(2,1)}, u32[]{:S(2)}) copy-start(bf16[8,256,1024]{2,1,0:T(8,128)(2,1)} %get-tuple-element.46.refs_0_) | copy-start | bytes 12582916
  439.4 57.3 %copy-start.6 = (f32[256,2048]{1,0:T(8,128)S(1)}, f32[256,2048]{1,0:T(8,128)}, u32[]{:S(2)}) copy-start(f32[256,2048]{1,0:T(8,128)} %copy-done.5) | copy-start | bytes 6291460
  589.4 16.8 %slice-start = ((s8[6291456]{0:T(1024)(128)(4,1)}), s8[4194304]{0:T(1024)(128)(4,1)S(1)}, s32[]{:S(2)}) async-start(s8[6291456]{0:T(1024)(128)(4,1)} %bitcast.77), calls=%async_computation.4 | async-start | bytes 8388608
  589.4 16.8 %slice-start.1 = ((s8[6291456]{0:T(1024)(128)(4,1)}), s8[2097152]{0:T(1024)(128)(4,1)S(1)}, s32[]{:S(2)}) async-start(s8[6291456]{0:T(1024)(128)(4,1)} %bitcast.77), calls=%async_computation.5 | async-start | bytes 4194304
  589.4 16.8 %copy-start.20 = (f32[512]{0:T(512)S(1)}, f32[512]{0:T(512)}, u32[]{:S(2)}) copy-start(f32[512]{0:T(512)} %dynamic_slice.6) | copy-start | bytes 6148
  589.4 16.8 %copy-start.21 = (f32[512]{0:T(512)S(1)}, f32[512]{0:T(512)}, u32[]{:S(2)}) copy-start(f32[512]{0:T(512)} %dynamic_slice.7) | copy-start | bytes 6148
  606.2 11.6 %copy-start.19 = (f32[16,128]{1,0:T(8,128)S(1)}, f32[16,128]{1,0:T(8,128)}, u32[]{:S(2)}) copy-start(f32[16,128]{1,0:T(8,128)} %stats.2) | copy-start | bytes 24580
  610.1 5.9 collective-permute-start
  616.0 4.0 collective-permute-start.1
  620.1 6.1 collective-permute-start.2
  626.2 13.1 %collective-permute-start.3 = (f32[4,2048]{1,0:T(4,128)S(1)}, f32[4,2048]{1,0:T(4,128)S(1)}, u32[]{:S(2)}, u32[]{:S(2)}) collective-permute-start(f32[4,2048]{1,0:T(4,128)S(1)} %add.102), channel_id=1, source_target_pairs={{0,8},{24,16},{1,9},{25,17},{2,10},{26,18},{3,11},{27,19},{4,12},{... | collective-permute-start | bytes 98312 | tf_op jit(solution)/shard_map/ppermute | solution.py:1753
  628.1 11.9 %copy-start.22 = (bf16[4,256,2048]{2,1,0:T(8,128)(2,1)S(1)}, bf16[4,256,2048]{2,1,0:T(8,128)(2,1)}, u32[]{:S(2)}) copy-start(bf16[4,256,2048]{2,1,0:T(8,128)(2,1)} %get-tuple-element.38) | copy-start | bytes 12582916
  639.3 79.7 %collective-permute-start.4 = (f32[4,2048]{1,0:T(4,128)S(1)}, f32[4,2048]{1,0:T(4,128)S(1)}, u32[]{:S(2)}, u32[]{:S(2)}) collective-permute-start(f32[4,2048]{1,0:T(4,128)S(1)} %add.103), channel_id=1, source_target_pairs={{8,16},{16,8},{9,17},{17,9},{10,18},{18,10},{11,19},{19,11},{12,20... | collective-permute-start | bytes 98312 | tf_op jit(solution)/shard_map/ppermute | solution.py:1753
  649.1 71.2 %copy-start.3 = (f32[256,2048]{1,0:T(8,128)S(1)}, f32[256,2048]{1,0:T(8,128)}, u32[]{:S(2)}) copy-start(f32[256,2048]{1,0:T(8,128)} %back_scatter.1) | copy-start | bytes 6291460
  719.0 9.5 collective-permute-start.5
  1036.4 6.1 copy-start.11
  (11 other events, 31.6 us)
Sparse Core Ops, SparseCore 0:
  76.9 65.7 all-gather.1
  412.3 177.0 all-reduce.1
  593.8 73.6 reduce-scatter.1

commit v3 on v2

--- a/solution.py
+++ b/solution.py
@@ -641,6 +641,68 @@
 EXCHANGE = [DMA, DMA((8,)), DMA((8,))]
 
 
+class PairExchange(ColumnExchange):
+    def start(self):
+        _, cols, local, send, receive = self.parts
+        seq, shard = self.seq, self.shard
+        self.sender = lax.rem(shard, 2) == lax.rem(seq, 2)
+        copies = {
+            mask: remote(
+                self.block(flip_mask(shard, mask)),
+                cols.at[shard],
+                send.at[mask],
+                receive.at[mask],
+                (seq, flip_mask(shard, mask)),
+            )
+            for mask in range(1, 8)
+        }
+        copies[1].start()
+        self.started = [copies[1]]
+        self.sent = [copies[mask] for mask in (2, 4, 3, 5, 6, 7)]
+
+        @pl.when(self.sender)
+        def _():
+            for copy in self.sent:
+                copy.start()
+
+        self.own = pltpu.make_async_copy(self.block(shard), cols.at[shard], local)
+        self.own.start()
+
+    def turn(self, bits):
+        _, cols, _, send, receive = self.parts
+        parity = lax.rem(lax.rem(self.shard, 2) + lax.rem(self.seq, 2), 2)
+        here, there = bits + parity, bits + 1 - parity
+        spot, came = cols.at[flip_by(self.shard, here)], cols.at[flip_by(self.shard, there)]
+        pair = (flip(self.seq, 1), self.shard)
+        arrival = remote(spot, spot, send.at[here], receive.at[here], pair)
+        onward = remote(spot, spot, send.at[8 + bits // 2], receive.at[here], pair)
+        swapped = remote(came, came, send.at[8 + bits // 2], receive.at[there], pair)
+        return arrival, onward, swapped
+
+    def relay(self, bits):
+        arrival, onward, _ = self.turn(bits)
+        arrival.wait_recv()
+        onward.start()
+
+    def wait(self):
+        self.own.wait()
+        for copy in self.started:
+            copy.wait()
+
+        @pl.when(self.sender)
+        def _():
+            for copy in self.sent:
+                copy.wait_send()
+
+        for bits in (2, 4, 6):
+            _, onward, swapped = self.turn(bits)
+            onward.wait_send()
+            swapped.wait_recv()
+
+
+PAIR_EXCHANGE = [DMA, DMA((12,)), DMA((8,))]
+
+
 def columns_shape(weight):
     rows, width = weight.shape
     return jax.ShapeDtypeStruct((8, rows, width // 8), weight.dtype)
@@ -718,12 +780,16 @@
     )
 
 
-def to_heads_kernel(tokens, heads, local, send, receive):
+def to_heads_kernel(
+    tokens, attended, grads, heads, out, part, *scratch
+):
+    local, send, receive = scratch[-3:]
+    scratch = scratch[:-3]
     seq, shard = place()
+    greet(column_others(seq, shard) + plane_others(seq, shard)[1:])
     core, half = lax.rem(shard, 2), lax.div(seq, 2)
     base = shard - core
     width = heads.shape[2]
-    greet(column_others(seq, shard))
     here = core == half
     mine = 2 * lax.rem(seq, 2) + core
     copies = []
@@ -743,6 +809,16 @@
             copy.start()
 
         copies.append((self_copy, own, copy))
+    def produce(block):
+        rows = out.shape[0]
+        span = pl.ds(pl.multiple_of(block * rows, rows), rows)
+
+        def tile(at):
+            part[block, :, at] = dot_tn(attended[:, span], grads[:, at]).astype(jnp.bfloat16)
+
+        tiles(grads.shape[1], tile)
+
+    scatter_products(produce, part, out, *scratch, meet=False)
     for self_copy, own, copy in copies:
 
         @pl.when(self_copy)
@@ -763,15 +839,19 @@
             arrival.wait_recv()
 
 
-def to_heads(tokens, number, after=()):
+def to_heads(tokens, attended, grads, number, after=()):
     rows, width = tokens.shape
+    low = tokens.dtype
     return comm_call(
         to_heads_kernel,
-        jax.ShapeDtypeStruct((4, rows, width // 4), tokens.dtype),
-        (tokens,),
-        [ANY],
-        ANY,
-        [DMA, DMA((4,)), DMA((4,))],
+        (
+            jax.ShapeDtypeStruct((4, rows, width // 4), low),
+            jax.ShapeDtypeStruct((rows, width), jnp.float32),
+        ),
+        (tokens, attended, grads),
+        [ANY, VM, VM],
+        (ANY, VM),
+        scatter_scratch(rows, width) + [DMA, DMA((4,)), DMA((4,))],
         "to_heads",
         number,
         after,
@@ -782,7 +862,7 @@
     seq, shard = place()
     core = lax.rem(shard, 2)
     near = [(seq, flip(shard, bit)) for bit in (2, 4, 1)]
-    greet(plane_others(seq, shard) if exchange else near)
+    greet(plane_others(seq, shard) + [(flip(seq, 1), shard)] if exchange else near)
     own = pltpu.make_async_copy(x, out.at[shard], local)
     own.start()
     firsts = [
@@ -821,6 +901,9 @@
     two.start()
     ready(first)
     ready(second)
+    if exchange:
+        exchange.relay(2)
+        exchange.relay(4)
     arrival(flip(mate_shard, 2), 4).wait_recv()
     ready(flip(mate_shard, 2))
     arrival(diagonal, 3).wait_recv()
@@ -831,6 +914,8 @@
     ready(diagonal)
     arrival(flip_mask(mate_shard, 6), 6).wait_recv()
     ready(flip_mask(mate_shard, 6))
+    if exchange:
+        exchange.relay(6)
     for copy in firsts + [across, one, two, three]:
         copy.wait_send()
 
@@ -874,7 +959,7 @@
     plane_in, up_in, gate_wide, gate_low, up_low, hidden_low, local, send, receive, store,
     up_store, cols_local, cols_send, cols_receive
 ):
-    exchange = ColumnExchange(weight, up_in, cols_local, cols_send, cols_receive)
+    exchange = PairExchange(weight, up_in, cols_local, cols_send, cols_receive)
     width = gate_wide.shape[2]
     early = Stores([(plane_in, plane), (gate_low, gate)], store.at[0])
     late = Stores([(up_low, upward), (hidden_low, hidden)], store.at[1])
@@ -931,7 +1016,7 @@
         ]
         + [pltpu.VMEM(narrow, low)] * 3
         + [DMA, DMA((7,)), DMA((7,)), DMA((2, 2, 8)), DMA]
-        + EXCHANGE,
+        + PAIR_EXCHANGE,
         "gather_hidden",
         number,
         after,
@@ -1000,7 +1085,9 @@
     lax.fori_loop(0, rows // step, one, 0)
 
 
-def scatter_products(produce, part, out, mated, first_in, second_in, sums, sem_s, sem_r):
+def scatter_products(
+    produce, part, out, mated, first_in, second_in, sums, sem_s, sem_r, meet=True
+):
     seq, shard = place()
     core, chip = lax.rem(shard, 2), lax.div(shard, 2)
     rows = out.shape[0] // PIECES
@@ -1009,7 +1096,8 @@
     first, second = flip_bit(chip, bit), flip_bit(chip, 3 - bit)
     diagonal = 3 - chip
     first_device, second_device = (seq, 2 * first + core), (seq, 2 * second + core)
-    greet([mate, first_device, second_device])
+    if meet:
+        greet([mate, first_device, second_device])
 
     def piece(index):
         return pl.ds(index * rows, rows)
@@ -1129,33 +1217,327 @@
     scatter_products(produce, part, out, *scratch)
 
 
+def scatter_scratch(rows, width):
+    low = jnp.bfloat16
+    return [
+        pltpu.VMEM((8, rows, width), low),
+        pltpu.VMEM((4, rows, width), low),
+        pltpu.VMEM((2, rows, width), low),
+        pltpu.VMEM((rows, width), low),
+        pltpu.VMEM((3, rows, width), low),
+        DMA((3, 4, PIECES)),
+        DMA((3, 4, PIECES)),
+    ]
+
+
 def plane_scatter(kernel, inputs, rows, width, name, number, after=()):
-    low = jnp.bfloat16
     return comm_call(
         kernel,
         jax.ShapeDtypeStruct((rows, width), jnp.float32),
         inputs,
         [VM] * len(inputs),
         VM,
-        [
-            pltpu.VMEM((8, rows, width), low),
-            pltpu.VMEM((4, rows, width), low),
-            pltpu.VMEM((2, rows, width), low),
-            pltpu.VMEM((rows, width), low),
-            pltpu.VMEM((3, rows, width), low),
-            DMA((3, 4, PIECES)),
-            DMA((3, 4, PIECES)),
-        ],
+        scatter_scratch(rows, width),
         name,
         number,
         after,
     )
 
 
+LINE_ROWS = 128
+RING = 4
+
+
+def flip_by(value, mask):
+    for bit in (1, 2, 4):
+        here, there = lax.rem(lax.div(value, bit), 2), lax.rem(lax.div(mask, bit), 2)
+        value = value + bit * (lax.rem(here + there, 2) - here)
+    return value
+
+
+class LineSums:
+    def __init__(self, gate, up, late, gate_rows, up_rows, out, landed, scratch):
+        self.gate, self.up, self.late = gate, up, late
+        self.rows_out, self.out = (gate_rows, up_rows), out
+        self.first_in, self.second_in, self.total_in = landed
+        (
+            self.own, self.sums, self.others, self.totals,
+            self.own_sem, self.load_sem, self.keep_sem, self.send, self.receive,
+            self.spread_send, self.spread_receive,
+        ) = scratch
+        self.seq, self.shard = place()
+        self.inner = jnp.logical_or(self.seq == 1, self.seq == 2)
+        self.outer = jnp.logical_not(self.inner)
+        self.beside = (self.seq + 1 - 2 * lax.rem(self.seq, 2), self.shard)
+        self.across = (3 - self.seq, self.shard)
+        self.rows, self.width = gate_rows.shape[0], gate.shape[1]
+        self.cuts = self.rows // LINE_ROWS
+        self.early = 8 * self.cuts
+        self.count = self.early + len(late)
+        self.away = 7 * self.cuts
+        self.halves = (slice(0, self.width), slice(self.width, 2 * self.width))
+
+    def is_late(self, index):
+        return isinstance(index, int) and index >= self.early
+
+    def owner(self, index):
+        return flip_by(self.shard, 7 - lax.div(index, self.cuts))
+
+    def sources(self, index):
+        if self.is_late(index):
+            return [(self.late[index - self.early], slice(0, 2 * self.width))]
+        start = self.owner(index) * self.rows + lax.rem(index, self.cuts) * LINE_ROWS
+        span = pl.ds(pl.multiple_of(start, LINE_ROWS), LINE_ROWS)
+        return list(zip((self.gate.at[span], self.up.at[span]), self.halves))
+
+    def inward(self, index):
+        return [
+            remote(
+                source,
+                self.first_in.at[index, :, half],
+                self.send.at[side, index],
+                self.receive.at[side, index],
+                self.beside,
+            )
+            for side, (source, half) in enumerate(self.sources(index))
+        ]
+
+    def swap(self, index):
+        return remote(
+            self.sums.at[lax.rem(index, RING)],
+            self.second_in.at[index],
+            self.send.at[2, index],
+            self.receive.at[2, index],
+            self.across,
+        )
+
+    def result(self, index):
+        if self.is_late(index):
+            start = (index - self.early) * LINE_ROWS
+            return self.out.at[start : start + LINE_ROWS]
+        return self.total_in.at[index]
+
+    def outward(self, index):
+        return remote(
+            self.totals.at[lax.rem(index, RING)],
+            self.result(index),
+            self.send.at[3, index],
+            self.receive.at[3, index],
+            self.beside,
+        )
+
+    def keep(self, index):
+        return pltpu.make_async_copy(
+            self.totals.at[lax.rem(index, RING)], self.result(index), self.keep_sem.at[index]
+        )
+
+    def own_loads(self, index):
+        slot = lax.rem(index, 2)
+        return [
+            pltpu.make_async_copy(
+                source, self.own.at[slot, :, half], self.own_sem.at[slot, side]
+            )
+            for side, (source, half) in enumerate(self.sources(index))
+        ]
+
+    def spread(self, index, side, source, away):
+        down = pl.ds(
+            pl.multiple_of(lax.rem(index, self.cuts) * LINE_ROWS, LINE_ROWS), LINE_ROWS
+        )
+        along = pl.ds(pl.multiple_of(self.shard * self.width, self.width), self.width)
+        source = source.at[:, self.halves[side]]
+        spot = self.rows_out[side].at[down, along]
+        if not away:
+            return pltpu.make_async_copy(source, spot, self.spread_send.at[side, index])
+        return remote(
+            source,
+            spot,
+            self.spread_send.at[side, index],
+            self.spread_receive.at[side, index],
+            (self.seq, self.owner(index)),
+        )
+
+    def spread_each(self, index, source, there, here):
+        for side in range(2):
+
+            @pl.when(index < self.away)
+            def _():
+                there(self.spread(index, side, source, True))
+
+            @pl.when(index >= self.away)
+            def _():
+                here(self.spread(index, side, source, False))
+
+    def spread_start(self, index, source):
+        self.spread_each(index, source, lambda copy: copy.start(), lambda copy: copy.start())
+
+    def spread_sent(self, index, source):
+        self.spread_each(index, source, lambda copy: copy.wait_send(), lambda copy: copy.wait())
+
+    def add_up(self, target, first, second):
+        def add(at):
+            target[at] = (
+                first[at].astype(jnp.float32) + second[at].astype(jnp.float32)
+            ).astype(jnp.bfloat16)
+
+        add_rows(LINE_ROWS, add)
+
+    def begin(self):
+        @pl.when(self.outer)
+        def _():
+            for copy in self.inward(0):
+                copy.start()
+
+        @pl.when(self.inner)
+        def _():
+            for copy in self.own_loads(0):
+                copy.start()
+
+    def retire(self, index):
+        self.outward(index).wait_send()
+        if self.is_late(index):
+            self.keep(index).wait()
+        else:
+            self.spread_sent(index, self.totals.at[lax.rem(index, RING)])
+
+    def close(self, index):
+        slot = lax.rem(index, RING)
+        self.swap(index).wait_recv()
+        load = pltpu.make_async_copy(
+            self.second_in.at[index], self.others, self.load_sem.at[1]
+        )
+        load.start()
+        if isinstance(index, int):
+            self.retire(index - RING)
+        else:
+
+            @pl.when(index >= RING)
+            def _():
+                self.retire(index - RING)
+
+        load.wait()
+        self.add_up(self.totals.at[slot], self.sums.at[slot], self.others)
+        self.outward(index).start()
+        if self.is_late(index):
+            self.keep(index).start()
+        else:
+            self.spread_start(index, self.totals.at[slot])
+
+    def inner_step(self, index, following):
+        slot = lax.rem(index, RING)
+        if following:
+            for copy in self.own_loads(index + 1):
+                copy.start()
+        for copy in self.inward(index):
+            copy.wait_recv()
+        if isinstance(index, int):
+            self.swap(index - RING).wait_send()
+        else:
+
+            @pl.when(index >= RING)
+            def _():
+                self.swap(index - RING).wait_send()
+
+        load = pltpu.make_async_copy(
+            self.first_in.at[index], self.sums.at[slot], self.load_sem.at[0]
+        )
+        load.start()
+        for copy in self.own_loads(index):
+            copy.wait()
+        load.wait()
+        self.add_up(self.sums.at[slot], self.sums.at[slot], self.own.at[lax.rem(index, 2)])
+        self.swap(index).start()
+        if isinstance(index, int):
+            self.close(index - 1)
+        else:
+
+            @pl.when(index > 0)
+            def _():
+                self.close(index - 1)
+
+    def outer_take(self, index):
+        self.outward(index).wait_recv()
+        if not self.is_late(index):
+            self.spread_start(index, self.total_in.at[index])
+
+    def outer_step(self, index, following):
+        if following:
+            for copy in self.inward(index + 1):
+                copy.start()
+        if isinstance(index, int):
+            self.outer_take(index - 3)
+        else:
+
+            @pl.when(index >= 3)
+            def _():
+                self.outer_take(index - 3)
+
+    def step(self, index, following=True):
+        @pl.when(self.inner)
+        def _():
+            self.inner_step(index, following)
+
+        @pl.when(self.outer)
+        def _():
+            self.outer_step(index, following)
+
+    def run(self, start, stop):
+        def one(index, carry):
+            self.step(index)
+            return carry
+
+        lax.fori_loop(start, min(stop, self.early - 1), one, 0)
+
+    def finish(self):
+        early, count = self.early, self.count
+        for index in range(early - 1, count):
+            self.step(index, index + 1 < count)
+
+        @pl.when(self.inner)
+        def _():
+            self.close(count - 1)
+            for index in range(count - RING, count):
+                self.swap(index).wait_send()
+                self.retire(index)
+
+        def each(body):
+            def one(index, carry):
+                body(index)
+                return carry
+
+            lax.fori_loop(0, early, one, 0)
+
+        @pl.when(self.outer)
+        def _():
+            for index in range(count - 3, count):
+                self.outer_take(index)
+
+            def sent(index):
+                for copy in self.inward(index):
+                    copy.wait_send()
+                self.spread_sent(index, self.total_in.at[index])
+
+            each(sent)
+            for index in range(early, count):
+                for copy in self.inward(index):
+                    copy.wait_send()
+
+        def received(index):
+            for side in range(2):
+
+                @pl.when(index < self.away)
+                def _():
+                    self.spread(index, side, self.total_in.at[index], True).wait_recv()
+
+        each(received)
+
+
 def finish_kernel(
-    part, grads, out, placed,
+    joined, weight, whole, gate, up, out_grad,
+    out, gate_rows, up_rows, line_out, first_chunks, second_chunks, total_chunks,
+    part, grads, placed,
     mated, sums, landed, first_in, second_in, onward, total, swapped,
-    local, sem_s, sem_r, grad_s, grad_r
+    local, sem_s, sem_r, grad_s, grad_r, *line_scratch
 ):
     seq, shard = place()
     core, half, quarter = lax.rem(shard, 2), lax.div(seq, 2), lax.rem(seq, 2)
@@ -1166,23 +1548,39 @@
     bit = 1 + core
     first, second, diagonal = flip_bit(chip, bit), flip_bit(chip, 3 - bit), 3 - chip
     first_device, second_device = (seq, 2 * first + core), (seq, 2 * second + core)
-    greet(column_others(seq, shard) + [first_device, second_device])
+    greet(column_others(seq, shard) + plane_others(seq, shard)[1:])
+    late = [
+        out_grad.at[start : start + LINE_ROWS] for start in range(0, out_grad.shape[0], LINE_ROWS)
+    ] + [
+        placed.at[index, start : start + LINE_ROWS]
+        for index in range(3)
+        for start in range(0, placed.shape[1], LINE_ROWS)
+    ]
+    line = LineSums(
+        gate, up, late, gate_rows, up_rows, line_out,
+        (first_chunks, second_chunks, total_chunks), line_scratch,
+    )
+    line.begin()
+
     mine = pl.ds(pl.multiple_of(core * rows, rows), rows)
     other = pl.ds(pl.multiple_of((1 - core) * rows, rows), rows)
     here = core == half
     order = [2 * (1 - half) + 1 - quarter, 2 * (1 - half) + quarter, flip(seq, 1), seq]
-    swaps = []
-    for slot, block in enumerate(order):
-        copy = remote(
-            part.at[block, other], mated.at[slot], sem_s.at[0, slot], sem_r.at[0, slot], mate
-        )
-        copy.start()
-        swaps.append(copy)
     long = grads.shape[1] // 2
+
+    def project(target):
+        span = pl.ds(pl.multiple_of(target * 2 * long, 2 * long), 2 * long)
+
+        def tile(at):
+            grads[target, :, at] = dot_tn(whole[:, span], joined[:, at]).astype(jnp.bfloat16)
+
+        tiles(grads.shape[2], tile)
+
     firsts = []
-    for index in range(2):
-        span = slice(index * long, (index + 1) * long)
-        for slot, target in ((0, diagonal), (1, first)):
+    for slot, target in ((0, diagonal), (1, first)):
+        project(target)
+        for index in range(2):
+            span = slice(index * long, (index + 1) * long)
             copy = remote(
                 grads.at[target, span],
                 first_in.at[slot, span],
@@ -1192,6 +1590,22 @@
             )
             copy.start()
             firsts.append(copy)
+    swaps = []
+    for slot, block in enumerate(order):
+        tokens = pl.ds(pl.multiple_of(block * 2 * rows, 2 * rows), 2 * rows)
+
+        def tile(at):
+            part[block, :, at] = dot_nt(joined[tokens], weight[at]).astype(jnp.bfloat16)
+
+        tiles(part.shape[2], tile)
+        copy = remote(
+            part.at[block, other], mated.at[slot], sem_s.at[0, slot], sem_r.at[0, slot], mate
+        )
+        copy.start()
+        swaps.append(copy)
+    line.run(0, 1)
+    project(second)
+    project(chip)
     placed[...] = jnp.zeros_like(placed)
 
     sends = []
@@ -1226,10 +1640,11 @@
                 copy.start()
 
         sends.append(copy)
+    line.run(1, 3)
 
     seconds = []
     for index in range(2):
-        firsts[2 * index].wait_recv()
+        firsts[index].wait_recv()
 
         def add(span, index=index):
             span = pl.ds(span.start + index * long, span.size)
@@ -1245,10 +1660,11 @@
         )
         copy.start()
         seconds.append(copy)
+    line.run(3, 6)
     for turn in range(2):
         start = pl.multiple_of((1 - core if turn == 0 else core) * long, long)
         if turn == 0:
-            for copy in (firsts[1], firsts[3], seconds[0], seconds[1]):
+            for copy in (firsts[2], firsts[3], seconds[0], seconds[1]):
                 copy.wait_recv()
 
         def add(span, start=start):
@@ -1278,6 +1694,7 @@
         placed[index, :, pl.ds(spot, part_width)] = swapped[
             :, index * part_width : (index + 1) * part_width
         ]
+    line.run(6, 8)
 
     for slot in range(3):
         sends[slot].wait_send()
@@ -1314,40 +1731,69 @@
         add_rows(rows, add)
     for copy in swaps + firsts + seconds + [swap]:
         copy.wait_send()
-
-
-def finish(part, grads, number, after=()):
-    _, rows, width = part.shape
-    _, long, joined = grads.shape
-    low = part.dtype
-    return comm_call(
+    line.run(8, line.early)
+    line.finish()
+
+
+def finish(joined, weight, whole, gate, up, out_grad, number, after=()):
+    length, width = whole.shape
+    rows, long, wide = length // 4, weight.shape[0] // 4, weight.shape[1]
+    low = joined.dtype
+    hidden_width = gate.shape[1]
+    tail = out_grad.shape[0] + 3 * long // 2
+    early, late = gate.shape[0] // LINE_ROWS, tail // LINE_ROWS
+    count = early + late
+    block = (LINE_ROWS, 2 * hidden_width)
+    owned = jax.ShapeDtypeStruct((gate.shape[0] // 8, 8 * hidden_width), low)
+    chunks = jax.ShapeDtypeStruct((count,) + block, low)
+    results = comm_call(
         finish_kernel,
         (
             jax.ShapeDtypeStruct((rows, width), jnp.float32),
-            jax.ShapeDtypeStruct((3, long // 2, width), low),
+            owned,
+            owned,
+            jax.ShapeDtypeStruct((tail, width), low),
+            chunks,
+            chunks,
+            chunks,
         ),
-        (part, grads),
-        [VM] * 2,
-        (VM, VM),
+        (joined, weight, whole, gate, up, out_grad),
+        [VM] * 3 + [ANY] * 3,
+        (VM,) + (ANY,) * 6,
         [
+            pltpu.VMEM((4, rows, width), low),
+            pltpu.VMEM((4, long, wide), low),
+            pltpu.VMEM((3, long // 2, width), low),
             pltpu.VMEM((4, rows // 2, width), low),
             pltpu.VMEM((4, rows // 2, width), low),
             pltpu.VMEM((2, 2, rows // 2, width), low),
-            pltpu.VMEM((2, long, joined), low),
-            pltpu.VMEM((long, joined), low),
-            pltpu.VMEM((long, joined), low),
-            pltpu.VMEM((long, joined), low),
-            pltpu.VMEM((long // 2, joined), low),
+            pltpu.VMEM((2, long, wide), low),
+            pltpu.VMEM((long, wide), low),
+            pltpu.VMEM((long, wide), low),
+            pltpu.VMEM((long, wide), low),
+            pltpu.VMEM((long // 2, wide), low),
             DMA,
             DMA((2, 4)),
             DMA((2, 4)),
             DMA((4, 2)),
             DMA((4, 2)),
+            pltpu.VMEM((2,) + block, low),
+            pltpu.VMEM((RING,) + block, low),
+            pltpu.VMEM(block, low),
+            pltpu.VMEM((RING,) + block, low),
+            DMA((2, 2)),
+            DMA((2,)),
+            DMA((count,)),
+            DMA((4, count)),
+            DMA((4, count)),
+            DMA((2, early)),
+            DMA((2, early)),
         ],
         "finish",
         number,
         after,
     )
+    return results[:4]
 
 
 def turn_heads(values, cosine, signed):
@@ -1486,268 +1932,6 @@
     )(*inputs, *after)
 
 
-LINE_ROWS = 128
-
-
-def flip_by(value, mask):
-    for bit in (1, 2, 4):
-        here, there = lax.rem(lax.div(value, bit), 2), lax.rem(lax.div(mask, bit), 2)
-        value = value + bit * (lax.rem(here + there, 2) - here)
-    return value
-
-
-def line_kernel(
-    gate, up, out_part, rest, gate_rows, up_rows, out,
-    first, second, held, total, load_sem, send, receive, spread_send, spread_receive
-):
-    seq, shard = place()
-    inner = jnp.logical_or(seq == 1, seq == 2)
-    outer = jnp.logical_not(inner)
-    beside = (seq + 1 - 2 * lax.rem(seq, 2), shard)
-    across = (3 - seq, shard)
-    greet([beside, across] + plane_others(seq, shard))
-    rows, width = gate_rows.shape[0], gate.shape[1]
-    cuts = rows // LINE_ROWS
-    early = 8 * cuts
-    late = [
-        part.at[start : start + LINE_ROWS]
-        for part in (out_part, rest)
-        for start in range(0, part.shape[0], LINE_ROWS)
-    ]
-    count = early + len(late)
-
-    def owner(index):
-        return flip_by(shard, 7 - lax.div(index, cuts))
-
-    def sources(index):
-        start = owner(index) * rows + lax.rem(index, cuts) * LINE_ROWS
-        span = pl.ds(pl.multiple_of(start, LINE_ROWS), LINE_ROWS)
-        return gate.at[span], up.at[span]
-
-    halves = (slice(0, width), slice(width, 2 * width))
-
-    def inward(index, side, source):
-        return remote(
-            source,
-            first.at[index, :, halves[side]],
-            send.at[side, index],
-            receive.at[side, index],
-            beside,
-        )
-
-    def inward_late(index, source):
-        return remote(source, first.at[index], send.at[0, index], receive.at[0, index], beside)
-
-    def swap(index):
-        return remote(
-            first.at[index], second.at[index], send.at[2, index], receive.at[2, index], across
-        )
-
-    def outward(index):
-        return remote(
-            total.at[index], total.at[index], send.at[3, index], receive.at[3, index], beside
-        )
-
-    def outward_late(index, place_in_out):
-        here = out.at[place_in_out * LINE_ROWS : (place_in_out + 1) * LINE_ROWS]
-        return remote(here, here, send.at[3, index], receive.at[3, index], beside)
-
-    def spread(index, side, away=True):
-        target = (gate_rows, up_rows)[side]
-        down = pl.ds(pl.multiple_of(lax.rem(index, cuts) * LINE_ROWS, LINE_ROWS), LINE_ROWS)
-        along = pl.ds(pl.multiple_of(shard * width, width), width)
-        source, spot = total.at[index, :, halves[side]], target.at[down, along]
-        if not away:
-            return pltpu.make_async_copy(source, spot, spread_send.at[side, index])
-        return remote(
-            source,
-            spot,
-            spread_send.at[side, index],
-            spread_receive.at[side, index],
-            (seq, owner(index)),
-        )
-
-    away = 7 * cuts
-
-    def each(start, stop, body):
-        def one(index, carry):
-            body(index)
-            return carry
-
-        lax.fori_loop(start, stop, one, 0)
-
-    def spread_start(index):
-        for side in range(2):
-
-            @pl.when(index < away)
-            def _():
-                spread(index, side).start()
-
-            @pl.when(index >= away)
-            def _():
-                spread(index, side, False).start()
-
-    @pl.when(outer)
-    def _():
-        def start(index):
-            for side, source in enumerate(sources(index)):
-                inward(index, side, source).start()
-
-        each(0, early, start)
-        for spot, part in enumerate(late):
-            inward_late(early + spot, part).start()
-
-        def finish_one(index):
-            outward(index).wait_recv()
-            spread_start(index)
-
-        each(0, early, finish_one)
-        for spot in range(len(late)):
-            outward_late(early + spot, spot).wait_recv()
-
-        def sent(index):
-            for side, source in enumerate(sources(index)):
-                inward(index, side, source).wait_send()
-
-        each(0, early, sent)
-        for spot, part in enumerate(late):
-            inward_late(early + spot, part).wait_send()
-
-    @pl.when(inner)
-    def _():
-        def loads(index):
-            slot = lax.rem(index, 2)
-            for side, source in enumerate(sources(index)):
-                yield pltpu.make_async_copy(
-                    source, held.at[slot, :, halves[side]], load_sem.at[slot, side]
-                )
-
-        def load(index):
-            for copy in loads(index):
-                copy.start()
-
-        def add_in(index, own):
-            def add(at):
-                first[index, at] = (
-                    first[index, at].astype(jnp.float32) + own(at).astype(jnp.float32)
-                ).astype(jnp.bfloat16)
-
-            add_rows(LINE_ROWS, add)
-            swap(index).start()
-
-        def add_up(index, store):
-            swap(index).wait_recv()
-
-            def add(at):
-                store(
-                    at,
-                    (
-                        first[index, at].astype(jnp.float32)
-                        + second[index, at].astype(jnp.float32)
-                    ).astype(jnp.bfloat16),
-                )
-
-            add_rows(LINE_ROWS, add)
-
-        def total_store(index):
-            def store(at, value):
-                total[index, at] = value
-
-            return store
-
-        def close(index):
-            add_up(index, total_store(index))
-            outward(index).start()
-            spread_start(index)
-
-        def step(index):
-            @pl.when(index + 1 < early)
-            def _():
-                load(index + 1)
-
-            for copy in loads(index):
-                copy.wait()
-            for side, source in enumerate(sources(index)):
-                inward(index, side, source).wait_recv()
-            slot = lax.rem(index, 2)
-            add_in(index, lambda at: held[slot, at])
-
-            @pl.when(index > 0)
-            def _():
-                close(index - 1)
-
-        load(0)
-        each(0, early, step)
-
-        def close_late(spot):
-            def store(at, value):
-                out[pl.ds(at.start + spot * LINE_ROWS, at.size)] = value
-
-            add_up(early + spot, store)
-            outward_late(early + spot, spot).start()
-
-        for spot, part in enumerate(late):
-            inward_late(early + spot, part).wait_recv()
-            add_in(early + spot, lambda at, part=part: part[at])
-            if spot:
-                close_late(spot - 1)
-            else:
-                close(early - 1)
-        close_late(len(late) - 1)
-
-        def sent(index):
-            swap(index).wait_send()
-            outward(index).wait_send()
-
-        each(0, early, sent)
-        for spot in range(len(late)):
-            swap(early + spot).wait_send()
-            outward_late(early + spot, spot).wait_send()
-
-    def spread_wait(index):
-        for side in range(2):
-
-            @pl.when(index < away)
-            def _():
-                spread(index, side).wait()
-
-            @pl.when(index >= away)
-            def _():
-                spread(index, side, False).wait()
-
-    each(0, early, spread_wait)
-
-
-def line_sums(gate, up, out_part, rest, number, after=()):
-    rows, width = gate.shape[0] // 8, gate.shape[1]
-    low = gate.dtype
-    tail = (out_part.shape[0] + rest.shape[0], rest.shape[1])
-    early, late = gate.shape[0] // LINE_ROWS, tail[0] // LINE_ROWS
-    block = (LINE_ROWS, 2 * width)
-    owned = jax.ShapeDtypeStruct((rows, 8 * width), low)
-    return comm_call(
-        line_kernel,
-        (owned, owned, jax.ShapeDtypeStruct(tail, low)),
-        (gate, up, out_part, rest),
-        [ANY, ANY, VM, VM],
-        (ANY, ANY, VM),
-        [
-            pltpu.VMEM((early + late,) + block, low),
-            pltpu.VMEM((early + late,) + block, low),
-            pltpu.VMEM((2,) + block, low),
-            pltpu.VMEM((early,) + block, low),
-            DMA((2, 2)),
-            DMA((4, early + late)),
-            DMA((4, early + late)),
-            DMA((2, early)),
-            DMA((2, early)),
-        ],
-        "line_sums",
-        number,
-        after,
-    )
-
-
 def line_total(part):
     for route in ([(0, 1), (3, 2)], [(1, 2), (2, 1)]):
         part = part + lax.ppermute(part, "seq", route)
@@ -1849,10 +2033,8 @@
     )
     branch_grad = branch_float.astype(low)
     attended_grad = times_transposed(branch_grad, out_full).astype(low)
-    head_grad = to_heads(attended_grad, 8).reshape(length, group_width)
-    out_grad = lax.psum_scatter(
-        transposed_times(attended, branch_grad).astype(low), "fsdp", scatter_dimension=0, tiled=True
-    )
+    head_grad, out_grad = to_heads(attended_grad, attended, branch_grad, 8)
+    head_grad, out_grad = head_grad.reshape(length, group_width), out_grad.astype(low)
     q_norm_grad, k_norm_grad, value_grad = attend_back(
         queries, keys, values, head_grad, log_total, cosine, signed, head_size, (down_sum,)
     )
@@ -1865,18 +2047,11 @@
     q_raw_grad = (q_factor * q_scaled - q_raw * (q_factor * q_factor * q_factor * q_inner)).astype(low)
     k_raw_grad = (k_factor * k_scaled - k_raw * (k_factor * k_factor * k_factor * k_inner)).astype(low)
     joined = jnp.concatenate([q_raw_grad, k_raw_grad, value_grad], axis=1)
-    input_part = times_transposed(joined, qkv).astype(low)
-    qkv_grad = transposed_times(whole, joined).astype(low)
-    input_sum, attention_part = finish(
-        input_part.reshape(4, tokens, width),
-        qkv_grad.reshape(4, 2 * rows, 3 * group_width),
-        10,
+    input_sum, gate_rows, up_rows, late = finish(
+        joined, qkv, whole, gate_sum, up_sum, out_grad, 10
     )
     input_grad = residual_grad + input_sum
 
-    gate_rows, up_rows, late = line_sums(
-        gate_sum, up_sum, out_grad, attention_part.reshape(3 * rows, width), 11
-    )
     down_total = down_sum.astype(jnp.float32)
     gate_total, up_total = gate_rows.astype(jnp.float32), up_rows.astype(jnp.float32)
     out_total, query_total, key_total, value_total = (

time: 1070 us -> 1040 us (0.972)
  matrix products: 89.1 us -> 62.9 us
    dot_general x5 -> x3, matrix products: 54.9 us -> 40 us  [transposed_times(): lax.dot_general(operand, matrix, (((0,), (0,)), ((), ())), preferred_elem...]
    dot_general x2 -> x1, matrix products: 18 us -> 6.74 us  [times_transposed(): lax.dot_general(operand, matrix, (((1,), (1,)), ((), ())), preferred_elem...]
    pallas_call x11 -> x10, Pallas kernels: 809 us -> 814 us  [comm_call(): pl.pallas_call(ordered(kernel, inputs, after), out_shape=out_shape, in_sp...]
  transfers between devices with their start and end apart: 9 -> 8, of which waited for: 2 -> 2; matrix products, arithmetic and copies ran while one was open for 10% -> 9% of each run, Pallas kernels for 25% -> 55%
where the time goes in v3:
time: 1040 us; the launch traced here: 1030 us
  Pallas kernels  849 us (82%)
  matrix products  62.9 us (6%)
  other arithmetic  48 us (5%)
  waiting for transfers between devices  35.1 us (3%)
  between operations  15 us (1%)
  local copies, waits for them, and re-layouts  11.8 us (1%)
    pallas_call x10, Pallas kernels, comm_call(): pl.pallas_call(ordered(kernel, inputs, after), out_shape=out_shape, in_sp...  814 us
    dot_general x3, matrix products, transposed_times(): lax.dot_general(operand, matrix, (((0,), (0,)), ((), ())), preferred_elem...  40 us
    psum x1, waiting for transfers between devices, split_layer(): down_sum = lax.psum(down_grad, 'seq')  33.3 us
  transfers between devices with their start and end apart: 8, of which 2 were waited for; matrix products, arithmetic and copies ran while one was open for 9% of the time, Pallas kernels for 55%

profile of v3, /device:TPU:0, one launch (start us, length us, event | category | flops | bytes accessed | tf_op | source)
XLA Modules:
  0.0 1029.3 jit_solution(5795020772435114895)
XLA Ops:
  7.2 67.3 %entry.1 = (bf16[4,256,2048]{2,1,0:T(8,128)(2,1)}, bf16[2048,1536]{1,0:T(8,128)(2,1)}) custom-call(bf16[256,2048]{1,0:T(8,128)(2,1)} %bitcast.74, bf16[256,2048]{1,0:T(8,128)(2,1)} %refs_1_.5, bf16[256,2048]{1,0:T(8,128)(2,1)} %refs_2_.1, bf16[256,2048]{1,0:T(8,128)(2,1)} %refs_3_.1), custom_call_target="tpu_custom_call" | custom-call | flops 1 | bytes 1 | tf_op jit(solution)/shard_map/entry/pallas_call | solution.py:384
  76.9 10.0 fusion.15.refs_0_.refs_1_.refs_2_
  90.6 14.8 %stats.2 = f32[16,128]{1,0:T(8,128)} custom-call(f32[16,128]{1,0:T(8,128)} %reshape.215.refs_0_), custom_call_target="tpu_custom_call" | custom-call | flops 1 | bytes 1 | tf_op jit(solution)/shard_map/stats/pallas_call | solution.py:384
  114.1 16.4 %attend.1 = (bf16[1024,512]{1,0:T(8,128)(2,1)}, bf16[1024,512]{1,0:T(8,128)(2,1)}, bf16[1024,512]{1,0:T(8,128)(2,1)}, bf16[1024,512]{1,0:T(8,128)(2,1)}, f32[4,1024,1]{2,1,0:T(8,128)}) custom-call(f32[1024,1536]{1,0:T(8,128)} %copy-done, f32[1024,1536]{1,0:T(8,128)} %copy-done, f32[1024,1536]{1,0:T(8,128)} %copy-done, f32[1024,1]{1,0:T(8,128)} %copy.26.refs_3_, ...), custom_call_target="tpu_custom_call" | custom-call | flops 1073741824 | bytes 10485760 | tf_op jit(solution)/shard_map/attend/pallas_call | solution.py:1868
  130.5 53.4 %to_tokens.1 = (bf16[256,2048]{1,0:T(8,128)(2,1)}, bf16[8,256,1024]{2,1,0:T(8,128)(2,1)}) custom-call(bf16[4,256,512]{2,1,0:T(8,128)(2,1)} %bitcast.78, bf16[256,8192]{1,0:T(8,128)(2,1)} %refs_1_.6), custom_call_target="tpu_custom_call" | custom-call | flops 1 | bytes 1 | tf_op jit(solution)/shard_map/to_tokens/pallas_call | solution.py:384
  183.9 6.2 multiply_reduce_fusion.7
  191.8 93.3 %gather_hidden.1 = (bf16[8,256,2048]{2,1,0:T(8,128)(2,1)}, bf16[8,256,1024]{2,1,0:T(8,128)(2,1)}, bf16[8,256,1024]{2,1,0:T(8,128)(2,1)}, bf16[8,256,1024]{2,1,0:T(8,128)(2,1)}, bf16[8,256,1024]{2,1,0:T(8,128)(2,1)}) custom-call(bf16[256,2048]{1,0:T(8,128)(2,1)} %fusion.7.refs_0_, bf16[256,8192]{1,0:T(8,128)(2,1)} %refs_1_.7, bf16[2048,1024]{1,0:T(8,128)(2,1)} %bitcast.72), custom_call_target="tpu_custom_call" | custom-call | flops 1 | bytes 1 | tf_op jit(solution)/shard_map/gather_hidden/pallas_call | solution.py:384
  285.1 49.2 %out_scatter.1 = f32[256,2048]{1,0:T(8,128)} custom-call(bf16[8,256,1024]{2,1,0:T(8,128)(2,1)} %get-tuple-element.44.refs_0_, bf16[1024,2048]{1,0:T(8,128)(2,1)} %refs_1_.9), custom_call_target="tpu_custom_call" | custom-call | flops 1 | bytes 1 | tf_op jit(solution)/shard_map/out_scatter/pallas_call | solution.py:384
  338.9 52.0 %gather_hidden_grad.1 = (bf16[8,256,2048]{2,1,0:T(8,128)(2,1)}, bf16[8,256,1024]{2,1,0:T(8,128)(2,1)}, bf16[8,256,1024]{2,1,0:T(8,128)(2,1)}) custom-call(bf16[256,2048]{1,0:T(8,128)(2,1)} %fusion.3.refs_0_, bf16[1024,2048]{1,0:T(8,128)(2,1)} %refs_1_.9, bf16[8,256,1024]{2,1,0:T(8,128)(2,1)} %get-tuple-element.45.refs_2_, ...), custom_call_target="tpu_custom_call" | custom-call | flops 1 | bytes 1 | tf_op jit(solution)/shard_map/gather_hidden_grad/pallas_call | solution.py:384
  390.9 12.8 %bitcast_convert_fusion = bf16[1024,2048]{1,0:T(8,128)(2,1)} fusion(bf16[8,256,1024]{2,1,0:T(8,128)(2,1)S(1)} %copy-done.14, bf16[8,256,2048]{2,1,0:T(8,128)(2,1)} %get-tuple-element.56), kind=kOutput, calls=%fused_computation | convolution fusion | flops 8592031744 | bytes 16777216 | tf_op jit(solution)/shard_map/dot_general | solution.py:53
  403.8 14.1 %bitcast_convert_fusion.2.refs_4_.refs_3_ = bf16[2048,1024]{1,0:T(8,128)(2,1)} fusion(bf16[8,256,2048]{2,1,0:T(8,128)(2,1)} %get-tuple-element.50, bf16[8,256,1024]{2,1,0:T(8,128)(2,1)} %get-tuple-element.47.refs_0_), kind=kOutput, calls=%fused_computation.2 | convolution fusion | flops 8592031744 | bytes 16777216 | tf_op jit(solution)/shard_map/dot_general | solution.py:53
  417.9 13.0 %bitcast_convert_fusion.1.refs_5_.refs_4_ = bf16[2048,1024]{1,0:T(8,128)(2,1)} fusion(bf16[8,256,2048]{2,1,0:T(8,128)(2,1)} %get-tuple-element.50, bf16[8,256,1024]{2,1,0:T(8,128)(2,1)S(1)} %copy-done.15), kind=kOutput, calls=%fused_computation.1 | convolution fusion | flops 8592031744 | bytes 16777216 | tf_op jit(solution)/shard_map/dot_general | solution.py:53
  430.9 57.5 %back_scatter.1 = f32[256,2048]{1,0:T(8,128)} custom-call(bf16[8,256,1024]{2,1,0:T(8,128)(2,1)} %get-tuple-element.47.refs_0_, bf16[8,256,1024]{2,1,0:T(8,128)(2,1)} %get-tuple-element.48.refs_1_, bf16[2048,1024]{1,0:T(8,128)(2,1)} %bitcast.73, bf16[2048,1024]{1,0:T(8,128)(2,1)} %bitcast.77, bf16[2048,1024]{1,0:T(8,128)(2,1)} %bitcast_convert_fusion.2.refs_4_.refs_3_, ...), custom_call_target="tpu_custom_call" | custom-call | flops 1 | bytes 1 | tf_op jit(solution)/shard_map/back_scatter/pallas_call | solution.py:384
  494.3 6.7 convolution_convert_fusion.refs_0_
  501.1 45.7 %to_heads.1 = (bf16[4,256,512]{2,1,0:T(8,128)(2,1)}, f32[256,2048]{1,0:T(8,128)}) custom-call(bf16[256,2048]{1,0:T(8,128)(2,1)} %convolution_convert_fusion.refs_0_, bf16[256,2048]{1,0:T(8,128)(2,1)} %get-tuple-element.42.refs_1_, bf16[256,2048]{1,0:T(8,128)(2,1)} %copy-done.13), custom_call_target="tpu_custom_call" | custom-call | flops 1 | bytes 1 | tf_op jit(solution)/shard_map/to_heads/pallas_call | solution.py:384
  546.8 33.3 %all-reduce.2.cloned.1.call-done.refs_7_ = bf16[1024,2048]{1,0:T(8,128)(2,1)} async-done(((bf16[1024,2048]{1,0:T(8,128)(2,1)}), bf16[1024,2048]{1,0:T(8,128)(2,1)}) %all-reduce.2.cloned.1.call-update) | async-done | bytes 4194320 | tf_op jit(solution)/shard_map/psum | solution.py:2017
  580.1 16.7 %attend_back.1 = (f32[1024,512]{1,0:T(8,128)}, f32[1024,512]{1,0:T(8,128)}, bf16[1024,512]{1,0:T(8,128)(2,1)}) custom-call(bf16[1024,512]{1,0:T(8,128)(2,1)} %get-tuple-element.51.refs_0_, bf16[1024,512]{1,0:T(8,128)(2,1)} %get-tuple-element.52.refs_1_, bf16[1024,512]{1,0:T(8,128)(2,1)} %get-tuple-element.53.refs_2_, bf16[1024,512]{1,0:T(8,128)(2,1)} %bitcast.79, ...), custom_call_target="tpu_custom_call" | custom-call | flops 2684354560 | bytes 10485760 | tf_op jit(solution)/shard_map/attend_back/pallas_call | solution.py:1917
  603.3 5.1 stats.3
  614.2 3.4 subtract_convert_fusion.1
  621.9 375.2 %finish.1 = (f32[256,2048]{1,0:T(8,128)}, bf16[256,8192]{1,0:T(8,128)(2,1)}, bf16[256,8192]{1,0:T(8,128)(2,1)}, bf16[1024,2048]{1,0:T(8,128)(2,1)}, bf16[24,128,...) custom-call(bf16[1024,1536]{1,0:T(8,128)(2,1)} %pad_maximum_fusion.refs_0_, ...), custom_call_target="tpu_custom_call" | custom-call | flops 1 | bytes 1 | tf_op jit(solution)/shard_map/finish/pallas_call | solution.py:384
  997.8 6.1 slice_convert_fusion
  1008.2 4.4 convert_element_type.91
  1012.6 4.4 convert_element_type.92
  1016.9 4.4 convert_element_type.93
  (110 shorter events, 48.7 us)
Async XLA Ops:
  7.2 176.7 %all-gather.2.cloned.1.call-start = ((), (), s32[]{:S(2)}) async-start(), calls=%async_computation | async-start | bytes 9437184 | tf_op jit(solution)/shard_map/all_gather | solution.py:1968
  76.8 503.3 %all-reduce.2.cloned.1.call-start = ((), (), s32[]{:S(2)}) async-start(), calls=%async_computation.1 | async-start | bytes 8388608 | tf_op jit(solution)/shard_map/psum | solution.py:2017
  183.9 6.3 copy-start.8
  183.9 6.2 copy-start.18
  285.1 51.3 %copy-start.4 = (bf16[1,256,2048]{2,1,0:T(8,128)(2,1)S(1)}, bf16[1,256,2048]{2,1,0:T(8,128)(2,1)}, u32[]{:S(2)}) copy-start(bf16[1,256,2048]{2,1,0:T(8,128)(2,1)} %param.25) | copy-start | bytes 3145732
  285.1 51.3 %copy-start.19 = (f32[2048]{0:T(1024)S(1)}, f32[2048]{0:T(1024)}, u32[]{:S(2)}) copy-start(f32[2048]{0:T(1024)} %param.24) | copy-start | bytes 24580
  338.9 52.0 %copy-start.14 = (bf16[8,256,1024]{2,1,0:T(8,128)(2,1)S(1)}, bf16[8,256,1024]{2,1,0:T(8,128)(2,1)}, u32[]{:S(2)}) copy-start(bf16[8,256,1024]{2,1,0:T(8,128)(2,1)} %get-tuple-element.44.refs_0_) | copy-start | bytes 12582916
  403.8 14.1 %copy-start.15 = (bf16[8,256,1024]{2,1,0:T(8,128)(2,1)S(1)}, bf16[8,256,1024]{2,1,0:T(8,128)(2,1)}, u32[]{:S(2)}) copy-start(bf16[8,256,1024]{2,1,0:T(8,128)(2,1)} %get-tuple-element.48.refs_1_) | copy-start | bytes 12582916
  430.9 57.5 %copy-start.6 = (f32[256,2048]{1,0:T(8,128)S(1)}, f32[256,2048]{1,0:T(8,128)}, u32[]{:S(2)}) copy-start(f32[256,2048]{1,0:T(8,128)} %copy-done.5) | copy-start | bytes 6291460
  580.1 16.8 %slice-start = ((s8[6291456]{0:T(1024)(128)(4,1)}), s8[4194304]{0:T(1024)(128)(4,1)S(1)}, s32[]{:S(2)}) async-start(s8[6291456]{0:T(1024)(128)(4,1)} %bitcast.70), calls=%async_computation.2 | async-start | bytes 8388608
  580.1 16.8 %slice-start.1 = ((s8[6291456]{0:T(1024)(128)(4,1)}), s8[2097152]{0:T(1024)(128)(4,1)S(1)}, s32[]{:S(2)}) async-start(s8[6291456]{0:T(1024)(128)(4,1)} %bitcast.70), calls=%async_computation.3 | async-start | bytes 4194304
  580.1 16.8 %copy-start.21 = (f32[512]{0:T(512)S(1)}, f32[512]{0:T(512)}, u32[]{:S(2)}) copy-start(f32[512]{0:T(512)} %dynamic_slice.6) | copy-start | bytes 6148
  580.1 16.8 %copy-start.22 = (f32[512]{0:T(512)S(1)}, f32[512]{0:T(512)}, u32[]{:S(2)}) copy-start(f32[512]{0:T(512)} %dynamic_slice.7) | copy-start | bytes 6148
  599.8 10.3 %copy-start.20 = (f32[16,128]{1,0:T(8,128)S(1)}, f32[16,128]{1,0:T(8,128)}, u32[]{:S(2)}) copy-start(f32[16,128]{1,0:T(8,128)} %stats.2) | copy-start | bytes 24580
  599.8 14.3 %copy-start.10 = (f32[1024,512]{1,0:T(8,128)S(1)}, f32[1024,512]{1,0:T(8,128)}, u32[]{:S(2)}) copy-start(f32[1024,512]{1,0:T(8,128)} %get-tuple-element.57) | copy-start | bytes 6291460
  599.9 8.6 collective-permute-start
  608.5 4.0 collective-permute-start.1
  612.6 5.0 collective-permute-start.2
  614.1 5.7 copy-start.17
  617.5 379.5 %collective-permute-start.3 = (f32[4,2048]{1,0:T(4,128)S(1)}, f32[4,2048]{1,0:T(4,128)S(1)}, u32[]{:S(2)}, u32[]{:S(2)}) collective-permute-start(f32[4,2048]{1,0:T(4,128)S(1)} %add.100), channel_id=1, source_target_pairs={{0,8},{24,16},{1,9},{25,17},{2,10},{26,18},{3,11},{27,19},{4,12},{... | collective-permute-start | bytes 98312 | tf_op jit(solution)/shard_map/ppermute | solution.py:1937
  997.1 6.8 collective-permute-start.4
  997.8 7.4 copy-start.3
  997.8 7.4 copy-start.16
  1003.9 17.5 %collective-permute-start.5 = (f32[4,2048]{1,0:T(4,128)S(1)}, f32[4,2048]{1,0:T(4,128)S(1)}, u32[]{:S(2)}, u32[]{:S(2)}) collective-permute-start(f32[4,2048]{1,0:T(4,128)S(1)} %add.102), channel_id=1, source_target_pairs={{8,0},{16,24},{9,1},{17,25},{10,2},{18,26},{11,3},{19,27},{12,4},{... | collective-permute-start | bytes 98312 | tf_op jit(solution)/shard_map/ppermute | solution.py:1940
  (9 other events, 24.4 us)
Sparse Core Ops, SparseCore 0:
  76.9 65.7 all-gather.1
  403.9 176.1 all-reduce.1

commit v4 on v3

--- a/solution.py
+++ b/solution.py
@@ -332,7 +332,7 @@
 ANY = pl.BlockSpec(memory_space=pl.ANY)
 VM = pl.BlockSpec(memory_space=pltpu.VMEM)
 DMA = pltpu.SemaphoreType.DMA
-VMEM_LIMIT = 56 * 1024 * 1024
+VMEM_LIMIT = 60 * 1024 * 1024
 
 
 def flip(value, bit):
@@ -1246,6 +1246,8 @@
 
 LINE_ROWS = 128
 RING = 4
+CLOSE_LAG = 2
+TAKE_LAG = 5
 
 
 def flip_by(value, mask):
@@ -1448,12 +1450,12 @@
         self.add_up(self.sums.at[slot], self.sums.at[slot], self.own.at[lax.rem(index, 2)])
         self.swap(index).start()
         if isinstance(index, int):
-            self.close(index - 1)
+            self.close(index - CLOSE_LAG)
         else:
 
-            @pl.when(index > 0)
+            @pl.when(index >= CLOSE_LAG)
             def _():
-                self.close(index - 1)
+                self.close(index - CLOSE_LAG)
 
     def outer_take(self, index):
         self.outward(index).wait_recv()
@@ -1465,12 +1467,12 @@
             for copy in self.inward(index + 1):
                 copy.start()
         if isinstance(index, int):
-            self.outer_take(index - 3)
+            self.outer_take(index - TAKE_LAG)
         else:
 
-            @pl.when(index >= 3)
+            @pl.when(index >= TAKE_LAG)
             def _():
-                self.outer_take(index - 3)
+                self.outer_take(index - TAKE_LAG)
 
     def step(self, index, following=True):
         @pl.when(self.inner)
@@ -1495,7 +1497,8 @@
 
         @pl.when(self.inner)
         def _():
-            self.close(count - 1)
+            for index in range(count - CLOSE_LAG, count):
+                self.close(index)
             for index in range(count - RING, count):
                 self.swap(index).wait_send()
                 self.retire(index)
@@ -1509,7 +1512,7 @@
 
         @pl.when(self.outer)
         def _():
-            for index in range(count - 3, count):
+            for index in range(count - TAKE_LAG, count):
                 self.outer_take(index)
 
             def sent(index):
@@ -1532,17 +1535,69 @@
         each(received)
 
 
+class HeadLoads:
+    def __init__(self, sources, log_total, raw, low, logs, wide, sems):
+        self.sources, self.log_total, self.raw = sources, log_total, raw
+        self.low, self.logs, self.wide, self.sems = low, logs, wide, sems
+        self.size = low.shape[3]
+
+    def raws(self, head):
+        slot, size = lax.rem(head, 2), self.size
+        heads = self.raw.shape[1] // (3 * size)
+        return [
+            pltpu.make_async_copy(
+                self.raw.at[:, pl.ds(pl.multiple_of((part * heads + head) * size, size), size)],
+                self.wide.at[slot, part],
+                self.sems.at[slot, 5 + part],
+            )
+            for part in range(2)
+        ]
+
+    def lows(self, head):
+        slot, size = lax.rem(head, 2), self.size
+        at = pl.ds(pl.multiple_of(head * size, size), size)
+        copies = [
+            pltpu.make_async_copy(
+                source.at[:, at], self.low.at[slot, index], self.sems.at[slot, index]
+            )
+            for index, source in enumerate(self.sources)
+        ]
+        return copies + [
+            pltpu.make_async_copy(
+                self.log_total.at[head], self.logs.at[slot], self.sems.at[slot, 4]
+            )
+        ]
+
+
+def exact_nt(a, b):
+    return lax.dot_general(
+        a, b, (((1,), (1,)), ((), ())), preferred_element_type=jnp.float32,
+        precision=lax.Precision.HIGHEST,
+    )
+
+
+def exact_tn(a, b):
+    return lax.dot_general(
+        a, b, (((0,), (0,)), ((), ())), preferred_element_type=jnp.float32,
+        precision=lax.Precision.HIGHEST,
+    )
+
+
 def finish_kernel(
-    joined, weight, whole, gate, up, out_grad,
-    out, gate_rows, up_rows, line_out, first_chunks, second_chunks, total_chunks,
+    queries, keys, values, head_grad, log_total, raw, weight, cosine, signed, q_factor, k_factor,
+    q_gain, k_gain, token_gains, whole, gate, up, out_grad,
+    out, gains, gate_rows, up_rows, line_out, first_chunks, second_chunks, total_chunks,
+    low, logs, wide, q_turned, k_turned, k_sum, v_sum, joined, stat, stat_in, gain, gain_in,
     part, grads, placed,
-    mated, sums, landed, first_in, second_in, onward, total, swapped,
+    mated, landed, first_in, second_in, swapped,
+    head_sem, weight_sem, stat_s, stat_r, gain_s, gain_r,
     local, sem_s, sem_r, grad_s, grad_r, *line_scratch
 ):
     seq, shard = place()
     core, half, quarter = lax.rem(shard, 2), lax.div(seq, 2), lax.rem(seq, 2)
     chip = lax.div(shard, 2)
     base = shard - core
+    group = 2 * quarter + core
     rows = out.shape[0] // 2
     mate = (seq, flip(shard, 1))
     bit = 1 + core
@@ -1562,6 +1617,117 @@
     )
     line.begin()
 
+    length, size = cosine.shape
+    heads = q_gain.shape[1] // size
+    loads = HeadLoads(
+        (queries, keys, values, head_grad), log_total, raw, low, logs, wide, head_sem
+    )
+    for copy in loads.lows(0) + loads.raws(0):
+        copy.start()
+    blocks = grads.shape[1]
+    weight_loads = [
+        pltpu.make_async_copy(
+            weight.at[index * blocks : (index + 1) * blocks], grads.at[index],
+            weight_sem.at[index],
+        )
+        for index in range(4)
+    ]
+    for copy in weight_loads:
+        copy.start()
+    stat[...] = jnp.zeros_like(stat)
+    gain[...] = jnp.zeros_like(gain)
+    gain[2:4] = token_gains[...]
+    ones = jnp.ones((8, size), jnp.float32)
+
+    def columns(head):
+        return pl.ds(pl.multiple_of(head * size, size), size)
+
+    def back(head, carry):
+        slot, at = lax.rem(head, 2), columns(head)
+        for copy in loads.lows(head):
+            copy.wait()
+
+        @pl.when(head + 1 < heads)
+        def _():
+            for copy in loads.lows(head + 1) + loads.raws(head + 1):
+                copy.start()
+
+        attend_back_kernel(
+            low.at[slot, 0], low.at[slot, 1], low.at[slot, 2], low.at[slot, 3],
+            logs.at[pl.ds(slot, 1)], cosine, signed,
+            q_turned.at[:, at], k_turned.at[:, at],
+            joined.at[:, columns(2 * heads + head)],
+            k_sum, v_sum,
+        )
+        for copy in loads.raws(head):
+            copy.wait()
+        for index, (turned, factor, gain_part) in enumerate(
+            ((q_turned, q_factor, q_gain), (k_turned, k_factor, k_gain))
+        ):
+            along = turned[:, at].astype(jnp.float32) * wide[slot, index]
+            stat[8 * index : 8 * index + 8] += exact_nt(ones, along * gain_part[:, at])
+            spot = pl.multiple_of(group * heads * size + head * size, size)
+            gain[index : index + 1, pl.ds(spot, size)] = jnp.sum(
+                along * factor[...], axis=0, keepdims=True
+            )
+
+        @pl.when(lax.rem(head, 2) == 1)
+        def _():
+            line.step(lax.div(head, 2))
+
+        return carry
+
+    lax.fori_loop(0, heads, back, 0)
+    partners = [mate, (flip(seq, 1), shard), (flip(seq, 1), flip(shard, 1))]
+    stat_copies = [
+        remote(stat, stat_in.at[index], stat_s.at[index], stat_r.at[index], partner)
+        for index, partner in enumerate(partners)
+    ]
+    for copy in stat_copies:
+        copy.start()
+    own_gain = pltpu.make_async_copy(gain, gain_in.at[shard], gain_s.at[0])
+    own_gain.start()
+    gain_copies = [
+        remote(
+            gain, gain_in.at[shard], gain_s.at[mask], gain_r.at[mask],
+            (seq, flip_mask(shard, mask)),
+        )
+        for mask in range(1, 8)
+    ]
+    for copy in gain_copies:
+        copy.start()
+    for copy in loads.raws(0):
+        copy.start()
+    line.run(heads // 2, heads // 2 + 1)
+    for copy in stat_copies:
+        copy.wait()
+    stat[...] = (stat[...] + stat_in[0]) + (stat_in[1] + stat_in[2])
+    spreading = jnp.full((8, size), 0.125 / whole.shape[1], jnp.float32)
+
+    def norm_back(head, carry):
+        slot, at = lax.rem(head, 2), columns(head)
+        for copy in loads.raws(head):
+            copy.wait()
+
+        @pl.when(head + 1 < heads)
+        def _():
+            for copy in loads.raws(head + 1):
+                copy.start()
+
+        for index, (turned, factor, gain_part) in enumerate(
+            ((q_turned, q_factor, q_gain), (k_turned, k_factor, k_gain))
+        ):
+            inner = exact_tn(stat[8 * index : 8 * index + 8], spreading)
+            scale = factor[...]
+            joined[:, columns(index * heads + head)] = (
+                scale * (turned[:, at].astype(jnp.float32) * gain_part[:, at])
+                - wide[slot, index] * (scale * scale * scale * inner)
+            ).astype(jnp.bfloat16)
+        return carry
+
+    lax.fori_loop(0, heads, norm_back, 0)
+    line.run(heads // 2 + 1, heads // 2 + 2)
+
     mine = pl.ds(pl.multiple_of(core * rows, rows), rows)
     other = pl.ds(pl.multiple_of((1 - core) * rows, rows), rows)
     here = core == half
@@ -1576,6 +1742,23 @@
 
         tiles(grads.shape[2], tile)
 
+    for copy in weight_loads:
+        copy.wait()
+    swaps = []
+    for slot, block in enumerate(order):
+        tokens = pl.ds(pl.multiple_of(block * 2 * rows, 2 * rows), 2 * rows)
+
+        def tile(index, carry, block=block, tokens=tokens):
+            at = pl.ds(pl.multiple_of(index * blocks, blocks), blocks)
+            part[block, :, at] = dot_nt(joined[tokens], grads[index]).astype(jnp.bfloat16)
+            return carry
+
+        lax.fori_loop(0, 4, tile, 0)
+        copy = remote(
+            part.at[block, other], mated.at[slot], sem_s.at[0, slot], sem_r.at[0, slot], mate
+        )
+        copy.start()
+        swaps.append(copy)
     firsts = []
     for slot, target in ((0, diagonal), (1, first)):
         project(target)
@@ -1590,22 +1773,27 @@
             )
             copy.start()
             firsts.append(copy)
-    swaps = []
-    for slot, block in enumerate(order):
-        tokens = pl.ds(pl.multiple_of(block * 2 * rows, 2 * rows), 2 * rows)
-
-        def tile(at):
-            part[block, :, at] = dot_nt(joined[tokens], weight[at]).astype(jnp.bfloat16)
-
-        tiles(part.shape[2], tile)
-        copy = remote(
-            part.at[block, other], mated.at[slot], sem_s.at[0, slot], sem_r.at[0, slot], mate
-        )
-        copy.start()
-        swaps.append(copy)
-    line.run(0, 1)
+    line.run(4, 5)
     project(second)
     project(chip)
+    own_gain.wait()
+    for copy in gain_copies:
+        copy.wait()
+    plane_gain = gain_in[0]
+    for index in range(1, 8):
+        plane_gain = plane_gain + gain_in[index]
+    gain[...] = plane_gain
+    own_gain = pltpu.make_async_copy(gain, gain_in.at[8 + seq], gain_s.at[8])
+    own_gain.start()
+    gain_copies = [
+        remote(
+            gain, gain_in.at[8 + seq], gain_s.at[8 + step], gain_r.at[7 + step],
+            (lax.rem(seq + step, 4), shard),
+        )
+        for step in (1, 2, 3)
+    ]
+    for copy in gain_copies:
+        copy.start()
     placed[...] = jnp.zeros_like(placed)
 
     sends = []
@@ -1614,13 +1802,13 @@
 
         def add(span, slot=slot, block=block):
             source = pl.ds(pl.multiple_of(span.start + core * rows, 32), span.size)
-            sums[slot, span] = (
+            mated[slot, span] = (
                 part[block, source].astype(jnp.float32) + mated[slot, span].astype(jnp.float32)
             ).astype(jnp.bfloat16)
 
         add_rows(rows, add)
         copy = remote(
-            sums.at[slot],
+            mated.at[slot],
             landed.at[quarter, core],
             sem_s.at[1, slot],
             sem_r.at[1, 2 * quarter + core],
@@ -1629,7 +1817,7 @@
         if slot < 3:
             copy.start()
         else:
-            own = pltpu.make_async_copy(sums.at[slot], landed.at[quarter, core], local)
+            own = pltpu.make_async_copy(mated.at[slot], landed.at[quarter, core], local)
 
             @pl.when(here)
             def _():
@@ -1640,7 +1828,7 @@
                 copy.start()
 
         sends.append(copy)
-    line.run(1, 3)
+    line.run(5, 7)
 
     seconds = []
     for index in range(2):
@@ -1648,19 +1836,19 @@
 
         def add(span, index=index):
             span = pl.ds(span.start + index * long, span.size)
-            onward[span] = (
+            first_in[0, span] = (
                 grads[second, span].astype(jnp.float32) + first_in[0, span].astype(jnp.float32)
             ).astype(jnp.bfloat16)
 
         add_rows(long, add)
         span = slice(index * long, (index + 1) * long)
         copy = remote(
-            onward.at[span], second_in.at[span], grad_s.at[2, index], grad_r.at[2, index],
+            first_in.at[0, span], second_in.at[span], grad_s.at[2, index], grad_r.at[2, index],
             second_device,
         )
         copy.start()
         seconds.append(copy)
-    line.run(3, 6)
+    line.run(7, 10)
     for turn in range(2):
         start = pl.multiple_of((1 - core if turn == 0 else core) * long, long)
         if turn == 0:
@@ -1669,7 +1857,7 @@
 
         def add(span, start=start):
             span = pl.ds(pl.multiple_of(span.start + start, 32), span.size)
-            total[span] = (
+            first_in[1, span] = (
                 (grads[chip, span].astype(jnp.float32) + first_in[1, span].astype(jnp.float32))
                 + second_in[span].astype(jnp.float32)
             ).astype(jnp.bfloat16)
@@ -1677,16 +1865,15 @@
         add_rows(long, add)
         if turn == 0:
             swap = remote(
-                total.at[pl.ds(start, long)], swapped, grad_s.at[3, 0], grad_r.at[3, 0], mate
+                first_in.at[1, pl.ds(start, long)], swapped, grad_s.at[3, 0], grad_r.at[3, 0], mate
             )
             swap.start()
-    group = 2 * quarter + core
     part_width = out.shape[1] // 4
     own_rows = pl.ds(pl.multiple_of(core * long, long), long)
     for index in range(3):
         spot = pl.multiple_of(group * part_width, part_width)
-        placed[index, :, pl.ds(spot, part_width)] = total[
-            own_rows, index * part_width : (index + 1) * part_width
+        placed[index, :, pl.ds(spot, part_width)] = first_in[
+            1, own_rows, index * part_width : (index + 1) * part_width
         ]
     swap.wait_recv()
     for index in range(3):
@@ -1694,7 +1881,7 @@
         placed[index, :, pl.ds(spot, part_width)] = swapped[
             :, index * part_width : (index + 1) * part_width
         ]
-    line.run(6, 8)
+    line.run(10, 12)
 
     for slot in range(3):
         sends[slot].wait_send()
@@ -1709,7 +1896,7 @@
 
     for source in range(4):
         arrival = remote(
-            sums.at[0],
+            mated.at[0],
             landed.at[source // 2, source % 2],
             sem_s.at[1, 0],
             sem_r.at[1, source],
@@ -1731,14 +1918,22 @@
         add_rows(rows, add)
     for copy in swaps + firsts + seconds + [swap]:
         copy.wait_send()
-    line.run(8, line.early)
+    own_gain.wait()
+    for copy in gain_copies:
+        copy.wait()
+    gains[...] = (gain_in[8] + gain_in[9]) + (gain_in[10] + gain_in[11])
+    line.run(12, line.early)
     line.finish()
 
 
-def finish(joined, weight, whole, gate, up, out_grad, number, after=()):
+def finish(
+    heads_in, log_total, raw, weight, tables, factors, head_gains, token_gains, whole, gate, up,
+    out_grad, number, after=()
+):
     length, width = whole.shape
     rows, long, wide = length // 4, weight.shape[0] // 4, weight.shape[1]
-    low = joined.dtype
+    size, group_width = tables[0].shape[1], wide // 3
+    low = whole.dtype
     hidden_width = gate.shape[1]
     tail = out_grad.shape[0] + 3 * long // 2
     early, late = gate.shape[0] // LINE_ROWS, tail // LINE_ROWS
@@ -1750,6 +1945,7 @@
         finish_kernel,
         (
             jax.ShapeDtypeStruct((rows, width), jnp.float32),
+            jax.ShapeDtypeStruct((8, width), jnp.float32),
             owned,
             owned,
             jax.ShapeDtypeStruct((tail, width), low),
@@ -1757,21 +1953,37 @@
             chunks,
             chunks,
         ),
-        (joined, weight, whole, gate, up, out_grad),
-        [VM] * 3 + [ANY] * 3,
-        (VM,) + (ANY,) * 6,
+        (*heads_in, log_total, raw, weight, *tables, *factors, *head_gains, token_gains)
+        + (whole, gate, up, out_grad),
+        [ANY] * 7 + [VM] * 8 + [ANY] * 3,
+        (VM, VM) + (ANY,) * 6,
         [
+            pltpu.VMEM((2, 4, length, size), low),
+            pltpu.VMEM((2, length, 1), jnp.float32),
+            pltpu.VMEM((2, 2, length, size), jnp.float32),
+            pltpu.VMEM((length, group_width), low),
+            pltpu.VMEM((length, group_width), low),
+            pltpu.VMEM((length, size), jnp.float32),
+            pltpu.VMEM((length, size), jnp.float32),
+            pltpu.VMEM((length, wide), low),
+            pltpu.VMEM((16, length), jnp.float32),
+            pltpu.VMEM((3, 16, length), jnp.float32),
+            pltpu.VMEM((8, width), jnp.float32),
+            pltpu.VMEM((12, 8, width), jnp.float32),
             pltpu.VMEM((4, rows, width), low),
             pltpu.VMEM((4, long, wide), low),
             pltpu.VMEM((3, long // 2, width), low),
             pltpu.VMEM((4, rows // 2, width), low),
-            pltpu.VMEM((4, rows // 2, width), low),
             pltpu.VMEM((2, 2, rows // 2, width), low),
             pltpu.VMEM((2, long, wide), low),
             pltpu.VMEM((long, wide), low),
-            pltpu.VMEM((long, wide), low),
-            pltpu.VMEM((long, wide), low),
             pltpu.VMEM((long // 2, wide), low),
+            DMA((2, 7)),
+            DMA((4,)),
+            DMA((3,)),
+            DMA((3,)),
+            DMA((12,)),
+            DMA((11,)),
             DMA,
             DMA((2, 4)),
             DMA((2, 4)),
@@ -1793,7 +2005,7 @@
         number,
         after,
     )
-    return results[:4]
+    return results[:5]
 
 
 def turn_heads(values, cosine, signed):
@@ -1899,51 +2111,13 @@
         q_low = (dot_nn(score_grad, keys[:stop]) * scale).astype(jnp.bfloat16)
         q_grad[start:stop] = turn_heads(
             q_low.astype(jnp.float32), cosine[start:stop], -signed[start:stop]
-        )
+        ).astype(q_grad.dtype)
         k_sum[:stop] += dot_tn(score_grad, query)
     k_low = (k_sum[...] * scale).astype(jnp.bfloat16)
-    k_grad[...] = turn_heads(k_low.astype(jnp.float32), cosine[...], -signed[...])
+    k_grad[...] = turn_heads(k_low.astype(jnp.float32), cosine[...], -signed[...]).astype(
+        k_grad.dtype
+    )
     v_grad[...] = v_sum[...].astype(jnp.bfloat16)
-
-
-def attend_back(queries, keys, values, grads, log_total, cosine, signed, size, after=()):
-    length, width = queries.shape
-    heads = width // size
-    by_head = pl.BlockSpec((length, size), lambda h: (0, h))
-    fixed = pl.BlockSpec((length, size), lambda h: (0, 0))
-    wide = jax.ShapeDtypeStruct((length, width), jnp.float32)
-    flops = heads * length * length * size * 5
-    inputs = (queries, keys, values, grads, log_total, cosine, signed)
-    return pl.pallas_call(
-        ordered(attend_back_kernel, inputs, after),
-        grid=(heads,),
-        out_shape=(wide, wide, jax.ShapeDtypeStruct((length, width), jnp.bfloat16)),
-        in_specs=[by_head] * 4
-        + [pl.BlockSpec((1, length, 1), lambda h: (h, 0, 0))]
-        + [fixed] * 2
-        + [ANY] * len(after),
-        out_specs=[by_head] * 3,
-        scratch_shapes=[pltpu.VMEM((length, size), jnp.float32)] * 2,
-        name="attend_back",
-        compiler_params=pltpu.CompilerParams(vmem_limit_bytes=VMEM_LIMIT),
-        cost_estimate=pl.CostEstimate(
-            flops=flops, bytes_accessed=20 * length * width, transcendentals=flops // (10 * size)
-        ),
-    )(*inputs, *after)
-
-
-def line_total(part):
-    for route in ([(0, 1), (3, 2)], [(1, 2), (2, 1)]):
-        part = part + lax.ppermute(part, "seq", route)
-    seq = lax.axis_index("seq")
-    inner = jnp.logical_or(seq == 1, seq == 2)
-    return jnp.where(inner, part, lax.ppermute(part, "seq", [(1, 0), (2, 3)]))
-
-
-def gain_sums(part):
-    for mask in (1, 2, 4):
-        part = part + lax.ppermute(part, "fsdp", [(i, i ^ mask) for i in range(8)])
-    return line_total(part)
 
 
 def split_layer(
@@ -2035,20 +2209,21 @@
     attended_grad = times_transposed(branch_grad, out_full).astype(low)
     head_grad, out_grad = to_heads(attended_grad, attended, branch_grad, 8)
     head_grad, out_grad = head_grad.reshape(length, group_width), out_grad.astype(low)
-    q_norm_grad, k_norm_grad, value_grad = attend_back(
-        queries, keys, values, head_grad, log_total, cosine, signed, head_size, (down_sum,)
-    )
-    q_scaled, k_scaled = q_norm_grad * q_gain_part, k_norm_grad * k_gain_part
-    q_inner, k_inner = reduced(
-        jnp.sum(q_scaled * q_raw, axis=-1), jnp.sum(k_scaled * k_raw, axis=-1), 9
-    )
-    q_gain_sum = jnp.sum(q_norm_grad * q_raw * q_factor, axis=0)
-    k_gain_sum = jnp.sum(k_norm_grad * k_raw * k_factor, axis=0)
-    q_raw_grad = (q_factor * q_scaled - q_raw * (q_factor * q_factor * q_factor * q_inner)).astype(low)
-    k_raw_grad = (k_factor * k_scaled - k_raw * (k_factor * k_factor * k_factor * k_inner)).astype(low)
-    joined = jnp.concatenate([q_raw_grad, k_raw_grad, value_grad], axis=1)
-    input_sum, gate_rows, up_rows, late = finish(
-        joined, qkv, whole, gate_sum, up_sum, out_grad, 10
+    input_sum, gain_totals, gate_rows, up_rows, late = finish(
+        (queries, keys, values, head_grad),
+        log_total,
+        raw,
+        qkv,
+        (cosine, signed),
+        (q_factor, k_factor),
+        (q_gain_part, k_gain_part),
+        jnp.stack([attention_gain_grad, swiglu_gain_grad]),
+        whole,
+        gate_sum,
+        up_sum,
+        out_grad,
+        10,
+        (down_sum,),
     )
     input_grad = residual_grad + input_sum
 
@@ -2058,14 +2233,6 @@
         late[index * rows : (index + 1) * rows].astype(jnp.float32) for index in range(4)
     )
 
-    def widen(part):
-        return lax.dynamic_update_slice(
-            jnp.zeros((width,), jnp.float32), part, (group * group_width,)
-        )
-
-    gain_totals = gain_sums(
-        jnp.stack([widen(q_gain_sum), widen(k_gain_sum), attention_gain_grad, swiglu_gain_grad])
-    )
     return (
         output.reshape(1, tokens, width),
         input_grad.reshape(1, tokens, width),

time: 1040 us -> 991 us (0.953)
  Pallas kernels: 849 us -> 821 us
    pallas_call x1 -> x0, Pallas kernels: 16.7 us -> none  [attend_back(): pl.pallas_call(ordered(attend_back_kernel, inputs, after), grid=(heads,),...]
    pallas_call x10 -> x9, Pallas kernels: 814 us -> 803 us  [comm_call(): pl.pallas_call(ordered(kernel, inputs, after), out_shape=out_shape, in_sp...]
  transfers between devices with their start and end apart: 8 -> 2, of which waited for: 2 -> 1; matrix products, arithmetic and copies ran while one was open for 9% -> 6% of each run, Pallas kernels for 55% -> 19%
where the time goes in v4:
time: 991 us; the launch traced here: 980 us
  Pallas kernels  821 us (83%)
  matrix products  64.2 us (6%)
  other arithmetic  39.9 us (4%)
  waiting for transfers between devices  28.7 us (3%)
  between operations  14.8 us (1%)
  local copies, waits for them, and re-layouts  11.2 us (1%)
    pallas_call x9, Pallas kernels, comm_call(): pl.pallas_call(ordered(kernel, inputs, after), out_shape=out_shape, in_sp...  803 us
    dot_general x3, matrix products, transposed_times(): lax.dot_general(operand, matrix, (((0,), (0,)), ((), ())), preferred_elem...  41.2 us
    psum x1, waiting for transfers between devices, split_layer(): down_sum = lax.psum(down_grad, 'seq')  28.7 us
  transfers between devices with their start and end apart: 2, of which 1 were waited for; matrix products, arithmetic and copies ran while one was open for 6% of the time, Pallas kernels for 19%

profile of v4, /device:TPU:0, one launch (start us, length us, event | category | flops | bytes accessed | tf_op | source)
XLA Modules:
  0.0 980.1 jit_solution(13458664947774854985)
XLA Ops:
  7.2 67.3 %entry.1 = (bf16[4,256,2048]{2,1,0:T(8,128)(2,1)}, bf16[2048,1536]{1,0:T(8,128)(2,1)}) custom-call(bf16[256,2048]{1,0:T(8,128)(2,1)} %bitcast.58, bf16[256,2048]{1,0:T(8,128)(2,1)} %refs_1_.5, bf16[256,2048]{1,0:T(8,128)(2,1)} %refs_2_.1, bf16[256,2048]{1,0:T(8,128)(2,1)} %refs_3_.1), custom_call_target="tpu_custom_call" | custom-call | flops 1 | bytes 1 | tf_op jit(solution)/shard_map/entry/pallas_call | solution.py:384
  76.9 10.0 %fusion.12.refs_0_.refs_1_.refs_2_.refs_5_ = f32[1024,1536]{1,0:T(8,128)S(1)} fusion(bf16[1024,2048]{1,0:T(8,128)(2,1)} %bitcast.59, bf16[2048,1536]{1,0:T(8,128)(2,1)} %get-tuple-element.38.refs_1_.refs_6_), kind=kOutput, calls=%fused_computation.47 | convolution fusion | flops 6442450944 | bytes 16777216 | tf_op jit(solution)/shard_map/dot_general | solution.py:2027
  90.6 14.8 %stats.1 = f32[16,128]{1,0:T(8,128)} custom-call(f32[16,128]{1,0:T(8,128)} %reshape.153.refs_0_), custom_call_target="tpu_custom_call" | custom-call | flops 1 | bytes 1 | tf_op jit(solution)/shard_map/stats/pallas_call | solution.py:384
  114.1 16.4 %attend.1 = (bf16[1024,512]{1,0:T(8,128)(2,1)}, bf16[1024,512]{1,0:T(8,128)(2,1)}, bf16[1024,512]{1,0:T(8,128)(2,1)}, bf16[1024,512]{1,0:T(8,128)(2,1)}, f32[4,1024,1]{2,1,0:T(8,128)}) custom-call(f32[1024,1536]{1,0:T(8,128)} %copy-done, f32[1024,1536]{1,0:T(8,128)} %copy-done, f32[1024,1536]{1,0:T(8,128)} %copy-done, f32[1024,1]{1,0:T(8,128)} %copy.29.refs_3_.refs_9_, ...), custom_call_target="tpu_custom_call" | custom-call | flops 1073741824 | bytes 10485760 | tf_op jit(solution)/shard_map/attend/pallas_call | solution.py:2080
  130.5 53.4 %to_tokens.1 = (bf16[256,2048]{1,0:T(8,128)(2,1)}, bf16[8,256,1024]{2,1,0:T(8,128)(2,1)}) custom-call(bf16[4,256,512]{2,1,0:T(8,128)(2,1)} %bitcast.63, bf16[256,8192]{1,0:T(8,128)(2,1)} %refs_1_.6), custom_call_target="tpu_custom_call" | custom-call | flops 1 | bytes 1 | tf_op jit(solution)/shard_map/to_tokens/pallas_call | solution.py:384
  183.9 6.2 multiply_reduce_fusion.3
  191.8 93.3 %gather_hidden.1 = (bf16[8,256,2048]{2,1,0:T(8,128)(2,1)}, bf16[8,256,1024]{2,1,0:T(8,128)(2,1)}, bf16[8,256,1024]{2,1,0:T(8,128)(2,1)}, bf16[8,256,1024]{2,1,0:T(8,128)(2,1)}, bf16[8,256,1024]{2,1,0:T(8,128)(2,1)}) custom-call(bf16[256,2048]{1,0:T(8,128)(2,1)} %fusion.9.refs_0_, bf16[256,8192]{1,0:T(8,128)(2,1)} %refs_1_.7, bf16[2048,1024]{1,0:T(8,128)(2,1)} %bitcast.56), custom_call_target="tpu_custom_call" | custom-call | flops 1 | bytes 1 | tf_op jit(solution)/shard_map/gather_hidden/pallas_call | solution.py:384
  285.1 49.3 %out_scatter.1 = f32[256,2048]{1,0:T(8,128)} custom-call(bf16[8,256,1024]{2,1,0:T(8,128)(2,1)} %get-tuple-element.42.refs_0_, bf16[1024,2048]{1,0:T(8,128)(2,1)} %refs_1_.9), custom_call_target="tpu_custom_call" | custom-call | flops 1 | bytes 1 | tf_op jit(solution)/shard_map/out_scatter/pallas_call | solution.py:384
  338.9 51.9 %gather_hidden_grad.1 = (bf16[8,256,2048]{2,1,0:T(8,128)(2,1)}, bf16[8,256,1024]{2,1,0:T(8,128)(2,1)}, bf16[8,256,1024]{2,1,0:T(8,128)(2,1)}) custom-call(bf16[256,2048]{1,0:T(8,128)(2,1)} %fusion.3.refs_0_, bf16[1024,2048]{1,0:T(8,128)(2,1)} %refs_1_.9, bf16[8,256,1024]{2,1,0:T(8,128)(2,1)} %get-tuple-element.43.refs_2_, ...), custom_call_target="tpu_custom_call" | custom-call | flops 1 | bytes 1 | tf_op jit(solution)/shard_map/gather_hidden_grad/pallas_call | solution.py:384
  390.8 14.1 %bitcast_convert_fusion = bf16[1024,2048]{1,0:T(8,128)(2,1)} fusion(bf16[8,256,1024]{2,1,0:T(8,128)(2,1)} %get-tuple-element.42.refs_0_, bf16[8,256,2048]{2,1,0:T(8,128)(2,1)} %get-tuple-element.55), kind=kOutput, calls=%fused_computation | convolution fusion | flops 8592031744 | bytes 16777216 | tf_op jit(solution)/shard_map/dot_general | solution.py:53
  405.0 14.1 %bitcast_convert_fusion.2.refs_4_.refs_15_ = bf16[2048,1024]{1,0:T(8,128)(2,1)} fusion(bf16[8,256,2048]{2,1,0:T(8,128)(2,1)} %get-tuple-element.48, bf16[8,256,1024]{2,1,0:T(8,128)(2,1)} %get-tuple-element.45.refs_0_), kind=kOutput, calls=%fused_computation.2 | convolution fusion | flops 8592031744 | bytes 16777216 | tf_op jit(solution)/shard_map/dot_general | solution.py:53
  419.1 13.0 %bitcast_convert_fusion.1.refs_5_.refs_16_ = bf16[2048,1024]{1,0:T(8,128)(2,1)} fusion(bf16[8,256,2048]{2,1,0:T(8,128)(2,1)} %get-tuple-element.48, bf16[8,256,1024]{2,1,0:T(8,128)(2,1)S(1)} %copy-done.14), kind=kOutput, calls=%fused_computation.1 | convolution fusion | flops 8592031744 | bytes 16777216 | tf_op jit(solution)/shard_map/dot_general | solution.py:53
  432.1 57.4 %back_scatter.1 = f32[256,2048]{1,0:T(8,128)} custom-call(bf16[8,256,1024]{2,1,0:T(8,128)(2,1)} %get-tuple-element.45.refs_0_, bf16[8,256,1024]{2,1,0:T(8,128)(2,1)} %get-tuple-element.46.refs_1_, bf16[2048,1024]{1,0:T(8,128)(2,1)} %bitcast.57, bf16[2048,1024]{1,0:T(8,128)(2,1)} %bitcast.61, bf16[2048,1024]{1,0:T(8,128)(2,1)} %bitcast_convert_fusion.2.refs_4_.refs_15_, ...), custom_call_target="tpu_custom_call" | custom-call | flops 1 | bytes 1 | tf_op jit(solution)/shard_map/back_scatter/pallas_call | solution.py:384
  489.5 3.1 multiply_reduce_fusion
  496.7 6.8 convolution_convert_fusion.refs_0_
  503.5 45.8 %to_heads.1 = (bf16[4,256,512]{2,1,0:T(8,128)(2,1)}, f32[256,2048]{1,0:T(8,128)}) custom-call(bf16[256,2048]{1,0:T(8,128)(2,1)} %convolution_convert_fusion.refs_0_, bf16[256,2048]{1,0:T(8,128)(2,1)} %get-tuple-element.40.refs_1_, bf16[256,2048]{1,0:T(8,128)(2,1)} %copy-done.13), custom_call_target="tpu_custom_call" | custom-call | flops 1 | bytes 1 | tf_op jit(solution)/shard_map/to_heads/pallas_call | solution.py:384
  549.2 2.7 convert_element_type.77.refs_17_
  552.6 28.7 %all-reduce.2.cloned.1.call-done.refs_18_ = bf16[1024,2048]{1,0:T(8,128)(2,1)} async-done(((bf16[1024,2048]{1,0:T(8,128)(2,1)}), bf16[1024,2048]{1,0:T(8,128)(2,1)}) %all-reduce.2.cloned.1.call-update) | async-done | bytes 4194320 | tf_op jit(solution)/shard_map/psum | solution.py:2191
  581.2 369.5 %finish.1 = (f32[256,2048]{1,0:T(8,128)}, f32[8,2048]{1,0:T(8,128)}, bf16[256,8192]{1,0:T(8,128)(2,1)}, bf16[256,8192]{1,0:T(8,128)(2,1)}, bf16[1024,2048]{1,0:T...) custom-call(bf16[1024,512]{1,0:T(8,128)(2,1)} %get-tuple-element.49.ref, ...), custom_call_target="tpu_custom_call" | custom-call | flops 1 | bytes 1 | tf_op jit(solution)/shard_map/finish/pallas_call | solution.py:384
  950.8 3.5 add_bitcast_fusion
  954.3 4.1 slice_convert_fusion
  958.9 4.4 convert_element_type.83
  963.3 4.4 convert_element_type.84
  968.3 4.4 convert_element_type.85
  (65 shorter events, 26.7 us)
Async XLA Ops:
  7.2 176.7 %all-gather.2.cloned.1.call-start = ((), (), s32[]{:S(2)}) async-start(), calls=%async_computation | async-start | bytes 9437184 | tf_op jit(solution)/shard_map/all_gather | solution.py:2142
  76.8 504.4 %all-reduce.2.cloned.1.call-start = ((), (), s32[]{:S(2)}) async-start(), calls=%async_computation.1 | async-start | bytes 8388608 | tf_op jit(solution)/shard_map/psum | solution.py:2191
  86.9 2.7 copy-start
  183.9 6.3 copy-start.8
  183.9 6.2 copy-start.15
  190.1 1.7 copy-start.5
  285.1 51.3 %copy-start.4 = (bf16[1,256,2048]{2,1,0:T(8,128)(2,1)S(1)}, bf16[1,256,2048]{2,1,0:T(8,128)(2,1)}, u32[]{:S(2)}) copy-start(bf16[1,256,2048]{2,1,0:T(8,128)(2,1)} %param.25) | copy-start | bytes 3145732
  285.1 51.3 %copy-start.16 = (f32[2048]{0:T(1024)S(1)}, f32[2048]{0:T(1024)}, u32[]{:S(2)}) copy-start(f32[2048]{0:T(1024)} %param.24) | copy-start | bytes 24580
  334.4 2.2 copy-start.1
  404.9 14.1 %copy-start.14 = (bf16[8,256,1024]{2,1,0:T(8,128)(2,1)S(1)}, bf16[8,256,1024]{2,1,0:T(8,128)(2,1)}, u32[]{:S(2)}) copy-start(bf16[8,256,1024]{2,1,0:T(8,128)(2,1)} %get-tuple-element.46.refs_1_) | copy-start | bytes 12582916
  489.5 3.2 copy-start.2
  489.5 3.6 copy-start.6
  489.5 3.9 copy-start.9
  495.7 1.0 copy-start.13
  581.2 369.5 %copy-start.3 = (f32[256,2048]{1,0:T(8,128)S(1)}, f32[256,2048]{1,0:T(8,128)}, u32[]{:S(2)}) copy-start(f32[256,2048]{1,0:T(8,128)} %back_scatter.1) | copy-start | bytes 6291460
  950.8 3.5 copy-start.12
  954.3 4.6 copy-start.11
  958.9 4.4 copy-start.10
  963.3 4.4 copy-start.17
  963.3 5.0 copy-start.7
Sparse Core Ops, SparseCore 0:
  76.9 65.7 all-gather.1
  405.1 176.1 all-reduce.1

commit v5 on v4

--- a/solution.py
+++ b/solution.py
@@ -395,37 +395,9 @@
     )(*inputs, *after)
 
 
-def keep_kernel(x, out):
-    out[...] = x[...]
-
-
-def hold_kernel(x, out):
-    pass
-
-
-def hold(x, after):
-    return pl.pallas_call(
-        ordered(hold_kernel, (x,), after),
-        out_shape=jax.ShapeDtypeStruct(x.shape, x.dtype),
-        in_specs=[ANY] * (1 + len(after)),
-        out_specs=ANY,
-        input_output_aliases={0: 0},
-        name="hold",
-    )(x, *after)
-
-
-def keep(x, after):
-    return pl.pallas_call(
-        ordered(keep_kernel, (x,), after),
-        out_shape=jax.ShapeDtypeStruct(x.shape, x.dtype),
-        in_specs=[VM] + [ANY] * len(after),
-        out_specs=VM,
-        name="keep",
-    )(x, *after)
-
-
 def entry_kernel(
-    x, wq, wk, wv, xo, wo, local, x_send, x_recv, fwd_send, w_send, w_recv
+    x, wq, wk, wv, out_weight, xo, wo, out_kept,
+    local, x_send, x_recv, fwd_send, w_send, w_recv
 ):
     seq, shard = place()
     core, half = lax.rem(shard, 2), lax.div(seq, 2)
@@ -445,12 +417,16 @@
         group = 2 * quarter + lax.rem(target, 2)
         return weights[index].at[:, pl.ds(pl.multiple_of(group * width, width), width)]
 
+    near = 1 + core
     x_copies = []
     for which in (0, 1):
         target = 2 * core + which
+        wanted = jnp.logical_and(
+            target != seq, jnp.logical_or(core == half, target == near)
+        )
         copy = remote(x, xo.at[seq], x_send.at[which], x_recv.at[seq], (target, shard))
 
-        @pl.when(target != seq)
+        @pl.when(wanted)
         def _():
             copy.start()
 
@@ -458,7 +434,9 @@
         def _():
             pltpu.make_async_copy(x, xo.at[seq], local.at[3]).start()
 
-        x_copies.append((target, copy))
+        x_copies.append((wanted, copy))
+    kept = pltpu.make_async_copy(out_weight, out_kept, local.at[4])
+    kept.start()
     copies = []
     for index in range(3):
         for mask in (2, 4, 3, 5, 1):
@@ -480,11 +458,20 @@
         copy.start()
 
     mate = (seq, flip(shard, 1))
-    for turn in range(4):
-        source = lax.rem(seq + turn, 4)
+    relays = []
+    places = (seq, flip(seq, 1), 2 * (1 - half) + half, 2 * (1 - half) + 1 - half)
+
+    def pass_input(turn):
+        source = places[turn]
         forward = remote(
             xo.at[source], xo.at[source], fwd_send.at[turn], x_recv.at[source], mate
         )
+        if turn > 1:
+            relay = remote(
+                xo.at[source], xo.at[source], fwd_send.at[turn + 2], x_recv.at[source],
+                (flip(seq, 1), shard),
+            )
+            relays.append(relay)
 
         @pl.when(core == half)
         def _():
@@ -492,21 +479,13 @@
                 pltpu.make_async_copy(x, xo.at[seq], local.at[3]).wait()
             else:
                 forward.wait_recv()
+            if turn > 1:
+
+                @pl.when(seq == near)
+                def _():
+                    relay.start()
+
             forward.start()
-
-    for turn in range(4):
-        source = lax.rem(seq + turn, 4)
-        forward = remote(
-            xo.at[source], xo.at[source], fwd_send.at[turn], x_recv.at[source], mate
-        )
-
-        @pl.when(core == half)
-        def _():
-            forward.wait_send()
-
-        @pl.when(core != half)
-        def _():
-            forward.wait_recv()
 
     def arrival(index, origin, mask):
         spot = wo.at[pl.ds(pl.multiple_of(origin * rows, rows), rows), columns(index)]
@@ -516,6 +495,7 @@
     side, above = flip(base, 2), flip(base, 4)
     onward = []
     for index in range(3):
+        pass_input(index)
         for origin, mask, slot, target in (
             (side, 2 + core, 6 + core, flip(shard, 4)),
             (above + 1, 5 - core, 7 - core, flip(shard, 2)),
@@ -531,9 +511,30 @@
             )
             copy.start()
             onward.append(copy)
-    for target, copy in x_copies:
-
-        @pl.when(target != seq)
+    pass_input(3)
+    for relay in relays:
+
+        @pl.when(jnp.logical_and(core == half, seq == near))
+        def _():
+            relay.wait_send()
+
+    for turn, source in enumerate(places):
+        forward = remote(
+            xo.at[source], xo.at[source], fwd_send.at[turn], x_recv.at[source], mate
+        )
+
+        @pl.when(core == half)
+        def _():
+            forward.wait_send()
+
+        @pl.when(core != half)
+        def _():
+            forward.wait_recv()
+
+    kept.wait()
+    for wanted, copy in x_copies:
+
+        @pl.when(wanted)
         def _():
             copy.wait_send()
 
@@ -550,7 +551,7 @@
         arrival(index, far + 1, 7 - core).wait_recv()
 
 
-def entry(x, wq, wk, wv, number):
+def entry(x, wq, wk, wv, out_weight, number):
     rows, width = wq.shape
     group = width // 4
     return comm_call(
@@ -558,11 +559,12 @@
         (
             jax.ShapeDtypeStruct((4,) + x.shape, x.dtype),
             jax.ShapeDtypeStruct((8 * rows, 3 * group), wq.dtype),
+            jax.ShapeDtypeStruct(out_weight.shape, out_weight.dtype),
         ),
-        (x, wq, wk, wv),
-        [ANY] * 4,
-        (ANY, ANY),
-        [DMA((4,)), DMA((2,)), DMA((4,)), DMA((4,)), DMA((3, 7)), DMA((3, 7))],
+        (x, wq, wk, wv, out_weight),
+        [VM] * 5,
+        (ANY,) * 3,
+        [DMA((5,)), DMA((2,)), DMA((4,)), DMA((6,)), DMA((3, 7)), DMA((3, 7))],
         "entry",
         number,
     )
@@ -1589,9 +1591,9 @@
     out, gains, gate_rows, up_rows, line_out, first_chunks, second_chunks, total_chunks,
     low, logs, wide, q_turned, k_turned, k_sum, v_sum, joined, stat, stat_in, gain, gain_in,
     part, grads, placed,
-    mated, landed, first_in, second_in, swapped,
+    mated, relayed, landed, first_in, second_in, swapped,
     head_sem, weight_sem, stat_s, stat_r, gain_s, gain_r,
-    local, sem_s, sem_r, grad_s, grad_r, *line_scratch
+    local, sem_s, sem_r, relay_r, grad_s, grad_r, *line_scratch
 ):
     seq, shard = place()
     core, half, quarter = lax.rem(shard, 2), lax.div(seq, 2), lax.rem(seq, 2)
@@ -1731,7 +1733,7 @@
     mine = pl.ds(pl.multiple_of(core * rows, rows), rows)
     other = pl.ds(pl.multiple_of((1 - core) * rows, rows), rows)
     here = core == half
-    order = [2 * (1 - half) + 1 - quarter, 2 * (1 - half) + quarter, flip(seq, 1), seq]
+    order = [2 * (1 - half), 2 * (1 - half) + 1, flip(seq, 1), seq]
     long = grads.shape[1] // 2
 
     def project(target):
@@ -1796,7 +1798,25 @@
         copy.start()
     placed[...] = jnp.zeros_like(placed)
 
+    near = quarter + half == 1
+    far = jnp.logical_not(near)
     sends = []
+
+    def to_target(slot, block):
+        return remote(
+            mated.at[slot],
+            landed.at[quarter, core],
+            sem_s.at[1, slot],
+            sem_r.at[1, 2 * quarter + core],
+            (block, base + half),
+        )
+
+    def to_near(slot):
+        return remote(
+            mated.at[slot], relayed.at[slot], sem_s.at[1, slot], relay_r.at[slot],
+            (flip(seq, 1), shard),
+        )
+
     for slot, block in enumerate(order):
         swaps[slot].wait_recv()
 
@@ -1807,14 +1827,14 @@
             ).astype(jnp.bfloat16)
 
         add_rows(rows, add)
-        copy = remote(
-            mated.at[slot],
-            landed.at[quarter, core],
-            sem_s.at[1, slot],
-            sem_r.at[1, 2 * quarter + core],
-            (block, base + half),
-        )
-        if slot < 3:
+        copy = to_target(slot, block)
+        if slot < 2:
+
+            @pl.when(far)
+            def _():
+                to_near(slot).start()
+
+        elif slot == 2:
             copy.start()
         else:
             own = pltpu.make_async_copy(mated.at[slot], landed.at[quarter, core], local)
@@ -1828,6 +1848,21 @@
                 copy.start()
 
         sends.append(copy)
+
+    @pl.when(near)
+    def _():
+        for slot in range(2):
+            to_near(slot).wait_recv()
+
+            def add(span, slot=slot):
+                mated[slot, span] = (
+                    mated[slot, span].astype(jnp.float32)
+                    + relayed[slot, span].astype(jnp.float32)
+                ).astype(jnp.bfloat16)
+
+            add_rows(rows, add)
+            sends[slot].start()
+
     line.run(5, 7)
 
     seconds = []
@@ -1883,8 +1918,17 @@
         ]
     line.run(10, 12)
 
-    for slot in range(3):
-        sends[slot].wait_send()
+    for slot in range(2):
+
+        @pl.when(near)
+        def _():
+            sends[slot].wait_send()
+
+        @pl.when(far)
+        def _():
+            to_near(slot).wait_send()
+
+    sends[2].wait_send()
 
     @pl.when(here)
     def _():
@@ -1902,20 +1946,32 @@
             sem_r.at[1, source],
             mate,
         )
-
-        @pl.when(jnp.logical_not(jnp.logical_and(here, 2 * quarter + core == source)))
+        expected = jnp.where(here, 2 * quarter + core != source, source // 2 == 1 - core)
+
+        @pl.when(expected)
         def _():
             arrival.wait_recv()
 
     for side in range(2):
 
-        def add(span, side=side):
+        def add_both(span, side=side):
             target = pl.ds(span.start + side * rows, span.size)
             out[target] = landed[0, side, span].astype(jnp.float32) + landed[
                 1, side, span
             ].astype(jnp.float32)
 
-        add_rows(rows, add)
+        def take_one(span, side=side):
+            target = pl.ds(span.start + side * rows, span.size)
+            out[target] = landed[1 - core, side, span].astype(jnp.float32)
+
+        @pl.when(here)
+        def _():
+            add_rows(rows, add_both)
+
+        @pl.when(jnp.logical_not(here))
+        def _():
+            add_rows(rows, take_one)
+
     for copy in swaps + firsts + seconds + [swap]:
         copy.wait_send()
     own_gain.wait()
@@ -1974,6 +2030,7 @@
             pltpu.VMEM((4, long, wide), low),
             pltpu.VMEM((3, long // 2, width), low),
             pltpu.VMEM((4, rows // 2, width), low),
+            pltpu.VMEM((2, rows // 2, width), low),
             pltpu.VMEM((2, 2, rows // 2, width), low),
             pltpu.VMEM((2, long, wide), low),
             pltpu.VMEM((long, wide), low),
@@ -1987,6 +2044,7 @@
             DMA,
             DMA((2, 4)),
             DMA((2, 4)),
+            DMA((2,)),
             DMA((4, 2)),
             DMA((4, 2)),
             pltpu.VMEM((2,) + block, low),
@@ -2137,11 +2195,11 @@
     low = jnp.bfloat16
     sequence = block_input.reshape(tokens, width)
 
-    whole, qkv = entry(sequence, query_weight, key_weight, value_weight, 1)
+    whole, qkv, out_rows = entry(
+        sequence, query_weight, key_weight, value_weight, out_weight, 1
+    )
     whole = whole.reshape(length, width)
-    out_full = lax.all_gather(
-        keep(out_weight, (qkv,)), "fsdp", axis=0, tiled=True
-    )
+    out_full = lax.all_gather(out_rows, "fsdp", axis=0, tiled=True)
     raw = dot_nn(whole, qkv)
     q_raw, k_raw = raw[:, :group_width], raw[:, group_width : 2 * group_width]
 

time: 991 us -> 970 us (0.979)
  Pallas kernels: 821 us -> 800 us
    pallas_call x9, Pallas kernels: 803 us -> 783 us  [comm_call(): pl.pallas_call(ordered(kernel, inputs, after), out_shape=out_shape, in_sp...]
  transfers between devices with their start and end apart: 2 -> 2, of which waited for: 1 -> 1; matrix products, arithmetic and copies ran while one was open for 6% -> 7% of each run, Pallas kernels for 19% -> 19%
where the time goes in v5:
time: 970 us; the launch traced here: 959 us
  Pallas kernels  800 us (82%)
  matrix products  64.2 us (7%)
  other arithmetic  39.9 us (4%)
  waiting for transfers between devices  28.8 us (3%)
  between operations  14.8 us (2%)
  local copies, waits for them, and re-layouts  11.2 us (1%)
    pallas_call x9, Pallas kernels, comm_call(): pl.pallas_call(ordered(kernel, inputs, after), out_shape=out_shape, in_sp...  783 us
    dot_general x3, matrix products, transposed_times(): lax.dot_general(operand, matrix, (((0,), (0,)), ((), ())), preferred_elem...  41.2 us
    psum x1, waiting for transfers between devices, split_layer(): down_sum = lax.psum(down_grad, 'seq')  28.7 us
  transfers between devices with their start and end apart: 2, of which 1 were waited for; matrix products, arithmetic and copies ran while one was open for 7% of the time, Pallas kernels for 19%

profile of v5, /device:TPU:0, one launch (start us, length us, event | category | flops | bytes accessed | tf_op | source)
XLA Modules:
  0.0 958.5 jit_solution(9386654426688586478)
XLA Ops:
  7.2 60.7 %entry.1 = (bf16[4,256,2048]{2,1,0:T(8,128)(2,1)}, bf16[2048,1536]{1,0:T(8,128)(2,1)}, bf16[256,2048]{1,0:T(8,128)(2,1)}) custom-call(bf16[256,2048]{1,0:T(8,128)(2,1)} %bitcast.58, bf16[256,2048]{1,0:T(8,128)(2,1)} %refs_1_.5, bf16[256,2048]{1,0:T(8,128)(2,1)} %refs_2_.1, bf16[256,2048]{1,0:T(8,128)(2,1)} %refs_3_.1, bf16[256,2048]{1,0:T(8,128)(2,1)} %refs_4_.1), custom_call_target="tpu_custom_call" | custom-call | flops 1 | bytes 1 | tf_op jit(solution)/shard_map/entry/pallas_call | solution.py:384
  68.0 10.0 %fusion.12.refs_0_.refs_1_.refs_2_.refs_5_ = f32[1024,1536]{1,0:T(8,128)S(1)} fusion(bf16[1024,2048]{1,0:T(8,128)(2,1)} %bitcast.59, bf16[2048,1536]{1,0:T(8,128)(2,1)} %get-tuple-element.39.refs_6_), kind=kOutput, calls=%fused_computation.47 | convolution fusion | flops 6442450944 | bytes 16777216 | tf_op jit(solution)/shard_map/dot_general | solution.py:2085
  81.7 5.0 stats.1
  95.4 16.4 %attend.1 = (bf16[1024,512]{1,0:T(8,128)(2,1)}, bf16[1024,512]{1,0:T(8,128)(2,1)}, bf16[1024,512]{1,0:T(8,128)(2,1)}, bf16[1024,512]{1,0:T(8,128)(2,1)}, f32[4,1024,1]{2,1,0:T(8,128)}) custom-call(f32[1024,1536]{1,0:T(8,128)} %copy-done, f32[1024,1536]{1,0:T(8,128)} %copy-done, f32[1024,1536]{1,0:T(8,128)} %copy-done, f32[1024,1]{1,0:T(8,128)} %copy.29.refs_3_.refs_9_, ...), custom_call_target="tpu_custom_call" | custom-call | flops 1073741824 | bytes 10485760 | tf_op jit(solution)/shard_map/attend/pallas_call | solution.py:2138
  111.9 53.4 %to_tokens.1 = (bf16[256,2048]{1,0:T(8,128)(2,1)}, bf16[8,256,1024]{2,1,0:T(8,128)(2,1)}) custom-call(bf16[4,256,512]{2,1,0:T(8,128)(2,1)} %bitcast.63, bf16[256,8192]{1,0:T(8,128)(2,1)} %refs_1_.6), custom_call_target="tpu_custom_call" | custom-call | flops 1 | bytes 1 | tf_op jit(solution)/shard_map/to_tokens/pallas_call | solution.py:384
  165.3 6.2 multiply_reduce_fusion.3
  173.1 93.3 %gather_hidden.1 = (bf16[8,256,2048]{2,1,0:T(8,128)(2,1)}, bf16[8,256,1024]{2,1,0:T(8,128)(2,1)}, bf16[8,256,1024]{2,1,0:T(8,128)(2,1)}, bf16[8,256,1024]{2,1,0:T(8,128)(2,1)}, bf16[8,256,1024]{2,1,0:T(8,128)(2,1)}) custom-call(bf16[256,2048]{1,0:T(8,128)(2,1)} %fusion.9.refs_0_, bf16[256,8192]{1,0:T(8,128)(2,1)} %refs_1_.7, bf16[2048,1024]{1,0:T(8,128)(2,1)} %bitcast.56), custom_call_target="tpu_custom_call" | custom-call | flops 1 | bytes 1 | tf_op jit(solution)/shard_map/gather_hidden/pallas_call | solution.py:384
  266.4 49.3 %out_scatter.1 = f32[256,2048]{1,0:T(8,128)} custom-call(bf16[8,256,1024]{2,1,0:T(8,128)(2,1)} %get-tuple-element.44.refs_0_, bf16[1024,2048]{1,0:T(8,128)(2,1)} %refs_1_.9), custom_call_target="tpu_custom_call" | custom-call | flops 1 | bytes 1 | tf_op jit(solution)/shard_map/out_scatter/pallas_call | solution.py:384
  320.3 51.9 %gather_hidden_grad.1 = (bf16[8,256,2048]{2,1,0:T(8,128)(2,1)}, bf16[8,256,1024]{2,1,0:T(8,128)(2,1)}, bf16[8,256,1024]{2,1,0:T(8,128)(2,1)}) custom-call(bf16[256,2048]{1,0:T(8,128)(2,1)} %fusion.3.refs_0_, bf16[1024,2048]{1,0:T(8,128)(2,1)} %refs_1_.9, bf16[8,256,1024]{2,1,0:T(8,128)(2,1)} %get-tuple-element.45.refs_2_, ...), custom_call_target="tpu_custom_call" | custom-call | flops 1 | bytes 1 | tf_op jit(solution)/shard_map/gather_hidden_grad/pallas_call | solution.py:384
  372.2 14.1 %bitcast_convert_fusion = bf16[1024,2048]{1,0:T(8,128)(2,1)} fusion(bf16[8,256,1024]{2,1,0:T(8,128)(2,1)} %get-tuple-element.44.refs_0_, bf16[8,256,2048]{2,1,0:T(8,128)(2,1)} %get-tuple-element.57), kind=kOutput, calls=%fused_computation | convolution fusion | flops 8592031744 | bytes 16777216 | tf_op jit(solution)/shard_map/dot_general | solution.py:53
  386.3 14.1 %bitcast_convert_fusion.2.refs_4_.refs_15_ = bf16[2048,1024]{1,0:T(8,128)(2,1)} fusion(bf16[8,256,2048]{2,1,0:T(8,128)(2,1)} %get-tuple-element.50, bf16[8,256,1024]{2,1,0:T(8,128)(2,1)} %get-tuple-element.47.refs_0_), kind=kOutput, calls=%fused_computation.2 | convolution fusion | flops 8592031744 | bytes 16777216 | tf_op jit(solution)/shard_map/dot_general | solution.py:53
  400.4 13.0 %bitcast_convert_fusion.1.refs_5_.refs_16_ = bf16[2048,1024]{1,0:T(8,128)(2,1)} fusion(bf16[8,256,2048]{2,1,0:T(8,128)(2,1)} %get-tuple-element.50, bf16[8,256,1024]{2,1,0:T(8,128)(2,1)S(1)} %copy-done.14), kind=kOutput, calls=%fused_computation.1 | convolution fusion | flops 8592031744 | bytes 16777216 | tf_op jit(solution)/shard_map/dot_general | solution.py:53
  413.5 57.4 %back_scatter.1 = f32[256,2048]{1,0:T(8,128)} custom-call(bf16[8,256,1024]{2,1,0:T(8,128)(2,1)} %get-tuple-element.47.refs_0_, bf16[8,256,1024]{2,1,0:T(8,128)(2,1)} %get-tuple-element.48.refs_1_, bf16[2048,1024]{1,0:T(8,128)(2,1)} %bitcast.57, bf16[2048,1024]{1,0:T(8,128)(2,1)} %bitcast.61, bf16[2048,1024]{1,0:T(8,128)(2,1)} %bitcast_convert_fusion.2.refs_4_.refs_15_, ...), custom_call_target="tpu_custom_call" | custom-call | flops 1 | bytes 1 | tf_op jit(solution)/shard_map/back_scatter/pallas_call | solution.py:384
  470.9 3.1 multiply_reduce_fusion
  478.0 6.8 convolution_convert_fusion.refs_0_
  484.8 45.7 %to_heads.1 = (bf16[4,256,512]{2,1,0:T(8,128)(2,1)}, f32[256,2048]{1,0:T(8,128)}) custom-call(bf16[256,2048]{1,0:T(8,128)(2,1)} %convolution_convert_fusion.refs_0_, bf16[256,2048]{1,0:T(8,128)(2,1)} %get-tuple-element.41.refs_1_, bf16[256,2048]{1,0:T(8,128)(2,1)} %copy-done.13), custom_call_target="tpu_custom_call" | custom-call | flops 1 | bytes 1 | tf_op jit(solution)/shard_map/to_heads/pallas_call | solution.py:384
  530.6 2.7 convert_element_type.77.refs_17_
  533.9 28.7 %all-reduce.2.cloned.1.call-done.refs_18_ = bf16[1024,2048]{1,0:T(8,128)(2,1)} async-done(((bf16[1024,2048]{1,0:T(8,128)(2,1)}), bf16[1024,2048]{1,0:T(8,128)(2,1)}) %all-reduce.2.cloned.1.call-update) | async-done | bytes 4194320 | tf_op jit(solution)/shard_map/psum | solution.py:2249
  562.6 366.6 %finish.1 = (f32[256,2048]{1,0:T(8,128)}, f32[8,2048]{1,0:T(8,128)}, bf16[256,8192]{1,0:T(8,128)(2,1)}, bf16[256,8192]{1,0:T(8,128)(2,1)}, bf16[1024,2048]{1,0:T...) custom-call(bf16[1024,512]{1,0:T(8,128)(2,1)} %get-tuple-element.51.ref, ...), custom_call_target="tpu_custom_call" | custom-call | flops 1 | bytes 1 | tf_op jit(solution)/shard_map/finish/pallas_call | solution.py:384
  929.2 3.5 add_bitcast_fusion
  932.8 4.1 slice_convert_fusion
  937.4 4.4 convert_element_type.83
  941.8 4.4 convert_element_type.84
  946.8 4.4 convert_element_type.85
  (64 shorter events, 24.5 us)
Async XLA Ops:
  7.2 158.1 %all-gather.2.cloned.1.call-start = ((), (), s32[]{:S(2)}) async-start(), calls=%async_computation | async-start | bytes 9437184 | tf_op jit(solution)/shard_map/all_gather | solution.py:2202
  67.9 494.7 %all-reduce.2.cloned.1.call-start = ((), (), s32[]{:S(2)}) async-start(), calls=%async_computation.1 | async-start | bytes 8388608 | tf_op jit(solution)/shard_map/psum | solution.py:2249
  78.0 2.7 copy-start
  165.2 6.3 copy-start.8
  165.3 6.2 copy-start.15
  171.5 1.7 copy-start.5
  266.4 51.3 %copy-start.4 = (bf16[1,256,2048]{2,1,0:T(8,128)(2,1)S(1)}, bf16[1,256,2048]{2,1,0:T(8,128)(2,1)}, u32[]{:S(2)}) copy-start(bf16[1,256,2048]{2,1,0:T(8,128)(2,1)} %param.25) | copy-start | bytes 3145732
  266.4 51.3 %copy-start.16 = (f32[2048]{0:T(1024)S(1)}, f32[2048]{0:T(1024)}, u32[]{:S(2)}) copy-start(f32[2048]{0:T(1024)} %param.24) | copy-start | bytes 24580
  315.7 2.2 copy-start.1
  386.3 14.1 %copy-start.14 = (bf16[8,256,1024]{2,1,0:T(8,128)(2,1)S(1)}, bf16[8,256,1024]{2,1,0:T(8,128)(2,1)}, u32[]{:S(2)}) copy-start(bf16[8,256,1024]{2,1,0:T(8,128)(2,1)} %get-tuple-element.48.refs_1_) | copy-start | bytes 12582916
  470.8 3.2 copy-start.2
  470.8 3.6 copy-start.6
  470.8 3.9 copy-start.9
  477.0 1.0 copy-start.13
  562.6 366.6 %copy-start.3 = (f32[256,2048]{1,0:T(8,128)S(1)}, f32[256,2048]{1,0:T(8,128)}, u32[]{:S(2)}) copy-start(f32[256,2048]{1,0:T(8,128)} %back_scatter.1) | copy-start | bytes 6291460
  929.2 3.5 copy-start.12
  932.8 4.6 copy-start.11
  937.4 4.4 copy-start.10
  941.8 4.4 copy-start.17
  941.8 5.0 copy-start.7
Sparse Core Ops, SparseCore 0:
  68.0 54.6 all-gather.1
  386.4 176.1 all-reduce.1

commit v6 on v5

--- a/solution.py
+++ b/solution.py
@@ -1250,6 +1250,7 @@
 RING = 4
 CLOSE_LAG = 2
 TAKE_LAG = 5
+AHEAD = 3
 
 
 def flip_by(value, mask):
@@ -1389,8 +1390,9 @@
     def begin(self):
         @pl.when(self.outer)
         def _():
-            for copy in self.inward(0):
-                copy.start()
+            for index in range(AHEAD):
+                for copy in self.inward(index):
+                    copy.start()
 
         @pl.when(self.inner)
         def _():
@@ -1464,10 +1466,18 @@
         if not self.is_late(index):
             self.spread_start(index, self.total_in.at[index])
 
-    def outer_step(self, index, following):
-        if following:
-            for copy in self.inward(index + 1):
-                copy.start()
+    def outer_step(self, index):
+        if isinstance(index, int):
+            if index + AHEAD < self.count:
+                for copy in self.inward(index + AHEAD):
+                    copy.start()
+        else:
+
+            @pl.when(index + AHEAD < self.early)
+            def _():
+                for copy in self.inward(index + AHEAD):
+                    copy.start()
+
         if isinstance(index, int):
             self.outer_take(index - TAKE_LAG)
         else:
@@ -1483,7 +1493,7 @@
 
         @pl.when(self.outer)
         def _():
-            self.outer_step(index, following)
+            self.outer_step(index)
 
     def run(self, start, stop):
         def one(index, carry):
@@ -1494,6 +1504,13 @@
 
     def finish(self):
         early, count = self.early, self.count
+
+        @pl.when(self.outer)
+        def _():
+            for index in range(early, early - 1 + AHEAD):
+                for copy in self.inward(index):
+                    copy.start()
+
         for index in range(early - 1, count):
             self.step(index, index + 1 < count)
 

time: 970 us -> 985 us (1.015)
  Pallas kernels: 800 us -> 814 us
    pallas_call x9, Pallas kernels: 783 us -> 798 us  [comm_call(): pl.pallas_call(ordered(kernel, inputs, after), out_shape=out_shape, in_sp...]
  transfers between devices with their start and end apart: 2 -> 2, of which waited for: 1 -> 1; matrix products, arithmetic and copies ran while one was open for 7% -> 6% of each run, Pallas kernels for 19% -> 18%
where the time goes in v6:
time: 985 us; the launch traced here: 973 us
  Pallas kernels  814 us (83%)
  matrix products  64.2 us (7%)
  other arithmetic  39.9 us (4%)
  waiting for transfers between devices  28.8 us (3%)
  between operations  14.8 us (2%)
  local copies, waits for them, and re-layouts  11.2 us (1%)
    pallas_call x9, Pallas kernels, comm_call(): pl.pallas_call(ordered(kernel, inputs, after), out_shape=out_shape, in_sp...  798 us
    dot_general x3, matrix products, transposed_times(): lax.dot_general(operand, matrix, (((0,), (0,)), ((), ())), preferred_elem...  41.2 us
    psum x1, waiting for transfers between devices, split_layer(): down_sum = lax.psum(down_grad, 'seq')  28.7 us
  transfers between devices with their start and end apart: 2, of which 1 were waited for; matrix products, arithmetic and copies ran while one was open for 6% of the time, Pallas kernels for 18%

profile of v6, /device:TPU:0, one launch (start us, length us, event | category | flops | bytes accessed | tf_op | source)
XLA Modules:
  0.0 973.1 jit_solution(2461166618829282097)
XLA Ops:
  7.2 60.7 %entry.1 = (bf16[4,256,2048]{2,1,0:T(8,128)(2,1)}, bf16[2048,1536]{1,0:T(8,128)(2,1)}, bf16[256,2048]{1,0:T(8,128)(2,1)}) custom-call(bf16[256,2048]{1,0:T(8,128)(2,1)} %bitcast.58, bf16[256,2048]{1,0:T(8,128)(2,1)} %refs_1_.5, bf16[256,2048]{1,0:T(8,128)(2,1)} %refs_2_.1, bf16[256,2048]{1,0:T(8,128)(2,1)} %refs_3_.1, bf16[256,2048]{1,0:T(8,128)(2,1)} %refs_4_.1), custom_call_target="tpu_custom_call" | custom-call | flops 1 | bytes 1 | tf_op jit(solution)/shard_map/entry/pallas_call | solution.py:384
  68.0 10.0 %fusion.12.refs_0_.refs_1_.refs_2_.refs_5_ = f32[1024,1536]{1,0:T(8,128)S(1)} fusion(bf16[1024,2048]{1,0:T(8,128)(2,1)} %bitcast.59, bf16[2048,1536]{1,0:T(8,128)(2,1)} %get-tuple-element.39.refs_6_), kind=kOutput, calls=%fused_computation.47 | convolution fusion | flops 6442450944 | bytes 16777216 | tf_op jit(solution)/shard_map/dot_general | solution.py:2102
  81.7 5.0 stats.1
  95.4 16.4 %attend.1 = (bf16[1024,512]{1,0:T(8,128)(2,1)}, bf16[1024,512]{1,0:T(8,128)(2,1)}, bf16[1024,512]{1,0:T(8,128)(2,1)}, bf16[1024,512]{1,0:T(8,128)(2,1)}, f32[4,1024,1]{2,1,0:T(8,128)}) custom-call(f32[1024,1536]{1,0:T(8,128)} %copy-done, f32[1024,1536]{1,0:T(8,128)} %copy-done, f32[1024,1536]{1,0:T(8,128)} %copy-done, f32[1024,1]{1,0:T(8,128)} %copy.29.refs_3_.refs_9_, ...), custom_call_target="tpu_custom_call" | custom-call | flops 1073741824 | bytes 10485760 | tf_op jit(solution)/shard_map/attend/pallas_call | solution.py:2155
  111.9 53.4 %to_tokens.1 = (bf16[256,2048]{1,0:T(8,128)(2,1)}, bf16[8,256,1024]{2,1,0:T(8,128)(2,1)}) custom-call(bf16[4,256,512]{2,1,0:T(8,128)(2,1)} %bitcast.63, bf16[256,8192]{1,0:T(8,128)(2,1)} %refs_1_.6), custom_call_target="tpu_custom_call" | custom-call | flops 1 | bytes 1 | tf_op jit(solution)/shard_map/to_tokens/pallas_call | solution.py:384
  165.3 6.2 multiply_reduce_fusion.3
  173.1 93.3 %gather_hidden.1 = (bf16[8,256,2048]{2,1,0:T(8,128)(2,1)}, bf16[8,256,1024]{2,1,0:T(8,128)(2,1)}, bf16[8,256,1024]{2,1,0:T(8,128)(2,1)}, bf16[8,256,1024]{2,1,0:T(8,128)(2,1)}, bf16[8,256,1024]{2,1,0:T(8,128)(2,1)}) custom-call(bf16[256,2048]{1,0:T(8,128)(2,1)} %fusion.9.refs_0_, bf16[256,8192]{1,0:T(8,128)(2,1)} %refs_1_.7, bf16[2048,1024]{1,0:T(8,128)(2,1)} %bitcast.56), custom_call_target="tpu_custom_call" | custom-call | flops 1 | bytes 1 | tf_op jit(solution)/shard_map/gather_hidden/pallas_call | solution.py:384
  266.4 49.3 %out_scatter.1 = f32[256,2048]{1,0:T(8,128)} custom-call(bf16[8,256,1024]{2,1,0:T(8,128)(2,1)} %get-tuple-element.44.refs_0_, bf16[1024,2048]{1,0:T(8,128)(2,1)} %refs_1_.9), custom_call_target="tpu_custom_call" | custom-call | flops 1 | bytes 1 | tf_op jit(solution)/shard_map/out_scatter/pallas_call | solution.py:384
  320.3 51.9 %gather_hidden_grad.1 = (bf16[8,256,2048]{2,1,0:T(8,128)(2,1)}, bf16[8,256,1024]{2,1,0:T(8,128)(2,1)}, bf16[8,256,1024]{2,1,0:T(8,128)(2,1)}) custom-call(bf16[256,2048]{1,0:T(8,128)(2,1)} %fusion.3.refs_0_, bf16[1024,2048]{1,0:T(8,128)(2,1)} %refs_1_.9, bf16[8,256,1024]{2,1,0:T(8,128)(2,1)} %get-tuple-element.45.refs_2_, ...), custom_call_target="tpu_custom_call" | custom-call | flops 1 | bytes 1 | tf_op jit(solution)/shard_map/gather_hidden_grad/pallas_call | solution.py:384
  372.2 14.1 %bitcast_convert_fusion = bf16[1024,2048]{1,0:T(8,128)(2,1)} fusion(bf16[8,256,1024]{2,1,0:T(8,128)(2,1)} %get-tuple-element.44.refs_0_, bf16[8,256,2048]{2,1,0:T(8,128)(2,1)} %get-tuple-element.57), kind=kOutput, calls=%fused_computation | convolution fusion | flops 8592031744 | bytes 16777216 | tf_op jit(solution)/shard_map/dot_general | solution.py:53
  386.3 14.1 %bitcast_convert_fusion.2.refs_4_.refs_15_ = bf16[2048,1024]{1,0:T(8,128)(2,1)} fusion(bf16[8,256,2048]{2,1,0:T(8,128)(2,1)} %get-tuple-element.50, bf16[8,256,1024]{2,1,0:T(8,128)(2,1)} %get-tuple-element.47.refs_0_), kind=kOutput, calls=%fused_computation.2 | convolution fusion | flops 8592031744 | bytes 16777216 | tf_op jit(solution)/shard_map/dot_general | solution.py:53
  400.4 13.0 %bitcast_convert_fusion.1.refs_5_.refs_16_ = bf16[2048,1024]{1,0:T(8,128)(2,1)} fusion(bf16[8,256,2048]{2,1,0:T(8,128)(2,1)} %get-tuple-element.50, bf16[8,256,1024]{2,1,0:T(8,128)(2,1)S(1)} %copy-done.14), kind=kOutput, calls=%fused_computation.1 | convolution fusion | flops 8592031744 | bytes 16777216 | tf_op jit(solution)/shard_map/dot_general | solution.py:53
  413.5 57.4 %back_scatter.1 = f32[256,2048]{1,0:T(8,128)} custom-call(bf16[8,256,1024]{2,1,0:T(8,128)(2,1)} %get-tuple-element.47.refs_0_, bf16[8,256,1024]{2,1,0:T(8,128)(2,1)} %get-tuple-element.48.refs_1_, bf16[2048,1024]{1,0:T(8,128)(2,1)} %bitcast.57, bf16[2048,1024]{1,0:T(8,128)(2,1)} %bitcast.61, bf16[2048,1024]{1,0:T(8,128)(2,1)} %bitcast_convert_fusion.2.refs_4_.refs_15_, ...), custom_call_target="tpu_custom_call" | custom-call | flops 1 | bytes 1 | tf_op jit(solution)/shard_map/back_scatter/pallas_call | solution.py:384
  470.9 3.1 multiply_reduce_fusion
  478.0 6.8 convolution_convert_fusion.refs_0_
  484.8 45.7 %to_heads.1 = (bf16[4,256,512]{2,1,0:T(8,128)(2,1)}, f32[256,2048]{1,0:T(8,128)}) custom-call(bf16[256,2048]{1,0:T(8,128)(2,1)} %convolution_convert_fusion.refs_0_, bf16[256,2048]{1,0:T(8,128)(2,1)} %get-tuple-element.41.refs_1_, bf16[256,2048]{1,0:T(8,128)(2,1)} %copy-done.13), custom_call_target="tpu_custom_call" | custom-call | flops 1 | bytes 1 | tf_op jit(solution)/shard_map/to_heads/pallas_call | solution.py:384
  530.6 2.7 convert_element_type.77.refs_17_
  533.9 28.7 %all-reduce.2.cloned.1.call-done.refs_18_ = bf16[1024,2048]{1,0:T(8,128)(2,1)} async-done(((bf16[1024,2048]{1,0:T(8,128)(2,1)}), bf16[1024,2048]{1,0:T(8,128)(2,1)}) %all-reduce.2.cloned.1.call-update) | async-done | bytes 4194320 | tf_op jit(solution)/shard_map/psum | solution.py:2266
  562.6 381.2 %finish.1 = (f32[256,2048]{1,0:T(8,128)}, f32[8,2048]{1,0:T(8,128)}, bf16[256,8192]{1,0:T(8,128)(2,1)}, bf16[256,8192]{1,0:T(8,128)(2,1)}, bf16[1024,2048]{1,0:T...) custom-call(bf16[1024,512]{1,0:T(8,128)(2,1)} %get-tuple-element.51.ref, ...), custom_call_target="tpu_custom_call" | custom-call | flops 1 | bytes 1 | tf_op jit(solution)/shard_map/finish/pallas_call | solution.py:384
  943.8 3.5 add_bitcast_fusion
  947.3 4.1 slice_convert_fusion
  952.0 4.4 convert_element_type.83
  956.3 4.4 convert_element_type.84
  961.4 4.4 convert_element_type.85
  (64 shorter events, 24.5 us)
Async XLA Ops:
  7.2 158.1 %all-gather.2.cloned.1.call-start = ((), (), s32[]{:S(2)}) async-start(), calls=%async_computation | async-start | bytes 9437184 | tf_op jit(solution)/shard_map/all_gather | solution.py:2219
  67.9 494.7 %all-reduce.2.cloned.1.call-start = ((), (), s32[]{:S(2)}) async-start(), calls=%async_computation.1 | async-start | bytes 8388608 | tf_op jit(solution)/shard_map/psum | solution.py:2266
  78.0 2.7 copy-start
  165.2 6.3 copy-start.8
  165.3 6.2 copy-start.15
  171.5 1.7 copy-start.5
  266.4 51.3 %copy-start.4 = (bf16[1,256,2048]{2,1,0:T(8,128)(2,1)S(1)}, bf16[1,256,2048]{2,1,0:T(8,128)(2,1)}, u32[]{:S(2)}) copy-start(bf16[1,256,2048]{2,1,0:T(8,128)(2,1)} %param.25) | copy-start | bytes 3145732
  266.4 51.3 %copy-start.16 = (f32[2048]{0:T(1024)S(1)}, f32[2048]{0:T(1024)}, u32[]{:S(2)}) copy-start(f32[2048]{0:T(1024)} %param.24) | copy-start | bytes 24580
  315.7 2.2 copy-start.1
  386.3 14.1 %copy-start.14 = (bf16[8,256,1024]{2,1,0:T(8,128)(2,1)S(1)}, bf16[8,256,1024]{2,1,0:T(8,128)(2,1)}, u32[]{:S(2)}) copy-start(bf16[8,256,1024]{2,1,0:T(8,128)(2,1)} %get-tuple-element.48.refs_1_) | copy-start | bytes 12582916
  470.8 3.2 copy-start.2
  470.8 3.6 copy-start.6
  470.8 3.9 copy-start.9
  477.0 1.0 copy-start.13
  562.6 381.2 %copy-start.3 = (f32[256,2048]{1,0:T(8,128)S(1)}, f32[256,2048]{1,0:T(8,128)}, u32[]{:S(2)}) copy-start(f32[256,2048]{1,0:T(8,128)} %back_scatter.1) | copy-start | bytes 6291460
  943.8 3.5 copy-start.12
  947.3 4.6 copy-start.11
  952.0 4.4 copy-start.10
  956.3 4.4 copy-start.17
  956.3 5.0 copy-start.7
Sparse Core Ops, SparseCore 0:
  68.0 54.6 all-gather.1
  386.4 176.1 all-reduce.1
